TPU v7x, 32 devices: a whole 2x2x4 slice. The times are simulated.
32 devices in a mesh: gx: 8 (over y, x, core), gy: 4 (over z).
Axes of the slice: x: 2, y: 2, z: 4, core: 2. Of those that a mesh axis runs over, the one named last changes fastest.
Arguments:
- field: bfloat16 [64, 128, 512], P(None, 'gx', 'gy'), may hold values from -6 to 6
- spectral_weight: bfloat16 [2, 128, 128, 64, 64], P(None, 'gx', 'gy'), may hold values from -1.5 to 1.5
- kernel_weight: bfloat16 [3, 3, 64, 64], replicated, may hold values from -1 to 1
- cotangent: bfloat16 [64, 128, 512], P(None, 'gx', 'gy'), may hold values from -6 to 6
Outputs:
- layer_out: bfloat16 [64, 128, 512], P(None, 'gx', 'gy')
- field_grad: bfloat16 [64, 128, 512], P(None, 'gx', 'gy')
- spectral_grad: bfloat16 [2, 128, 128, 64, 64], P(None, 'gx', 'gy')
- kernel_grad: float32 [3, 3, 64, 64], replicated
All inputs are finite; a program needn't handle non-finite values.
Results may differ from a plain program's by a relative error of at most 0.009.
Values may be sent and summed in bfloat16 or wider, within the bound.
No kernel may reach another device: no remote copies, remote signals or barrier semaphores. Data moves between devices by JAX's collectives and lax.ppermute only.
A program may use at most 128 MiB of HBM per device.

v0:
```python
from functools import partial
import math

import jax
import jax.numpy as jnp
from jax import lax
from jax.sharding import PartitionSpec as P

KX = 128
KY = 128


def extended(array, sides, width):
    for axis, dim in sides:
        count, length = (lax.axis_size(axis), array.shape[dim])
        up = [(i, (i + 1) % count) for i in range(count)]
        down = [(j, i) for i, j in up]
        last = lax.slice_in_dim(array, length - width, length, axis=dim)
        initial = lax.slice_in_dim(array, 0, width, axis=dim)
        before = lax.ppermute(last, axis, up)
        after = lax.ppermute(initial, axis, down)
        array = jnp.concatenate([before, array, after], axis=dim)
    return array


def phases(waves, points, length):
    wrapped = jnp.mod(waves[:, None] * points[None, :], length).astype(jnp.float32)
    return wrapped * (2.0 * math.pi / length)


def widen(field):
    return extended(field, (("gx", 1), ("gy", 2)), 1)


def body(field, spectral_weight, kernel_weight, cotangent):
    highest = lax.Precision.HIGHEST
    channels, block_rows, block_cols = field.shape
    rows_total = block_rows * lax.axis_size("gx")
    cols_total = block_cols * lax.axis_size("gy")
    scale = 1.0 / math.sqrt(rows_total * cols_total)
    row_coord = lax.axis_index("gx") * block_rows + jnp.arange(block_rows, dtype=jnp.int32)
    col_coord = lax.axis_index("gy") * block_cols + jnp.arange(block_cols, dtype=jnp.int32)
    modes_x = KX // lax.axis_size("gx")
    modes_y = KY // lax.axis_size("gy")

    def analyse(source):
        waves = jnp.arange(lax.axis_size("gy") * modes_y, dtype=jnp.int32)
        angles = phases(waves, col_coord, cols_total)
        table = jnp.concatenate([jnp.cos(angles), -jnp.sin(angles)], 0).astype(jnp.bfloat16)
        product = jnp.dot(
            source.reshape(channels * block_rows, block_cols),
            table.T,
            preferred_element_type=jnp.float32,
        )
        product = product.reshape(channels, block_rows, 2, lax.axis_size("gy") * modes_y).transpose(
            3, 1, 2, 0
        )
        col_modes = lax.psum_scatter(
            product.reshape(lax.axis_size("gy") * modes_y, block_rows, 2 * channels),
            "gy",
            scatter_dimension=0,
            tiled=True,
        )
        split_modes = col_modes.reshape(modes_y, block_rows, 2, channels)
        real_in = split_modes[:, :, 0]
        imag_in = split_modes[:, :, 1]
        waves = jnp.arange(lax.axis_size("gx") * modes_x, dtype=jnp.int32) - KX // 2
        angles = phases(waves, row_coord, rows_total)
        cosines = jnp.cos(angles)
        sines = jnp.sin(angles)
        contract = partial(jnp.einsum, "jx,lxc->jlc", precision=highest)
        real_out = contract(cosines, real_in) + contract(sines, imag_in)
        imag_out = contract(cosines, imag_in) - contract(sines, real_in)
        return lax.psum_scatter(
            jnp.stack([real_out, imag_out], 2).reshape(
                lax.axis_size("gx") * modes_x, modes_y, 2 * channels
            )
            * scale,
            "gx",
            scatter_dimension=0,
            tiled=True,
        ).reshape(modes_x, modes_y, 2, channels)

    def synthesise(modes):
        start_rows = jnp.zeros((modes_y, block_rows, 2 * channels), jnp.float32)
        shard_rows = lax.all_gather(
            modes.reshape(modes_x, modes_y, 2 * channels), "gx", axis=0, tiled=True
        )
        amount = shard_rows.shape[0]
        waves = jnp.arange(amount, dtype=jnp.int32) - KX // 2
        angles = phases(waves, row_coord, rows_total)
        cosines = jnp.cos(angles).astype(jnp.bfloat16)
        sines = jnp.sin(angles).astype(jnp.bfloat16)
        split_rows = shard_rows.reshape(amount, modes_y, 2, channels)
        real_in = split_rows[:, :, 0]
        imag_in = split_rows[:, :, 1]
        contract = partial(jnp.einsum, "jx,jlc->lxc", preferred_element_type=jnp.float32)
        real_out = contract(cosines, real_in) - contract(sines, imag_in)
        imag_out = contract(sines, real_in) + contract(cosines, imag_in)
        row_sum = start_rows + jnp.stack([real_out, imag_out], 2).reshape(
            modes_y, block_rows, 2 * channels
        )
        row_sum = row_sum.astype(jnp.bfloat16)
        shard_rows = lax.all_gather(row_sum, "gy", axis=0, tiled=True)
        amount = shard_rows.shape[0]
        waves = jnp.arange(amount, dtype=jnp.int32)
        angles = phases(waves, col_coord, cols_total)
        table = jnp.stack([jnp.cos(angles), -jnp.sin(angles)], 1).astype(jnp.bfloat16)
        split_rows = shard_rows.reshape(amount, block_rows, 2, channels)
        return (
            jnp.einsum("lxpc,lpy->cxy", split_rows, table, preferred_element_type=jnp.float32)
            * scale
        )

    padded_field = widen(field)
    hidden = jnp.zeros((channels, block_rows, block_cols), jnp.float32)
    for row_tap in range(3):
        for col_tap in range(3):
            window = padded_field[:, row_tap : row_tap + block_rows, col_tap : col_tap + block_cols]
            hidden = hidden + jnp.einsum(
                "oi,ixy->oxy",
                kernel_weight[row_tap, col_tap],
                window,
                preferred_element_type=jnp.float32,
            )
    amodes = analyse(field)
    areal = amodes[:, :, 0]
    aimag = amodes[:, :, 1]
    wreal = spectral_weight[0].astype(jnp.float32)
    wimag = spectral_weight[1].astype(jnp.float32)
    mixing = partial(jnp.einsum, "jli,jlio->jlo", precision=highest)
    breal = mixing(areal, wreal) - mixing(aimag, wimag)
    bimag = mixing(areal, wimag) + mixing(aimag, wreal)
    wave_index = lax.axis_index("gy") * modes_y + jnp.arange(modes_y, dtype=jnp.int32)
    weights = jnp.where(wave_index == 0, 1.0, 2.0).astype(jnp.float32)[None, :, None, None]
    bmodes = (jnp.stack([breal, bimag], 2) * weights).astype(jnp.bfloat16)
    hidden = hidden + synthesise(bmodes)
    activated, pullback = jax.vjp(jax.nn.gelu, hidden)
    layer_out = (field.astype(jnp.float32) + activated).astype(jnp.bfloat16)
    grads = pullback(cotangent.astype(jnp.float32))[0].astype(jnp.bfloat16)
    gmodes = analyse(grads) * weights
    greal = gmodes[:, :, 0]
    gimag = gmodes[:, :, 1]
    outer = partial(jnp.einsum, "jli,jlo->jlio", precision=highest)
    spectral_grad = jnp.stack(
        [outer(areal, greal) + outer(aimag, gimag), outer(areal, gimag) - outer(aimag, greal)], 0
    ).astype(jnp.bfloat16)
    back = partial(jnp.einsum, "jlio,jlo->jli", precision=highest)
    back_real = back(wreal, greal) + back(wimag, gimag)
    back_imag = back(wreal, gimag) - back(wimag, greal)
    back_modes = jnp.stack([back_real, back_imag], 2).astype(jnp.bfloat16)
    padded_grads = widen(grads)
    adjoint = jnp.zeros((channels, block_rows, block_cols), jnp.float32)
    tap_rows = []
    for row_tap in range(3):
        tap_cols = []
        for col_tap in range(3):
            window = padded_grads[
                :, 2 - row_tap : 2 - row_tap + block_rows, 2 - col_tap : 2 - col_tap + block_cols
            ]
            adjoint = adjoint + jnp.einsum(
                "oi,oxy->ixy",
                kernel_weight[row_tap, col_tap],
                window,
                preferred_element_type=jnp.float32,
            )
            source_window = padded_field[
                :, row_tap : row_tap + block_rows, col_tap : col_tap + block_cols
            ]
            tap_cols.append(
                jnp.einsum("oxy,ixy->oi", grads, source_window, preferred_element_type=jnp.float32)
            )
        tap_rows.append(jnp.stack(tap_cols, 0))
    kernel_grad = lax.psum(jnp.stack(tap_rows, 0), ("gx", "gy"))
    field_grad = (cotangent.astype(jnp.float32) + adjoint + synthesise(back_modes)).astype(
        jnp.bfloat16
    )
    return (layer_out, field_grad, spectral_grad, kernel_grad)


def solution(mesh):
    in_specs = (P(None, "gx", "gy"), P(None, "gx", "gy", None, None), P(), P(None, "gx", "gy"))
    out_specs = (P(None, "gx", "gy"), P(None, "gx", "gy"), P(None, "gx", "gy", None, None), P())
    return jax.shard_map(body, mesh=mesh, in_specs=in_specs, out_specs=out_specs, check_vma=False)
```

profile of v0, /device:TPU:8, one launch (start us, length us, event | category | flops | bytes accessed | tf_op | source)
XLA Modules:
  0.0 489.2 jit_solution(13057502457903456165)
XLA Ops:
  10.3 1.4 copy.127
  11.8 26.3 %reduce-scatter.5.cloned.1.call-done = f32[32,16,128]{2,1,0:T(8,128)} async-done(((f32[128,16,128]{2,1,0:T(8,128)}), f32[32,16,128]{2,1,0:T(8,128)}) %reduce-scatter.5.cloned.1.call-update) | async-done | bytes 262160 | tf_op jit(solution)/shard_map/reduce_scatter | solution.py:58
  38.1 1.3 reshape.185
  39.8 1.8 fusion.171
  41.6 1.8 fusion.173
  43.5 1.9 fusion.28
  45.3 1.9 fusion.29
  47.8 2.0 copy.131
  49.9 1.9 collective-permute-start.1
  52.9 3.1 collective-permute-done
  57.0 2.2 collective-permute-start.2
  59.4 32.4 %reduce-scatter.7.cloned.1.call-done = f32[16,32,128]{2,1,0:T(8,128)} async-done(((f32[128,32,128]{2,1,0:T(8,128)}), f32[16,32,128]{2,1,0:T(8,128)}) %reduce-scatter.7.cloned.1.call-update) | async-done | bytes 262160 | tf_op jit(solution)/shard_map/reduce_scatter | solution.py:74
  91.8 1.3 reshape.186
  93.1 9.1 %fusion.6 = f32[16,32,1,64]{3,2,1,0:T(1,128)S(1)} fusion(bf16[2,16,32,64,64]{4,3,2,1,0:T(8,128)(2,1)} %param.5, f32[16,32,2,64]{3,2,1,0:T(2,128)S(1)} %reshape.186), kind=kOutput, calls=%fused_computation.9 | convolution fusion | flops 25165824 | bytes 8781824 | tf_op jit(solution)/shard_map/jli,jlio->jlo/dot_general | solution.py:133
  102.2 9.8 %fusion.8 = f32[16,32,1,64]{3,2,1,0:T(1,128)S(1)} fusion(bf16[2,16,32,64,64]{4,3,2,1,0:T(8,128)(2,1)} %param.5, f32[16,32,2,64]{3,2,1,0:T(2,128)S(1)} %reshape.186), kind=kOutput, calls=%fused_computation.11 | convolution fusion | flops 25165824 | bytes 8781824 | tf_op jit(solution)/shard_map/jli,jlio->jlo/dot_general | solution.py:132
  112.1 6.7 %fusion.14 = f32[16,32,1,64]{3,2,1,0:T(1,128)S(1)} fusion(bf16[2,16,32,64,64]{4,3,2,1,0:T(8,128)(2,1)S(1)} %bitcast.384, f32[16,32,2,64]{3,2,1,0:T(2,128)S(1)} %reshape.186), kind=kOutput, calls=%fused_computation.17 | convolution fusion | flops 25165824 | bytes 8781824 | tf_op jit(solution)/shard_map/jli,jlio->jlo/dot_general | solution.py:133
  118.8 6.8 %fusion.16 = f32[16,32,1,64]{3,2,1,0:T(1,128)S(1)} fusion(bf16[2,16,32,64,64]{4,3,2,1,0:T(8,128)(2,1)S(1)} %bitcast.384, f32[16,32,2,64]{3,2,1,0:T(2,128)S(1)} %reshape.186), kind=kOutput, calls=%fused_computation.19 | convolution fusion | flops 25165824 | bytes 8781824 | tf_op jit(solution)/shard_map/jli,jlio->jlo/dot_general | solution.py:132
  131.7 19.6 %all-gather.3.cloned.1.call-done = bf16[128,32,128]{2,1,0:T(8,128)(2,1)} async-done(((bf16[16,32,128]{2,1,0:T(8,128)(2,1)}), bf16[128,32,128]{2,1,0:T(8,128)(2,1)}) %all-gather.3.cloned.1.call-update) | async-done | bytes 1048592 | tf_op jit(solution)/shard_map/all_gather | solution.py:86
  151.2 1.9 copy.132
  156.1 16.3 %all_gather.13 = bf16[128,16,128]{2,1,0:T(8,128)(2,1)S(1)} all-gather(bf16[32,16,128]{2,1,0:T(8,128)(2,1)S(1)} %convert_element_type.89), channel_id=1, replica_groups=mesh['gx'=8,'gy'=4] {'gy'}, dimensions={0}, use_global_device_ids=true | all-gather | bytes 655360 | tf_op jit(solution)/shard_map/all_gather | solution.py:104
  173.2 2.7 fusion.66
  177.7 1.4 copy.149
  179.5 24.9 %reduce-scatter.9.cloned.1.call-done = f32[32,16,128]{2,1,0:T(8,128)} async-done(((f32[128,16,128]{2,1,0:T(8,128)}), f32[32,16,128]{2,1,0:T(8,128)}) %reduce-scatter.9.cloned.1.call-update) | async-done | bytes 262160 | tf_op jit(solution)/shard_map/reduce_scatter | solution.py:58
  204.5 1.3 reshape.190
  206.1 1.8 fusion.167
  208.0 1.8 fusion.169
  209.9 1.9 fusion.26
  211.7 1.9 fusion.27
  214.1 2.0 copy.153
  216.8 2.8 collective-permute-start.5
  220.8 1.3 convolution_bitcast_fusion.8
  222.1 1.3 convolution_bitcast_fusion.10
  223.4 34.9 %reduce-scatter.11.cloned.1.call-done = f32[16,32,128]{2,1,0:T(8,128)} async-done(((f32[128,32,128]{2,1,0:T(8,128)}), f32[16,32,128]{2,1,0:T(8,128)}) %reduce-scatter.11.cloned.1.call-update) | async-done | bytes 262160 | tf_op jit(solution)/shard_map/reduce_scatter | solution.py:74
  258.2 1.3 reshape.191
  259.8 15.4 %fusion.2 = f32[16,32,1,64]{3,2,1,0:T(1,128)S(1)} fusion(bf16[2,16,32,64,64]{4,3,2,1,0:T(8,128)(2,1)} %param.5, f32[16,32,2,64]{3,2,1,0:T(2,128)S(1)} %broadcast_multiply_fusion), kind=kOutput, calls=%fused_computation.5 | convolution fusion | flops 25165824 | bytes 8781824 | tf_op jit(solution)/shard_map/jlio,jlo->jli/dot_general | solution.py:150
  275.2 15.4 %fusion.4 = f32[16,32,1,64]{3,2,1,0:T(1,128)S(1)} fusion(bf16[2,16,32,64,64]{4,3,2,1,0:T(8,128)(2,1)} %param.5, f32[16,32,2,64]{3,2,1,0:T(2,128)S(1)} %broadcast_multiply_fusion), kind=kOutput, calls=%fused_computation.7 | convolution fusion | flops 25165824 | bytes 8781824 | tf_op jit(solution)/shard_map/jlio,jlo->jli/dot_general | solution.py:149
  290.5 15.4 %fusion.10 = f32[16,32,1,64]{3,2,1,0:T(1,128)S(1)} fusion(bf16[2,16,32,64,64]{4,3,2,1,0:T(8,128)(2,1)} %param.5, f32[16,32,2,64]{3,2,1,0:T(2,128)S(1)} %broadcast_multiply_fusion), kind=kOutput, calls=%fused_computation.13 | convolution fusion | flops 25165824 | bytes 8781824 | tf_op jit(solution)/shard_map/jlio,jlo->jli/dot_general | solution.py:150
  305.9 15.6 %fusion.12 = f32[16,32,1,64]{3,2,1,0:T(1,128)S(1)} fusion(bf16[2,16,32,64,64]{4,3,2,1,0:T(8,128)(2,1)} %param.5, f32[16,32,2,64]{3,2,1,0:T(2,128)S(1)} %broadcast_multiply_fusion), kind=kOutput, calls=%fused_computation.15 | convolution fusion | flops 25165824 | bytes 8781824 | tf_op jit(solution)/shard_map/jlio,jlo->jli/dot_general | solution.py:149
  325.8 1.8 copy.161
  328.5 1.5 collective-permute-start.7
  330.5 6.4 %collective-permute-done.6 = bf16[64,18,1]{2,0,1:T(8,128)(2,1)S(1)} collective-permute-done((bf16[64,18,1]{2,0,1:T(8,128)(2,1)S(1)}, bf16[64,18,1]{2,0,1:T(8,128)(2,1)S(1)}, u32[]{:S(2)}, u32[]{:S(2)}) %collective-permute-start.6) | collective-permute-done | bytes 2336 | tf_op jit(solution)/shard_map/ppermute | solution.py:21
  336.9 8.0 %collective-permute-done.7 = bf16[64,18,1]{2,0,1:T(8,128)(2,1)S(1)} collective-permute-done((bf16[64,18,1]{2,0,1:T(8,128)(2,1)S(1)}, bf16[64,18,1]{2,0,1:T(8,128)(2,1)S(1)}, u32[]{:S(2)}, u32[]{:S(2)}) %collective-permute-start.7) | collective-permute-done | bytes 2336 | tf_op jit(solution)/shard_map/ppermute | solution.py:20
  347.6 10.1 %fusion = (bf16[1,16,32,64,64]{4,3,2,1,0:T(8,128)(2,1)S(1)}, bf16[1,16,32,64,64]{4,3,2,1,0:T(8,128)(2,1)S(1)}) fusion(f32[16,32,64]{2,1,0:T(8,128)S(1)} %bitcast.415, f32[16,32,64]{2,1,0:T(8,128)S(1)} %bitcast.413, f32[16,32,64]{2,1,0:T(8,128)S(1)} %bitcast.414, f32[16,32,64]{2,1,0:T(8,128)S(1)} %bitcast.412), kind=kLoop, calls=%fused_computation.3 | loop fusion | flops 16777216 | bytes 8912896 | tf_op jit(solution)/shard_map/stack | solution.py:145
  357.6 7.9 %pad_maximum_fusion = bf16[2,16,32,64,64]{4,3,2,1,0:T(8,128)(2,1)} fusion(bf16[1,16,32,64,64]{4,3,2,1,0:T(8,128)(2,1)S(1)} %get-tuple-element.21, bf16[1,16,32,64,64]{4,3,2,1,0:T(8,128)(2,1)S(1)} %get-tuple-element.20), kind=kLoop, calls=%fused_computation | loop fusion | flops 4194304 | bytes 16777216 | tf_op jit(solution)/shard_map/stack | solution.py:145
  365.5 1.9 copy.155
  370.4 14.0 %all_gather.15 = bf16[128,16,128]{2,1,0:T(8,128)(2,1)S(1)} all-gather(bf16[32,16,128]{2,1,0:T(8,128)(2,1)S(1)} %convert_element_type.95), channel_id=1, replica_groups=mesh['gx'=8,'gy'=4] {'gy'}, dimensions={0}, use_global_device_ids=true | all-gather | bytes 655360 | tf_op jit(solution)/shard_map/all_gather | solution.py:104
  386.0 94.4 %all-reduce.2.cloned.1.call-done = f32[3,3,64,64]{3,2,1,0:T(8,128)} async-done(((f32[3,3,64,64]{3,2,1,0:T(8,128)}), f32[3,3,64,64]{3,2,1,0:T(8,128)}) %all-reduce.2.cloned.1.call-update) | async-done | bytes 147472 | tf_op jit(solution)/shard_map/psum | solution.py:174
  480.4 1.7 copy.219
  (142 shorter events, 33.9 us)
Async XLA Ops:
  7.2 30.9 %reduce-scatter.5.cloned.1.call-start = ((), (), s32[]{:S(2)}) async-start(), calls=%async_computation.4 | async-start | bytes 1310720 | tf_op jit(solution)/shard_map/reduce_scatter | solution.py:58
  11.7 80.2 %reduce-scatter.7.cloned.1.call-start = ((), (), s32[]{:S(2)}) async-start(), calls=%async_computation.5 | async-start | bytes 2359296 | tf_op jit(solution)/shard_map/reduce_scatter | solution.py:74
  45.3 4.5 copy-start
  49.7 101.5 %all-gather.3.cloned.1.call-start = ((), (), s32[]{:S(2)}) async-start(), calls=%async_computation.6 | async-start | bytes 1179648 | tf_op jit(solution)/shard_map/all_gather | solution.py:86
  49.9 78.0 %copy-start.5 = (bf16[64,16,128]{2,0,1:T(8,128)(2,1)}, bf16[64,16,128]{2,0,1:T(8,128)(2,1)S(1)}, u32[]{:S(2)}) copy-start(bf16[64,16,128]{2,0,1:T(8,128)(2,1)S(1)} %copy.118) | copy-start | bytes 786436
  49.9 6.2 %collective-permute-start.1 = (bf16[64,1,128]{2,0,1:T(8,128)(2,1)S(1)}, bf16[64,1,128]{2,0,1:T(8,128)(2,1)S(1)}, u32[]{:S(2)}, u32[]{:S(2)}) collective-permute-start(bf16[64,1,128]{2,0,1:T(8,128)(2,1)S(1)} %get-tuple-element.40), channel_id=1, source_target_pairs={{4,0},{8,4},{12,8},{16,12},{20,16},{24,20},{28,24},{0,28},{5,1},{9... | collective-permute-start | bytes 49160 | tf_op jit(solution)/shard_map/ppermute | solution.py:21
  51.8 4.2 collective-permute-start
  56.1 71.7 %copy-start.10 = (bf16[64,1,128]{2,0,1:T(8,128)(2,1)}, bf16[64,1,128]{2,0,1:T(8,128)(2,1)S(1)}, u32[]{:S(2)}) copy-start(bf16[64,1,128]{2,0,1:T(8,128)(2,1)S(1)} %collective-permute-done.1) | copy-start | bytes 49156
  57.0 73.5 %collective-permute-start.2 = (bf16[64,18,1]{2,0,1:T(8,128)(2,1)S(1)}, bf16[64,18,1]{2,0,1:T(8,128)(2,1)S(1)}, u32[]{:S(2)}, u32[]{:S(2)}) collective-permute-start(bf16[64,18,1]{2,0,1:T(8,128)(2,1)S(1)} %get-tuple-element.36), channel_id=1, source_target_pairs={{0,1},{1,2},{2,3},{3,0},{4,5},{5,6},{6,7},{7,4},{8,9},{9,10},{10,1... | collective-permute-start | bytes 6920 | tf_op jit(solution)/shard_map/ppermute | solution.py:20
  59.2 69.7 %collective-permute-start.3 = (bf16[64,18,1]{2,0,1:T(8,128)(2,1)}, bf16[64,18,1]{2,0,1:T(8,128)(2,1)S(1)}, u32[]{:S(2)}, u32[]{:S(2)}) collective-permute-start(bf16[64,18,1]{2,0,1:T(8,128)(2,1)} %get-tuple-element.37), channel_id=1, source_target_pairs={{1,0},{2,1},{3,2},{0,3},{5,4},{6,5},{7,6},{4,7},{9,8},{10,9},{11,1... | collective-permute-start | bytes 6920 | tf_op jit(solution)/shard_map/ppermute | solution.py:21
  93.1 18.9 %slice-start = ((s8[16777216]{0:T(1024)(128)(4,1)}), s8[4194304]{0:T(1024)(128)(4,1)S(1)}, s32[]{:S(2)}) async-start(s8[16777216]{0:T(1024)(128)(4,1)} %bitcast.383), calls=%async_computation.11 | async-start | bytes 8388608
  93.1 18.9 %slice-start.1 = ((s8[16777216]{0:T(1024)(128)(4,1)}), s8[4194304]{0:T(1024)(128)(4,1)S(1)}, s32[]{:S(2)}) async-start(s8[16777216]{0:T(1024)(128)(4,1)} %bitcast.383), calls=%async_computation.12 | async-start | bytes 8388608
  102.2 9.9 %slice-start.2 = ((s8[16777216]{0:T(1024)(128)(4,1)}), s8[4194304]{0:T(1024)(128)(4,1)S(1)}, s32[]{:S(2)}) async-start(s8[16777216]{0:T(1024)(128)(4,1)} %bitcast.383), calls=%async_computation.13 | async-start | bytes 8388608
  102.2 9.9 %slice-start.3 = ((s8[16777216]{0:T(1024)(128)(4,1)}), s8[4194304]{0:T(1024)(128)(4,1)S(1)}, s32[]{:S(2)}) async-start(s8[16777216]{0:T(1024)(128)(4,1)} %bitcast.383), calls=%async_computation.14 | async-start | bytes 8388608
  118.8 8.8 %copy-start.7 = (bf16[3,3,64,64]{3,2,1,0:T(8,128)(2,1)S(1)}, bf16[3,3,64,64]{3,2,1,0:T(8,128)(2,1)}, u32[]{:S(2)}) copy-start(bf16[3,3,64,64]{3,2,1,0:T(8,128)(2,1)} %param.6) | copy-start | bytes 221188
  127.6 76.9 %reduce-scatter.9.cloned.1.call-start = ((), (), s32[]{:S(2)}) async-start(), calls=%async_computation.7 | async-start | bytes 1310720 | tf_op jit(solution)/shard_map/reduce_scatter | solution.py:58
  128.9 2.7 copy-start.1
  130.5 45.5 %copy-start.3 = (bf16[64,18,1]{2,0,1:T(8,128)(2,1)}, bf16[64,18,1]{2,0,1:T(8,128)(2,1)S(1)}, u32[]{:S(2)}) copy-start(bf16[64,18,1]{2,0,1:T(8,128)(2,1)S(1)} %collective-permute-done.2) | copy-start | bytes 6916
  179.1 79.2 %reduce-scatter.11.cloned.1.call-start = ((), (), s32[]{:S(2)}) async-start(), calls=%async_computation.8 | async-start | bytes 2359296 | tf_op jit(solution)/shard_map/reduce_scatter | solution.py:74
  216.1 149.4 %all-gather.5.cloned.1.call-start = ((), (), s32[]{:S(2)}) async-start(), calls=%async_computation.9 | async-start | bytes 1179648 | tf_op jit(solution)/shard_map/all_gather | solution.py:86
  216.7 110.9 %collective-permute-start.4 = (bf16[64,1,128]{2,0,1:T(8,128)(2,1)S(1)}, bf16[64,1,128]{2,0,1:T(8,128)(2,1)S(1)}, u32[]{:S(2)}, u32[]{:S(2)}) collective-permute-start(bf16[64,1,128]{2,0,1:T(8,128)(2,1)S(1)} %get-tuple-element.38), channel_id=1, source_target_pairs={{0,4},{4,8},{8,12},{12,16},{16,20},{20,24},{24,28},{28,0},{1,5},{5... | collective-permute-start | bytes 49160 | tf_op jit(solution)/shard_map/ppermute | solution.py:20
  216.8 110.8 %collective-permute-start.5 = (bf16[64,1,128]{2,0,1:T(8,128)(2,1)S(1)}, bf16[64,1,128]{2,0,1:T(8,128)(2,1)S(1)}, u32[]{:S(2)}, u32[]{:S(2)}) collective-permute-start(bf16[64,1,128]{2,0,1:T(8,128)(2,1)S(1)} %get-tuple-element.39), channel_id=1, source_target_pairs={{4,0},{8,4},{12,8},{16,12},{20,16},{24,20},{28,24},{0,28},{5,1},{9... | collective-permute-start | bytes 49160 | tf_op jit(solution)/shard_map/ppermute | solution.py:21
  305.9 17.0 %copy-start.6 = (bf16[64,16,128]{2,0,1:T(8,128)(2,1)S(1)}, bf16[64,16,128]{2,0,1:T(8,128)(2,1)}, u32[]{:S(2)}) copy-start(bf16[64,16,128]{2,0,1:T(8,128)(2,1)} %copy-done.5) | copy-start | bytes 786436
  305.9 17.2 %copy-start.2 = (bf16[64,18,1]{2,0,1:T(8,128)(2,1)S(1)}, bf16[64,18,1]{2,0,1:T(8,128)(2,1)}, u32[]{:S(2)}) copy-start(bf16[64,18,1]{2,0,1:T(8,128)(2,1)} %copy-done.1) | copy-start | bytes 6916
  305.9 18.0 %copy-start.4 = (bf16[64,18,1]{2,0,1:T(8,128)(2,1)S(1)}, bf16[64,18,1]{2,0,1:T(8,128)(2,1)}, u32[]{:S(2)}) copy-start(bf16[64,18,1]{2,0,1:T(8,128)(2,1)} %copy-done.3) | copy-start | bytes 6916
  305.9 18.8 %copy-start.8 = (bf16[3,3,64,64]{3,2,1,0:T(8,128)(2,1)S(1)}, bf16[3,3,64,64]{3,2,1,0:T(8,128)(2,1)}, u32[]{:S(2)}) copy-start(bf16[3,3,64,64]{3,2,1,0:T(8,128)(2,1)} %param.6) | copy-start | bytes 221188
  322.9 157.5 %all-reduce.2.cloned.1.call-start = ((), (), s32[]{:S(2)}) async-start(), calls=%async_computation.10 | async-start | bytes 589824 | tf_op jit(solution)/shard_map/psum | solution.py:174
  323.9 22.9 %copy-start.9 = (bf16[64,16,128]{2,1,0:T(8,128)(2,1)S(1)}, bf16[64,16,128]{2,1,0:T(8,128)(2,1)}, u32[]{:S(2)}) copy-start(bf16[64,16,128]{2,1,0:T(8,128)(2,1)} %param.7) | copy-start | bytes 786436
  327.9 9.0 %collective-permute-start.6 = (bf16[64,18,1]{2,0,1:T(8,128)(2,1)S(1)}, bf16[64,18,1]{2,0,1:T(8,128)(2,1)S(1)}, u32[]{:S(2)}, u32[]{:S(2)}) collective-permute-start(bf16[64,18,1]{2,0,1:T(8,128)(2,1)S(1)} %get-tuple-element.34), channel_id=1, source_target_pairs={{1,0},{2,1},{3,2},{0,3},{5,4},{6,5},{7,6},{4,7},{9,8},{10,9},{11,1... | collective-permute-start | bytes 6920 | tf_op jit(solution)/shard_map/ppermute | solution.py:21
  328.5 16.4 %collective-permute-start.7 = (bf16[64,18,1]{2,0,1:T(8,128)(2,1)S(1)}, bf16[64,18,1]{2,0,1:T(8,128)(2,1)S(1)}, u32[]{:S(2)}, u32[]{:S(2)}) collective-permute-start(bf16[64,18,1]{2,0,1:T(8,128)(2,1)S(1)} %get-tuple-element.35), channel_id=1, source_target_pairs={{0,1},{1,2},{2,3},{3,0},{4,5},{5,6},{6,7},{7,4},{8,9},{9,10},{10,1... | collective-permute-start | bytes 6920 | tf_op jit(solution)/shard_map/ppermute | solution.py:20
Sparse Core Ops, SparseCore 0:
  11.8 26.2 reduce-scatter.4
  49.9 41.9 reduce-scatter.6
  127.7 23.4 all-gather.2
  179.2 25.1 reduce-scatter.8
  216.2 41.9 reduce-scatter.10
  323.0 23.4 all-gather.4
  352.4 127.9 all-reduce.1
where the time goes:
time: 498 us; the launch traced here: 489 us
  waiting for transfers between devices  250 us (50%)
  matrix products  131 us (26%)
  blocking collectives  30.3 us (6%)
  local copies, waits for them, and re-layouts  28.8 us (6%)
  other arithmetic  23.2 us (5%)
  between operations  15.2 us (3%)
  starting transfers between devices  10.1 us (2%)
    psum x1, waiting for transfers between devices, body(): kernel_grad = lax.psum(jnp.stack(tap_rows, 0), ('gx', 'gy'))  94.4 us
    reduce_scatter x2, waiting for transfers between devices, analyse(): lax.psum_scatter(jnp.stack([real_out, imag_out], 2).reshape(lax.axis_size...  67.3 us
    reduce_scatter x2, waiting for transfers between devices, analyse(): lax.psum_scatter(product.reshape(lax.axis_size('gy') * modes_y, block_row...  51.2 us
    dot_general x2, matrix products, body(): back_real = back(wreal, greal) + back(wimag, gimag)  31 us
    dot_general x2, matrix products, body(): back_imag = back(wreal, gimag) - back(wimag, greal)  30.7 us
    all_gather x2, blocking collectives, synthesise(): shard_rows = lax.all_gather(row_sum, 'gy', axis=0, tiled=True)  30.3 us
    all_gather x2, waiting for transfers between devices, synthesise(): lax.all_gather(modes.reshape(modes_x, modes_y, 2 * channels), 'gx', axis=...  19.6 us
    another operation x2, other arithmetic, body(): jnp.stack([outer(areal, greal) + outer(aimag, gimag), outer(areal, gimag)...  18 us
  transfers between devices with their start and end apart: 15, of which 9 were waited for; matrix products, arithmetic and copies ran while one was open for 29% of the time, Pallas kernels for 0%

commit v1 on v0

--- a/solution.py
+++ b/solution.py
@@ -3,7 +3,11 @@
 
 import jax
 import jax.numpy as jnp
+import ml_dtypes
+import numpy as np
 from jax import lax
+from jax.experimental import pallas as pl
+from jax.experimental.pallas import tpu as pltpu
 from jax.sharding import PartitionSpec as P
 
 KX = 128
@@ -32,7 +36,7 @@
     return extended(field, (("gx", 1), ("gy", 2)), 1)
 
 
-def body(field, spectral_weight, kernel_weight, cotangent):
+def general_body(field, spectral_weight, kernel_weight, cotangent):
     highest = lax.Precision.HIGHEST
     channels, block_rows, block_cols = field.shape
     rows_total = block_rows * lax.axis_size("gx")
@@ -178,6 +182,451 @@
     return (layer_out, field_grad, spectral_grad, kernel_grad)
 
 
+BF16 = jnp.bfloat16
+F32 = jnp.float32
+BOTH = ("gx", "gy")
+VMEM = 48 * 1024 * 1024
+
+
+def whole(count):
+    return [pl.BlockSpec(memory_space=pltpu.VMEM)] * count
+
+
+class Plan:
+    def __init__(self, channels, block_rows, block_cols, gx, gy):
+        self.gx, self.gy, self.devices = gx, gy, gx * gy
+        self.channels, self.bx, self.by = channels, block_rows, block_cols
+        self.nx, self.ny = block_rows * gx, block_cols * gy
+        self.mx, self.my = KX // gx, KY // gy
+        self.cpd = channels // self.devices if channels % self.devices == 0 else 0
+        self.lanes = self.cpd * 2 * self.my
+        self.fits = (
+            self.cpd > 0
+            and self.lanes == 128
+            and KX % gx == 0
+            and KY % gy == 0
+            and self.bx % 16 == 0
+            and self.by % 128 == 0
+            and self.mx % 16 == 0
+            and self.my % 8 == 0
+            and KX % 128 == 0
+            and self.nx % 128 == 0
+            and self.channels == 64
+        )
+        self.scale = 1.0 / math.sqrt(self.nx * self.ny)
+
+    def tables(self):
+        two_pi = np.float32(2.0 * math.pi)
+        waves, points = np.arange(KY), np.arange(self.ny)
+        angles = np.float32((waves[:, None] * points[None, :]) % self.ny) * (two_pi / self.ny)
+        cos, sin = np.cos(angles).T, np.sin(angles).T
+        col = np.zeros((self.cpd, self.ny, 2, self.gy, self.cpd, 2, self.my), np.float32)
+        for c in range(self.cpd):
+            split = (self.ny, self.gy, self.my)
+            col[c, :, 0, :, c, 0] = cos.reshape(split)
+            col[c, :, 0, :, c, 1] = -sin.reshape(split)
+            col[c, :, 1, :, c, 0] = -sin.reshape(split)
+            col[c, :, 1, :, c, 1] = -cos.reshape(split)
+        col = col.reshape(self.cpd * self.ny, -1).astype(ml_dtypes.bfloat16)
+        rows = np.arange(KX) - KX // 2
+        points = np.arange(self.nx)
+        angles = np.float32((rows[:, None] * points[None, :]) % self.nx) * (two_pi / self.nx)
+        row = np.concatenate([np.cos(angles), np.sin(angles)], 1).astype(np.float32)
+        high = row.astype(ml_dtypes.bfloat16)
+        low = (row - high.astype(np.float32)).astype(ml_dtypes.bfloat16)
+        row_analysis = np.concatenate([high, low], 1)
+        row_synthesis = np.concatenate([np.cos(angles).T, np.sin(angles).T], 0)
+        row_synthesis = row_synthesis.astype(ml_dtypes.bfloat16)
+        doubled = np.full((self.gy, self.cpd, 2, self.my), 2.0, np.float32)
+        doubled[0, :, :, 0] = 1.0
+        doubled = doubled.reshape(1, -1)
+        return col, np.ascontiguousarray(col.T), row_analysis, row_synthesis, doubled
+
+
+def dot(a, b):
+    return jnp.dot(a, b, preferred_element_type=F32)
+
+
+def analyse_plane(plan, planes, col, row, weight, out_ref):
+    half = col.shape[1] // 2
+    along_y = dot(planes, col[...]).astype(BF16)
+    stacked = jnp.concatenate([along_y[:, :half], along_y[:, half:]], 0)
+    modes = dot(row[...], jnp.concatenate([stacked, stacked], 0)) * weight
+    modes = modes.astype(BF16)
+    for i in range(plan.gx):
+        for k in range(plan.gy):
+            out_ref[i * plan.gy + k] = modes[
+                i * plan.mx : (i + 1) * plan.mx, k * plan.lanes : (k + 1) * plan.lanes
+            ]
+
+
+def synthesise_plane(plan, modes_ref, row, col_t, weight):
+    columns = []
+    for k in range(plan.gy):
+        columns.append(jnp.concatenate([modes_ref[i * plan.gy + k] for i in range(plan.gx)], 0))
+    sums = dot(row[...], jnp.concatenate(columns, 1))
+    if weight is not None:
+        sums = sums * weight
+    sums = sums.astype(BF16)
+    return dot(jnp.concatenate([sums[: plan.nx], sums[plan.nx :]], 1), col_t[...])
+
+
+def read_plane(plan, ref, c, k):
+    return jnp.concatenate([ref[i * plan.gy + k, c] for i in range(plan.gx)], 0)
+
+
+def write_planes(plan, ref, planes):
+    for c in range(plan.cpd):
+        for k in range(plan.gy):
+            start = c * plan.ny + k * plan.by
+            for i in range(plan.gx):
+                ref[i * plan.gy + k, c] = planes[
+                    i * plan.bx : (i + 1) * plan.bx, start : start + plan.by
+                ]
+
+
+def first_kernel(plan, field_ref, col, row, out_ref):
+    planes = [read_plane(plan, field_ref, c, k) for c in range(plan.cpd) for k in range(plan.gy)]
+    analyse_plane(plan, jnp.concatenate(planes, 1), col, row, plan.scale, out_ref)
+
+
+def gelu_parts(z):
+    cubic = math.sqrt(2.0 / math.pi)
+    inner = cubic * (z + 0.044715 * (z * z * z))
+    tanh = jnp.tanh(inner)
+    cdf = 0.5 * (1.0 + tanh)
+    slope = cdf + 0.5 * z * (1.0 - tanh * tanh) * (cubic * (1.0 + (3.0 * 0.044715) * (z * z)))
+    return z * cdf, slope
+
+
+def middle_kernel(
+    plan, modes_ref, conv_ref, cot_ref, col, col_t, row, row_s, doubled, out_ref, z_ref, grads
+):
+    syn = synthesise_plane(plan, modes_ref, row_s, col_t, doubled[...]) * plan.scale
+    for c in range(plan.cpd):
+        for k in range(plan.gy):
+            start = c * plan.ny + k * plan.by
+            z = syn[:, start : start + plan.by] + read_plane(plan, conv_ref, c, k).astype(F32)
+            z = z.astype(BF16)
+            for i in range(plan.gx):
+                z_ref[i * plan.gy + k, c] = z[i * plan.bx : (i + 1) * plan.bx]
+            slope = gelu_parts(z.astype(F32))[1]
+            cot = read_plane(plan, cot_ref, c, k).astype(F32)
+            grads[:, start : start + plan.by] = (cot * slope).astype(BF16)
+    analyse_plane(plan, grads[...], col, row, doubled[...] * plan.scale, out_ref)
+
+
+def last_kernel(plan, modes_ref, col_t, row_s, syn_ref):
+    syn = synthesise_plane(plan, modes_ref, row_s, col_t, None) * plan.scale
+    write_planes(plan, syn_ref, syn.astype(BF16))
+
+
+def group_mask(rows, groups, width):
+    row = lax.broadcasted_iota(jnp.int32, (rows, groups * width), 0)
+    lane = lax.broadcasted_iota(jnp.int32, (rows, groups * width), 1)
+    return lax.rem(row, groups) == lax.div(lane, width)
+
+
+def modes_to_rows(plan, x_ref, scratch):
+    half = plan.lanes // 2
+    values = x_ref[...].astype(F32)
+    for j in range(plan.mx):
+        turned = values[:, j, :].T
+        scratch[j] = jnp.concatenate([turned[:half], turned[half:]], 1)
+
+
+def rows_to_modes(plan, y_scratch, y_ref):
+    y_ref[...] = jnp.swapaxes(y_scratch[...], 0, 1).astype(BF16)
+
+
+def put_rows(plan, rows, y_scratch, j):
+    turned = rows.T
+    s = plan.devices
+    y_scratch[j] = jnp.concatenate([turned[i * s : (i + 1) * s] for i in range(plan.cpd)], 1)
+
+
+def mix_kernel(plan, x_ref, r_ref, y_ref, rows, y_scratch):
+    j = pl.program_id(0)
+
+    @pl.when(j == 0)
+    def _():
+        modes_to_rows(plan, x_ref, rows)
+
+    group, width = 8, plan.channels
+    mask = group_mask(2 * group, group, width)
+    real_out, imag_out = [], []
+    for g in range(plan.my // group):
+        real = rows[j, g * group : (g + 1) * group, :]
+        imag = rows[j, plan.my + g * group : plan.my + (g + 1) * group, :]
+        first = jnp.concatenate([jnp.concatenate([real, imag], 0)] * group, 1)
+        second = jnp.concatenate([jnp.concatenate([-imag, real], 0)] * group, 1)
+        first = jnp.where(mask, first, 0.0).astype(BF16)
+        second = jnp.where(mask, second, 0.0).astype(BF16)
+        r_real = r_ref[0, 0, g * group : (g + 1) * group].reshape(group * width, width)
+        r_imag = r_ref[1, 0, g * group : (g + 1) * group].reshape(group * width, width)
+        mixed = dot(first, r_real) + dot(second, r_imag)
+        real_out.append(mixed[:group])
+        imag_out.append(mixed[group:])
+    put_rows(plan, jnp.concatenate(real_out + imag_out, 0), y_scratch, j)
+
+    @pl.when(j == plan.mx - 1)
+    def _():
+        rows_to_modes(plan, y_scratch, y_ref)
+
+
+def dot_nt(a, b):
+    return lax.dot_general(a, b, (((1,), (1,)), ((), ())), preferred_element_type=F32)
+
+
+def back_kernel(plan, g_ref, r_ref, y_ref, rows, y_scratch):
+    j = pl.program_id(0)
+
+    @pl.when(j == 0)
+    def _():
+        modes_to_rows(plan, g_ref, rows)
+
+    group, width = 8, plan.channels
+    mask = group_mask(2 * group, group, width)
+    real_out, imag_out = [], []
+    for g in range(plan.my // group):
+        real = rows[j, g * group : (g + 1) * group, :]
+        imag = rows[j, plan.my + g * group : plan.my + (g + 1) * group, :]
+        first = jnp.concatenate([real, imag], 0).astype(BF16)
+        second = jnp.concatenate([imag, -real], 0).astype(BF16)
+        r_real = r_ref[0, 0, g * group : (g + 1) * group].reshape(group * width, width)
+        r_imag = r_ref[1, 0, g * group : (g + 1) * group].reshape(group * width, width)
+        mixed = dot_nt(first, r_real) + dot_nt(second, r_imag)
+        mixed = jnp.where(mask, mixed, 0.0)
+        total = mixed[:, :width]
+        for i in range(1, group):
+            total = total + mixed[:, i * width : (i + 1) * width]
+        real_out.append(total[:group])
+        imag_out.append(total[group:])
+    put_rows(plan, jnp.concatenate(real_out + imag_out, 0), y_scratch, j)
+
+    @pl.when(j == plan.mx - 1)
+    def _():
+        rows_to_modes(plan, y_scratch, y_ref)
+
+
+def outer_kernel(plan, x_ref, g_ref, out_ref, a_rows, g_rows):
+    j = pl.program_id(0)
+
+    @pl.when(j == 0)
+    def _():
+        modes_to_rows(plan, x_ref, a_rows)
+        modes_to_rows(plan, g_ref, g_rows)
+
+    my, width = plan.my, plan.channels
+    a_turned = a_rows[j].T
+    g_real, g_imag = g_rows[j, :my, :], g_rows[j, my:, :]
+    first = jnp.concatenate([g_real, g_imag], 0).astype(BF16)
+    second = jnp.concatenate([g_imag, -g_real], 0).astype(BF16)
+    lane = lax.rem(lax.broadcasted_iota(jnp.int32, (width, 2 * my), 1), my)
+    group = 8
+    for g in range(my // group):
+        left = jnp.concatenate(
+            [jnp.where(lane == g * group + l, a_turned, 0.0) for l in range(group)], 0
+        ).astype(BF16)
+        for part, right in ((0, first), (1, second)):
+            value = dot(left, right).astype(BF16)
+            out_ref[part, 0, g * group : (g + 1) * group] = value.reshape(group, width, width)
+
+
+def shift_kernel(plan, block_ref, rows_ref, cols_ref, weights_ref, after_ref, out_ref, taps_ref):
+    c, by, bx = plan.channels, plan.by, plan.bx
+    lane = lax.broadcasted_iota(jnp.int32, (c, by), 1)
+    for x in range(bx + 2):
+        if x == 0:
+            row = rows_ref[0]
+        elif x == bx + 1:
+            row = rows_ref[1]
+        else:
+            row = block_ref[:, (x - 1) * by : x * by]
+        lanes = slice(x * by, (x + 1) * by)
+        wide = row.astype(F32)
+        left = cols_ref[0, :, x : x + 1].astype(F32)
+        right = cols_ref[1, :, x : x + 1].astype(F32)
+        taps_ref[:c, lanes] = jnp.where(lane == 0, left, pltpu.roll(wide, 1, 1)).astype(BF16)
+        taps_ref[c : 2 * c, lanes] = row
+        taps_ref[2 * c :, lanes] = jnp.where(
+            lane == by - 1, right, pltpu.roll(wide, by - 1, 1)
+        ).astype(BF16)
+    for a in range(3):
+        part = dot(weights_ref[a], taps_ref[:, a * by : (a + bx) * by])
+        if a == 0:
+            total = part
+        else:
+            total = total + part
+    out_ref[...] = total.astype(out_ref.dtype)
+
+
+def taps_kernel(plan, grads_ref, taps_ref, out_ref):
+    for a in range(3):
+        out_ref[a] = dot_nt(grads_ref[...], taps_ref[:, a * plan.by : (a + plan.bx) * plan.by])
+
+
+def halo(block):
+    def swap(low, high, axis):
+        count = lax.axis_size(axis)
+        up = [(i, (i + 1) % count) for i in range(count)]
+        down = [(j, i) for i, j in up]
+        return lax.ppermute(high, axis, up), lax.ppermute(low, axis, down)
+
+    top, bottom = swap(block[:, 0, :], block[:, -1, :], "gx")
+
+    def column(y):
+        return jnp.concatenate([top[:, y, None], block[:, :, y], bottom[:, y, None]], 1)
+
+    left, right = swap(column(0), column(-1), "gy")
+    return jnp.stack([top, bottom], 0), jnp.stack([left, right], 0)
+
+
+def fast_body(plan, field, spectral_weight, kernel_weight, cotangent):
+    channels, bx, by, n, cpd = plan.channels, plan.bx, plan.by, plan.devices, plan.cpd
+    col, col_t, row, row_s, doubled = (jnp.asarray(t) for t in plan.tables())
+    params = pltpu.CompilerParams(vmem_limit_bytes=VMEM)
+    mode_shape = jax.ShapeDtypeStruct((n, plan.mx, plan.lanes), BF16)
+    block_shape = jax.ShapeDtypeStruct((n, cpd, bx, by), BF16)
+    taps_shape = jax.ShapeDtypeStruct((3 * channels, (bx + 2) * by), BF16)
+    anywhere = pl.BlockSpec(memory_space=pl.ANY)
+
+    def exchange(x):
+        return lax.all_to_all(x, BOTH, 0, 0, tiled=True)
+
+    def to_channels(x):
+        return exchange(x.reshape(cpd, n, bx, by).transpose(1, 0, 2, 3))
+
+    def to_space(x):
+        return x.transpose(1, 0, 2, 3).reshape(channels, bx, by)
+
+    def call(kernel, out_shape, *args, scratch=(), last=None):
+        several = isinstance(out_shape, tuple)
+        specs = whole(len(args))
+        if last is not None:
+            specs, args = specs + [anywhere], args + (last,)
+        return pl.pallas_call(
+            partial(kernel, plan),
+            out_shape=out_shape,
+            in_specs=specs,
+            out_specs=tuple(whole(len(out_shape))) if several else whole(1)[0],
+            scratch_shapes=scratch,
+            compiler_params=params,
+        )(*args)
+
+    weight_spec = pl.BlockSpec(
+        (2, 1, plan.my, channels, channels), lambda j: (0, j, 0, 0, 0)
+    )
+    mode_spec = pl.BlockSpec((n, plan.mx, plan.lanes), lambda j: (0, 0, 0))
+    rows_scratch = pltpu.VMEM((plan.mx, 2 * plan.my, channels), F32)
+    y_scratch = pltpu.VMEM((plan.mx, n, plan.lanes), F32)
+
+    def mode_call(kernel, x):
+        return pl.pallas_call(
+            partial(kernel, plan),
+            grid=(plan.mx,),
+            out_shape=mode_shape,
+            in_specs=[mode_spec, weight_spec],
+            out_specs=mode_spec,
+            scratch_shapes=[rows_scratch, y_scratch],
+            compiler_params=params,
+        )(x, spectral_weight)
+
+    forward_weight = kernel_weight.transpose(0, 2, 1, 3).reshape(3, channels, 3 * channels)
+    adjoint_weight = kernel_weight[::-1, ::-1].transpose(0, 3, 1, 2)
+    adjoint_weight = adjoint_weight.reshape(3, channels, 3 * channels)
+
+    field_c = to_channels(field)
+    a_part = call(first_kernel, mode_shape, field_c, col, row)
+    a_modes = exchange(a_part)
+    edge_rows, edge_cols = halo(field)
+    conv, taps = call(
+        shift_kernel,
+        (jax.ShapeDtypeStruct((channels, bx * by), BF16), taps_shape),
+        field.reshape(channels, bx * by),
+        edge_rows,
+        edge_cols,
+        forward_weight,
+        last=a_part,
+    )
+    cotangent_late, _ = lax.optimization_barrier((cotangent, a_part))
+    cot_c = to_channels(cotangent_late)
+    conv_c = to_channels(conv)
+
+    b_modes = exchange(mode_call(mix_kernel, a_modes))
+    g_part, z_part = call(
+        middle_kernel,
+        (mode_shape, block_shape),
+        b_modes,
+        conv_c,
+        cot_c,
+        col,
+        col_t,
+        row,
+        row_s,
+        doubled,
+        scratch=[pltpu.VMEM((plan.nx, cpd * plan.ny), BF16)],
+    )
+    g_modes = exchange(g_part)
+    hidden = to_space(exchange(z_part)).astype(F32)
+    activated, slope = gelu_parts(hidden)
+    layer_out = (field.astype(F32) + activated).astype(BF16)
+    grads = (cotangent.astype(F32) * slope).astype(BF16)
+    grads_flat = grads.reshape(channels, bx * by)
+    kernel_terms = call(
+        taps_kernel, jax.ShapeDtypeStruct((3, channels, 3 * channels), F32), grads_flat, taps
+    )
+    back_part = mode_call(back_kernel, g_modes)
+    piece = 9 * channels * channels // (n * 128)
+    terms = kernel_terms.reshape(n, piece, 128).astype(BF16)
+    terms = jnp.pad(terms, ((0, 0), (0, -piece % 16), (0, 0)))
+    back_both = exchange(jnp.concatenate([back_part, terms], 1))
+    back_modes = back_both[:, : plan.mx]
+    summed = back_both[:, plan.mx :].astype(F32).sum(0).astype(BF16)
+    synthesis_part = call(last_kernel, block_shape, back_modes, col_t, row_s)
+    last_part = jnp.concatenate(
+        [
+            synthesis_part.reshape(n, cpd * bx, by),
+            jnp.broadcast_to(summed[None], (n,) + summed.shape),
+        ],
+        1,
+    )
+    last_both = exchange(last_part)
+    synthesis = to_space(last_both[:, : cpd * bx].reshape(n, cpd, bx, by))
+    kernel_grad = last_both[:, cpd * bx : cpd * bx + piece].astype(F32)
+    kernel_grad = kernel_grad.reshape(3, channels, 3, channels).transpose(0, 2, 1, 3)
+
+    spectral_grad = pl.pallas_call(
+        lambda x, g, after, *rest: outer_kernel(plan, x, g, *rest),
+        grid=(plan.mx,),
+        out_shape=jax.ShapeDtypeStruct(spectral_weight.shape, BF16),
+        in_specs=[mode_spec, mode_spec, anywhere],
+        out_specs=weight_spec,
+        scratch_shapes=[rows_scratch, rows_scratch],
+        compiler_params=params,
+    )(a_modes, g_modes, back_part)
+
+    grad_rows, grad_cols = halo(grads)
+    adjoint, _ = call(
+        shift_kernel,
+        (jax.ShapeDtypeStruct((channels, bx * by), F32), taps_shape),
+        grads_flat,
+        grad_rows,
+        grad_cols,
+        adjoint_weight,
+        last=back_part,
+    )
+    field_grad = cotangent.astype(F32) + adjoint.reshape(channels, bx, by) + synthesis.astype(F32)
+    return (layer_out, field_grad.astype(BF16), spectral_grad, kernel_grad)
+
+
+def body(field, spectral_weight, kernel_weight, cotangent):
+    plan = Plan(*field.shape, lax.axis_size("gx"), lax.axis_size("gy"))
+    if plan.fits:
+        return fast_body(plan, field, spectral_weight, kernel_weight, cotangent)
+    return general_body(field, spectral_weight, kernel_weight, cotangent)
+
+
 def solution(mesh):
     in_specs = (P(None, "gx", "gy"), P(None, "gx", "gy", None, None), P(), P(None, "gx", "gy"))
     out_specs = (P(None, "gx", "gy"), P(None, "gx", "gy"), P(None, "gx", "gy", None, None), P())

time: 498 us -> 180 us (0.36); the launches traced: 489 us -> 178 us
  waiting for transfers between devices: 250 us -> 24.8 us
  matrix products: 131 us -> 0 us
  Pallas kernels: 0 us -> 51.1 us
  starting transfers between devices: 10.1 us -> 45.1 us
  other arithmetic: 23.2 us -> 6.42 us
  between operations: 15.2 us -> 1 us
  blocking collectives: 30.3 us -> 23.3 us
    dot_general x55 -> x0, matrix products: 131 us -> none  [the longest x2 31 us: body(): back_real = back(wreal, greal) + back(wimag, gimag)]
    reduce_scatter x4 -> x0, waiting for transfers between devices: 119 us -> none  [the longest x2 67.3 us: analyse(): lax.psum_scatter(jnp.stack([real_out, imag_out], 2).reshape(lax.axis_size...]
    psum x1 -> x0, waiting for transfers between devices: 94.4 us -> none  [body(): kernel_grad = lax.psum(jnp.stack(tap_rows, 0), ('gx', 'gy'))]
    pallas_call x0 -> x9, Pallas kernels: none -> 51.1 us  [the longest x2 31.7 us: mode_call(): pl.pallas_call(partial(kernel, plan), grid=(plan.mx,), out_shape=mode_sha...]
    all_to_all x0 -> x7, starting transfers between devices: none -> 35.8 us  [exchange(): return lax.all_to_all(x, BOTH, 0, 0, tiled=True)]
    all_gather x2 -> x0, blocking collectives: 30.3 us -> none  [synthesise(): shard_rows = lax.all_gather(row_sum, 'gy', axis=0, tiled=True)]
    all_to_all x0 -> x2, blocking collectives: none -> 23.3 us  [exchange(): return lax.all_to_all(x, BOTH, 0, 0, tiled=True)]
    another operation x11 -> x4, other arithmetic: 20.1 us -> 0.03 us  [halo(): return (jnp.stack([top, bottom], 0), jnp.stack([left, right], 0))]
  transfers between devices with their start and end apart: 15 -> 15, of which waited for: 9 -> 5; matrix products, arithmetic and copies ran while one was open for 29% -> 10% of each run, Pallas kernels for 0% -> 27%
where the time goes in v1:
time: 180 us; the launch traced here: 178 us
  Pallas kernels  51.1 us (28%)
  starting transfers between devices  45.1 us (25%)
  local copies, waits for them, and re-layouts  25.9 us (14%)
  waiting for transfers between devices  24.8 us (14%)
  blocking collectives  23.3 us (13%)
  other arithmetic  6.42 us (4%)
    all_to_all x7, starting transfers between devices, exchange(): return lax.all_to_all(x, BOTH, 0, 0, tiled=True)  35.8 us
    pallas_call x2, Pallas kernels, mode_call(): pl.pallas_call(partial(kernel, plan), grid=(plan.mx,), out_shape=mode_sha...  31.7 us
    all_to_all x2, blocking collectives, exchange(): return lax.all_to_all(x, BOTH, 0, 0, tiled=True)  23.3 us
    ppermute x8, waiting for transfers between devices, swap(): return (lax.ppermute(high, axis, up), lax.ppermute(low, axis, down))  14 us
    unnamed x38, local copies, waits for them, and re-layouts  12.7 us
    pallas_call x1, Pallas kernels, fast_body(): pl.pallas_call(lambda x, g, after, *rest: outer_kernel(plan, x, g, *rest)...  12.7 us
    all_to_all x7, waiting for transfers between devices, exchange(): return lax.all_to_all(x, BOTH, 0, 0, tiled=True)  10.9 us
    ppermute x8, starting transfers between devices, swap(): return (lax.ppermute(high, axis, up), lax.ppermute(low, axis, down))  9.31 us
  transfers between devices with their start and end apart: 15, of which 5 were waited for; matrix products, arithmetic and copies ran while one was open for 10% of the time, Pallas kernels for 27%

profile of v1, /device:TPU:8, one launch (start us, length us, event | category | flops | bytes accessed | tf_op | source)
XLA Modules:
  0.0 177.6 jit_solution(16535788315552363757)
XLA Ops:
  0.7 1.7 copy.155
  2.4 6.0 %all-to-all-start = ((bf16[32,2,16,128]{3,2,1,0:T(8,128)(2,1)}), bf16[32,2,16,128]{3,2,1,0:T(8,128)(2,1)S(1)}, u32[]{:S(2)}, u32[]{:S(2)}) async-start(bf16[32,2,16,128]{3,2,1,0:T(8,128)(2,1)} %bitcast.80), calls=%async_computation | async-start | bytes 524288 | tf_op jit(solution)/shard_map/all_to_all | solution.py:495
  8.4 1.0 copy.115
  9.7 2.5 %collective-permute-start.1 = (bf16[64,128]{1,0:T(8,128)(2,1)S(1)}, bf16[64,128]{1,0:T(8,128)(2,1)S(1)}, u32[]{:S(2)}, u32[]{:S(2)}) collective-permute-start(bf16[64,128]{1,0:T(8,128)(2,1)S(1)} %get-tuple-element.47), channel_id=1, source_target_pairs={{4,0},{8,4},{12,8},{16,12},{20,16},{24,20},{28,24},{0,28},{5,1},{9... | collective-permute-start | bytes 49160 | tf_op jit(solution)/shard_map/ppermute | solution.py:474
  12.2 5.8 %all-to-all-done.field_ref = bf16[32,2,16,128]{3,2,1,0:T(8,128)(2,1)S(1)} async-done(((bf16[32,2,16,128]{3,2,1,0:T(8,128)(2,1)}), bf16[32,2,16,128]{3,2,1,0:T(8,128)(2,1)S(1)}, u32[]{:S(2)}, u32[]{:S(2)}) %all-to-all-start) | async-done | bytes 262176 | tf_op jit(solution)/shard_map/all_to_all | solution.py:495
  18.0 1.6 copy-done
  19.6 0.9 copy-done.6
  20.5 1.3 shard_map.120.after_ref
  21.8 3.4 %all-to-all-start.1 = ((bf16[32,16,128]{2,1,0:T(8,128)(2,1)}), bf16[32,16,128]{2,1,0:T(8,128)(2,1)S(1)}, u32[]{:S(2)}, u32[]{:S(2)}) async-start(bf16[32,16,128]{2,1,0:T(8,128)(2,1)} %shard_map.120.after_ref), calls=%async_computation.1 | async-start | bytes 262144 | tf_op jit(solution)/shard_map/all_to_all | solution.py:495
  25.2 1.9 %fusion.18 = (bf16[64,16,1]{2,1,0:T(8,128)(2,1)}, bf16[64,16,1]{2,1,0:T(8,128)(2,1)S(1)}) fusion(bf16[64,16,128]{2,1,0:T(8,128)(2,1)} %param.9), kind=kLoop, calls=%fused_computation.47 | loop fusion | bytes 8192 | tf_op jit(solution)/shard_map/slice | solution.py:479
  27.1 1.0 copy.121
  28.2 1.0 copy.153
  29.3 1.4 copy.138
  31.8 15.5 %shard_map.121 = bf16[32,16,128]{2,1,0:T(8,128)(2,1)} custom-call(bf16[32,16,128]{2,1,0:T(8,128)(2,1)S(1)} %all-to-all-done.1.x_ref.x, bf16[2,16,32,64,64]{4,3,2,1,0:T(8,128)(2,1)} %r_ref.3), custom_call_target="tpu_custom_call" | custom-call | tf_op jit(solution)/shard_map/pallas_call | solution.py:525
  47.3 5.8 %all-to-all-start.2 = ((bf16[32,16,128]{2,1,0:T(8,128)(2,1)}), bf16[32,16,128]{2,1,0:T(8,128)(2,1)S(1)}, u32[]{:S(2)}, u32[]{:S(2)}) async-start(bf16[32,16,128]{2,1,0:T(8,128)(2,1)} %shard_map.121), calls=%async_computation.2 | async-start | bytes 262144 | tf_op jit(solution)/shard_map/all_to_all | solution.py:495
  53.2 1.4 pad_maximum_fusion.6
  55.6 3.6 %all-to-all-done.2.modes_ref = bf16[32,16,128]{2,1,0:T(8,128)(2,1)S(1)} async-done(((bf16[32,16,128]{2,1,0:T(8,128)(2,1)}), bf16[32,16,128]{2,1,0:T(8,128)(2,1)S(1)}, u32[]{:S(2)}, u32[]{:S(2)}) %all-to-all-start.2) | async-done | bytes 131104 | tf_op jit(solution)/shard_map/all_to_all | solution.py:495
  59.2 4.8 %all-to-all-start.4 = ((bf16[32,2,16,128]{3,2,1,0:T(8,128)(2,1)}), bf16[32,2,16,128]{3,2,1,0:T(8,128)(2,1)S(1)}, u32[]{:S(2)}, u32[]{:S(2)}) async-start(bf16[32,2,16,128]{3,2,1,0:T(8,128)(2,1)} %bitcast.91), calls=%async_computation.4 | async-start | bytes 524288 | tf_op jit(solution)/shard_map/all_to_all | solution.py:495
  64.1 1.6 collective-permute-start.2
  65.7 4.8 %collective-permute-done.2 = bf16[64,18]{1,0:T(8,128)(2,1)S(1)} collective-permute-done((bf16[64,18]{1,0:T(8,128)(2,1)S(1)}, bf16[64,18]{1,0:T(8,128)(2,1)S(1)}, u32[]{:S(2)}, u32[]{:S(2)}) %collective-permute-start.2) | collective-permute-done | bytes 2336 | tf_op jit(solution)/shard_map/ppermute | solution.py:474
  70.5 0.9 shard_map.122
  71.4 0.9 copy-done.4
  72.4 1.4 all-to-all-done.4.cot_ref
  73.8 14.0 %all_to_all.45.conv_ref = bf16[32,2,16,128]{3,2,1,0:T(8,128)(2,1)S(1)} all-to-all(bf16[32,2,16,128]{3,2,1,0:T(8,128)(2,1)S(1)} %copy_bitcast_fusion.3), channel_id=1, replica_groups=mesh['gx'=8,'gy'=4] {'gx','gy'}, dimensions={0} | all-to-all | bytes 524288 | tf_op jit(solution)/shard_map/all_to_all | solution.py:495
  87.8 1.6 copy-done.2
  89.4 1.6 shard_map.123
  91.0 9.3 %all_to_all.46.g_ref.g = bf16[32,16,128]{2,1,0:T(8,128)(2,1)S(1)} all-to-all(bf16[32,16,128]{2,1,0:T(8,128)(2,1)S(1)} %get-tuple-element.13), channel_id=1, replica_groups=mesh['gx'=8,'gy'=4] {'gx','gy'}, dimensions={0} | all-to-all | bytes 262144 | tf_op jit(solution)/shard_map/all_to_all | solution.py:495
  100.3 4.8 %all-to-all-start.5 = ((bf16[32,2,16,128]{3,2,1,0:T(8,128)(2,1)}), bf16[32,2,16,128]{3,2,1,0:T(8,128)(2,1)S(1)}, u32[]{:S(2)}, u32[]{:S(2)}) async-start(bf16[32,2,16,128]{3,2,1,0:T(8,128)(2,1)} %get-tuple-element.12), calls=%async_computation.5 | async-start | bytes 524288 | tf_op jit(solution)/shard_map/all_to_all | solution.py:495
  105.1 16.2 %shard_map.124.after_ref.after = bf16[32,16,128]{2,1,0:T(8,128)(2,1)S(1)} custom-call(bf16[32,16,128]{2,1,0:T(8,128)(2,1)S(1)} %all_to_all.46.g_ref.g, bf16[2,16,32,64,64]{4,3,2,1,0:T(8,128)(2,1)} %r_ref.3), custom_call_target="tpu_custom_call" | custom-call | tf_op jit(solution)/shard_map/pallas_call | solution.py:525
  121.8 1.1 fusion
  123.0 1.2 copy-done.5
  124.2 0.8 shard_map.126
  125.0 0.8 convert_element_type.56
  125.8 1.6 fusion.15
  127.5 6.0 %all-to-all-start.7 = ((bf16[32,32,128]{2,1,0:T(8,128)(2,1)}), bf16[32,32,128]{2,1,0:T(8,128)(2,1)}, u32[]{:S(2)}, u32[]{:S(2)}) async-start(bf16[32,32,128]{2,1,0:T(8,128)(2,1)} %fusion.15), calls=%async_computation.7 | async-start | bytes 524288 | tf_op jit(solution)/shard_map/all_to_all | solution.py:495
  133.5 1.6 rev.3
  135.0 1.0 copy.130.weights_ref
  136.1 12.7 %shard_map.128 = bf16[2,16,32,64,64]{4,3,2,1,0:T(8,128)(2,1)} custom-call(bf16[32,16,128]{2,1,0:T(8,128)(2,1)S(1)} %all-to-all-done.1.x_ref.x, bf16[32,16,128]{2,1,0:T(8,128)(2,1)S(1)} %all_to_all.46.g_ref.g, bf16[32,16,128]{2,1,0:T(8,128)(2,1)S(1)} %shard_map.124.after_ref.after), custom_call_target="tpu_custom_call" | custom-call | tf_op jit(solution)/shard_map/pallas_call | solution.py:599
  148.8 0.9 copy.133
  149.8 2.5 %collective-permute-start.5 = (bf16[64,128]{1,0:T(8,128)(2,1)S(1)}, bf16[64,128]{1,0:T(8,128)(2,1)S(1)}, u32[]{:S(2)}, u32[]{:S(2)}) collective-permute-start(bf16[64,128]{1,0:T(8,128)(2,1)S(1)} %get-tuple-element.43), channel_id=1, source_target_pairs={{4,0},{8,4},{12,8},{16,12},{20,16},{24,20},{28,24},{0,28},{5,1},{9... | collective-permute-start | bytes 49160 | tf_op jit(solution)/shard_map/ppermute | solution.py:474
  152.3 0.8 fusion.17
  153.1 1.4 copy.136
  155.1 1.0 fusion.16
  157.5 4.9 %all-to-all-start.8 = ((bf16[32,48,128]{2,1,0:T(8,128)(2,1)}), bf16[32,48,128]{2,1,0:T(8,128)(2,1)S(1)}, u32[]{:S(2)}, u32[]{:S(2)}) async-start(bf16[32,48,128]{2,1,0:T(8,128)(2,1)} %pad_maximum_fusion), calls=%async_computation.8 | async-start | bytes 786432 | tf_op jit(solution)/shard_map/all_to_all | solution.py:495
  163.1 1.8 %collective-permute-start.6 = (bf16[64,18]{1,0:T(8,128)(2,1)S(1)}, bf16[64,18]{1,0:T(8,128)(2,1)S(1)}, u32[]{:S(2)}, u32[]{:S(2)}) collective-permute-start(bf16[64,18]{1,0:T(8,128)(2,1)S(1)} %pad_maximum_fusion.7), channel_id=1, source_target_pairs={{0,1},{1,2},{2,3},{3,0},{4,5},{5,6},{6,7},{7,4},{8,9},{9,10},{10,1... | collective-permute-start | bytes 6920 | tf_op jit(solution)/shard_map/ppermute | solution.py:474
  164.9 9.2 %collective-permute-done.7 = bf16[64,18]{1,0:T(8,128)(2,1)S(1)} collective-permute-done((bf16[64,18]{1,0:T(8,128)(2,1)S(1)}, bf16[64,18]{1,0:T(8,128)(2,1)S(1)}, u32[]{:S(2)}, u32[]{:S(2)}) %collective-permute-start.7) | collective-permute-done | bytes 2336 | tf_op jit(solution)/shard_map/ppermute | solution.py:474
  174.1 1.5 shard_map.125
  176.8 0.9 copy.134
  (71 shorter events, 7.0 us)
Async XLA Ops:
  0.6 87.2 %copy-start.7 = (bf16[128,512]{1,0:T(8,128)(2,1)S(1)}, bf16[128,512]{1,0:T(8,128)(2,1)}, u32[]{:S(2)}) copy-start(bf16[128,512]{1,0:T(8,128)(2,1)} %constant.27.clone.row) | copy-start | bytes 393220
  0.6 87.2 %copy-start.8 = (bf16[256,128]{1,0:T(8,128)(2,1)S(1)}, bf16[256,128]{1,0:T(8,128)(2,1)}, u32[]{:S(2)}) copy-start(bf16[256,128]{1,0:T(8,128)(2,1)} %constant.28.clone.row_s) | copy-start | bytes 196612
  0.7 87.2 %copy-start.9 = (f32[1,512]{1,0:T(1,128)S(1)}, f32[1,512]{1,0:T(1,128)}, u32[]{:S(2)}) copy-start(f32[1,512]{1,0:T(1,128)} %constant.29.clone.doubled) | copy-start | bytes 6148
  2.4 15.6 %all-to-all-start = ((bf16[32,2,16,128]{3,2,1,0:T(8,128)(2,1)}), bf16[32,2,16,128]{3,2,1,0:T(8,128)(2,1)S(1)}, u32[]{:S(2)}, u32[]{:S(2)}) async-start(bf16[32,2,16,128]{3,2,1,0:T(8,128)(2,1)} %bitcast.80), calls=%async_computation | async-start | bytes 524288 | tf_op jit(solution)/shard_map/all_to_all | solution.py:495
  9.5 43.6 %collective-permute-start = (bf16[64,128]{1,0:T(8,128)(2,1)S(1)}, bf16[64,128]{1,0:T(8,128)(2,1)S(1)}, u32[]{:S(2)}, u32[]{:S(2)}) collective-permute-start(bf16[64,128]{1,0:T(8,128)(2,1)S(1)} %get-tuple-element.46), channel_id=1, source_target_pairs={{0,4},{4,8},{8,12},{12,16},{16,20},{20,24},{24,28},{28,0},{1,5},{5... | collective-permute-start | bytes 49160 | tf_op jit(solution)/shard_map/ppermute | solution.py:474
  9.7 21.5 %collective-permute-start.1 = (bf16[64,128]{1,0:T(8,128)(2,1)S(1)}, bf16[64,128]{1,0:T(8,128)(2,1)S(1)}, u32[]{:S(2)}, u32[]{:S(2)}) collective-permute-start(bf16[64,128]{1,0:T(8,128)(2,1)S(1)} %get-tuple-element.47), channel_id=1, source_target_pairs={{4,0},{8,4},{12,8},{16,12},{20,16},{24,20},{28,24},{0,28},{5,1},{9... | collective-permute-start | bytes 49160 | tf_op jit(solution)/shard_map/ppermute | solution.py:474
  18.0 1.6 copy-start
  19.6 0.9 copy-start.6
  20.5 67.4 %copy-start.1 = (bf16[1024,1024]{1,0:T(8,128)(2,1)S(1)}, bf16[1024,1024]{1,0:T(8,128)(2,1)}, u32[]{:S(2)}) copy-start(bf16[1024,1024]{1,0:T(8,128)(2,1)} %constant.25.clone.col) | copy-start | bytes 6291460
  21.8 33.1 %copy-start.11 = (bf16[64,16,128]{2,1,0:T(8,128)(2,1)S(1)}, bf16[64,16,128]{2,1,0:T(8,128)(2,1)}, u32[]{:S(2)}) copy-start(bf16[64,16,128]{2,1,0:T(8,128)(2,1)} %param.12) | copy-start | bytes 786436
  21.8 10.0 %all-to-all-start.1 = ((bf16[32,16,128]{2,1,0:T(8,128)(2,1)}), bf16[32,16,128]{2,1,0:T(8,128)(2,1)S(1)}, u32[]{:S(2)}, u32[]{:S(2)}) async-start(bf16[32,16,128]{2,1,0:T(8,128)(2,1)} %shard_map.120.after_ref), calls=%async_computation.1 | async-start | bytes 262144 | tf_op jit(solution)/shard_map/all_to_all | solution.py:495
  47.3 74.5 %copy-start.10 = (bf16[64,16,128]{2,1,0:T(8,128)(2,1)S(1)}, bf16[64,16,128]{2,1,0:T(8,128)(2,1)}, u32[]{:S(2)}) copy-start(bf16[64,16,128]{2,1,0:T(8,128)(2,1)} %param.9) | copy-start | bytes 786436
  47.3 12.0 %all-to-all-start.2 = ((bf16[32,16,128]{2,1,0:T(8,128)(2,1)}), bf16[32,16,128]{2,1,0:T(8,128)(2,1)S(1)}, u32[]{:S(2)}, u32[]{:S(2)}) async-start(bf16[32,16,128]{2,1,0:T(8,128)(2,1)} %shard_map.121), calls=%async_computation.2 | async-start | bytes 262144 | tf_op jit(solution)/shard_map/all_to_all | solution.py:495
  54.6 11.1 %collective-permute-start.3 = (bf16[64,18]{1,0:T(8,128)(2,1)}, bf16[64,18]{1,0:T(8,128)(2,1)S(1)}, u32[]{:S(2)}, u32[]{:S(2)}) collective-permute-start(bf16[64,18]{1,0:T(8,128)(2,1)} %pad_maximum_fusion.6), channel_id=1, source_target_pairs={{1,0},{2,1},{3,2},{0,3},{5,4},{6,5},{7,6},{4,7},{9,8},{10,9},{11,1... | collective-permute-start | bytes 6920 | tf_op jit(solution)/shard_map/ppermute | solution.py:474
  59.2 14.6 %all-to-all-start.4 = ((bf16[32,2,16,128]{3,2,1,0:T(8,128)(2,1)}), bf16[32,2,16,128]{3,2,1,0:T(8,128)(2,1)S(1)}, u32[]{:S(2)}, u32[]{:S(2)}) async-start(bf16[32,2,16,128]{3,2,1,0:T(8,128)(2,1)} %bitcast.91), calls=%async_computation.4 | async-start | bytes 524288 | tf_op jit(solution)/shard_map/all_to_all | solution.py:495
  64.1 6.3 %collective-permute-start.2 = (bf16[64,18]{1,0:T(8,128)(2,1)S(1)}, bf16[64,18]{1,0:T(8,128)(2,1)S(1)}, u32[]{:S(2)}, u32[]{:S(2)}) collective-permute-start(bf16[64,18]{1,0:T(8,128)(2,1)S(1)} %pad_maximum_fusion.5), channel_id=1, source_target_pairs={{0,1},{1,2},{2,3},{3,0},{4,5},{5,6},{6,7},{7,4},{8,9},{9,10},{10,1... | collective-permute-start | bytes 6920 | tf_op jit(solution)/shard_map/ppermute | solution.py:474
  71.4 0.9 copy-start.4
  87.8 1.6 copy-start.2
  91.0 30.7 %copy-start.12 = (bf16[64,16,128]{2,1,0:T(8,128)(2,1)S(1)}, bf16[64,16,128]{2,1,0:T(8,128)(2,1)}, u32[]{:S(2)}) copy-start(bf16[64,16,128]{2,1,0:T(8,128)(2,1)} %param.12) | copy-start | bytes 786436
  100.3 21.1 %all-to-all-start.5 = ((bf16[32,2,16,128]{3,2,1,0:T(8,128)(2,1)}), bf16[32,2,16,128]{3,2,1,0:T(8,128)(2,1)S(1)}, u32[]{:S(2)}, u32[]{:S(2)}) async-start(bf16[32,2,16,128]{3,2,1,0:T(8,128)(2,1)} %get-tuple-element.12), calls=%async_computation.5 | async-start | bytes 524288 | tf_op jit(solution)/shard_map/all_to_all | solution.py:495
  121.4 34.7 %copy-start.3 = (bf16[1024,1024]{1,0:T(8,128)(2,1)S(1)}, bf16[1024,1024]{1,0:T(8,128)(2,1)}, u32[]{:S(2)}) copy-start(bf16[1024,1024]{1,0:T(8,128)(2,1)} %constant.26.clone.col_t) | copy-start | bytes 6291460
  122.9 53.7 %copy-start.13 = (bf16[64,16,128]{2,1,0:T(8,128)(2,1)S(1)}, bf16[64,16,128]{2,1,0:T(8,128)(2,1)}, u32[]{:S(2)}) copy-start(bf16[64,16,128]{2,1,0:T(8,128)(2,1)} %param.12) | copy-start | bytes 786436
  122.9 1.2 copy-start.5
  127.5 27.6 %all-to-all-start.7 = ((bf16[32,32,128]{2,1,0:T(8,128)(2,1)}), bf16[32,32,128]{2,1,0:T(8,128)(2,1)}, u32[]{:S(2)}, u32[]{:S(2)}) async-start(bf16[32,32,128]{2,1,0:T(8,128)(2,1)} %fusion.15), calls=%async_computation.7 | async-start | bytes 524288 | tf_op jit(solution)/shard_map/all_to_all | solution.py:495
  136.1 12.7 %copy-start.14 = (bf16[64,16,128]{2,0,1:T(8,128)(2,1)S(1)}, bf16[64,16,128]{2,0,1:T(8,128)(2,1)}, u32[]{:S(2)}) copy-start(bf16[64,16,128]{2,0,1:T(8,128)(2,1)} %get-tuple-element.37) | copy-start | bytes 786436
  149.6 12.9 %collective-permute-start.4 = (bf16[64,128]{1,0:T(8,128)(2,1)S(1)}, bf16[64,128]{1,0:T(8,128)(2,1)S(1)}, u32[]{:S(2)}, u32[]{:S(2)}) collective-permute-start(bf16[64,128]{1,0:T(8,128)(2,1)S(1)} %get-tuple-element.42), channel_id=1, source_target_pairs={{0,4},{4,8},{8,12},{12,16},{16,20},{20,24},{24,28},{28,0},{1,5},{5... | collective-permute-start | bytes 49160 | tf_op jit(solution)/shard_map/ppermute | solution.py:474
  149.8 12.6 %collective-permute-start.5 = (bf16[64,128]{1,0:T(8,128)(2,1)S(1)}, bf16[64,128]{1,0:T(8,128)(2,1)S(1)}, u32[]{:S(2)}, u32[]{:S(2)}) collective-permute-start(bf16[64,128]{1,0:T(8,128)(2,1)S(1)} %get-tuple-element.43), channel_id=1, source_target_pairs={{4,0},{8,4},{12,8},{16,12},{20,16},{24,20},{28,24},{0,28},{5,1},{9... | collective-permute-start | bytes 49160 | tf_op jit(solution)/shard_map/ppermute | solution.py:474
  157.5 18.1 %all-to-all-start.8 = ((bf16[32,48,128]{2,1,0:T(8,128)(2,1)}), bf16[32,48,128]{2,1,0:T(8,128)(2,1)S(1)}, u32[]{:S(2)}, u32[]{:S(2)}) async-start(bf16[32,48,128]{2,1,0:T(8,128)(2,1)} %pad_maximum_fusion), calls=%async_computation.8 | async-start | bytes 786432 | tf_op jit(solution)/shard_map/all_to_all | solution.py:495
  162.7 11.4 %collective-permute-start.7 = (bf16[64,18]{1,0:T(8,128)(2,1)S(1)}, bf16[64,18]{1,0:T(8,128)(2,1)S(1)}, u32[]{:S(2)}, u32[]{:S(2)}) collective-permute-start(bf16[64,18]{1,0:T(8,128)(2,1)S(1)} %pad_maximum_fusion.8), channel_id=1, source_target_pairs={{1,0},{2,1},{3,2},{0,3},{5,4},{6,5},{7,6},{4,7},{9,8},{10,9},{11,1... | collective-permute-start | bytes 6920 | tf_op jit(solution)/shard_map/ppermute | solution.py:474
  163.1 11.0 %collective-permute-start.6 = (bf16[64,18]{1,0:T(8,128)(2,1)S(1)}, bf16[64,18]{1,0:T(8,128)(2,1)S(1)}, u32[]{:S(2)}, u32[]{:S(2)}) collective-permute-start(bf16[64,18]{1,0:T(8,128)(2,1)S(1)} %pad_maximum_fusion.7), channel_id=1, source_target_pairs={{0,1},{1,2},{2,3},{3,0},{4,5},{5,6},{6,7},{7,4},{8,9},{9,10},{10,1... | collective-permute-start | bytes 6920 | tf_op jit(solution)/shard_map/ppermute | solution.py:474

commit v2 on v0

--- a/solution.py
+++ b/solution.py
@@ -3,7 +3,11 @@
 
 import jax
 import jax.numpy as jnp
+import ml_dtypes
+import numpy as np
 from jax import lax
+from jax.experimental import pallas as pl
+from jax.experimental.pallas import tpu as pltpu
 from jax.sharding import PartitionSpec as P
 
 KX = 128
@@ -32,7 +36,7 @@
     return extended(field, (("gx", 1), ("gy", 2)), 1)
 
 
-def body(field, spectral_weight, kernel_weight, cotangent):
+def general_body(field, spectral_weight, kernel_weight, cotangent):
     highest = lax.Precision.HIGHEST
     channels, block_rows, block_cols = field.shape
     rows_total = block_rows * lax.axis_size("gx")
@@ -178,6 +182,668 @@
     return (layer_out, field_grad, spectral_grad, kernel_grad)
 
 
+BF16 = jnp.bfloat16
+F32 = jnp.float32
+BOTH = ("gx", "gy")
+EDGE = 16
+GROUP = 8
+CHUNK = 2
+
+
+class Plan:
+    def __init__(self, channels, block_rows, block_cols, gx, gy):
+        self.gx, self.gy, self.devices = gx, gy, gx * gy
+        self.channels, self.bx, self.by = channels, block_rows, block_cols
+        self.nx, self.ny = block_rows * gx, block_cols * gy
+        self.mx, self.my = KX // gx, KY // gy
+        self.cpd = channels // self.devices if channels % self.devices == 0 else 0
+        self.lanes = self.cpd * 2 * self.my
+        self.rows = self.cpd * self.bx
+        self.fits = (
+            self.cpd == 2
+            and channels == 64
+            and self.lanes == 128
+            and self.by == 128
+            and self.bx == 16
+            and KX % gx == 0
+            and KY % gy == 0
+            and self.mx == 16
+            and self.my % GROUP == 0
+            and gy % 2 == 0
+            and KX == 128
+            and self.nx == 128
+        )
+        self.scale = 1.0 / math.sqrt(self.nx * self.ny)
+
+    def tables(self):
+        two_pi = np.float32(2.0 * math.pi)
+        waves, points = np.arange(KY), np.arange(self.ny)
+        angles = np.float32((waves[:, None] * points[None, :]) % self.ny) * (two_pi / self.ny)
+        cos, sin = np.cos(angles).T, np.sin(angles).T
+        split = (self.ny, self.gy, self.my)
+        cos, sin = cos.reshape(split), sin.reshape(split)
+        top, bottom = np.stack([cos, -sin], 2), np.stack([-sin, -cos], 2)
+        col = np.stack([top, bottom], 1).reshape(self.ny, -1).astype(ml_dtypes.bfloat16)
+        rows = np.arange(KX) - KX // 2
+        points = np.arange(self.nx)
+        angles = np.float32((rows[:, None] * points[None, :]) % self.nx) * (two_pi / self.nx)
+        row = np.concatenate([np.cos(angles), np.sin(angles)], 1).astype(np.float32)
+        high = row.astype(ml_dtypes.bfloat16)
+        low = (row - high.astype(np.float32)).astype(ml_dtypes.bfloat16)
+        row_analysis = np.concatenate([high, low], 1)
+        row_synthesis = np.concatenate([np.cos(angles).T, np.sin(angles).T], 0)
+        row_synthesis = row_synthesis.astype(ml_dtypes.bfloat16)
+        return col, row_analysis, row_synthesis
+
+    def named(self):
+        names = ("col", "row", "row_s", "pick_rows", "pick_cols", "window")
+        return dict(zip(names, self.tables() + self.pickers()))
+
+    def pickers(self):
+        pick_rows = np.zeros((self.gx, EDGE, self.cpd, self.nx), np.float32)
+        pick_cols = np.zeros((self.gy, EDGE, self.cpd, self.ny), np.float32)
+        window = np.zeros((self.nx, self.gx, self.by), np.float32)
+        for c in range(self.cpd):
+            for g in range(self.gx):
+                pick_rows[g, 2 * c, c, (g * self.bx - 1) % self.nx] = 1
+                pick_rows[g, 2 * c + 1, c, ((g + 1) * self.bx) % self.nx] = 1
+            for g in range(self.gy):
+                pick_cols[g, 2 * self.cpd + 2 * c, c, (g * self.by - 1) % self.ny] = 1
+                pick_cols[g, 2 * self.cpd + 2 * c + 1, c, ((g + 1) * self.by) % self.ny] = 1
+        for g in range(self.gx):
+            for t in range(self.bx + 2):
+                window[(g * self.bx - 1 + t) % self.nx, g, t] = 1
+        kind = ml_dtypes.bfloat16
+        return (
+            pick_rows.reshape(self.gx * EDGE, -1).astype(kind),
+            pick_cols.reshape(self.gy * EDGE, -1).astype(kind),
+            window.reshape(self.nx, -1).astype(kind),
+        )
+
+
+def dot(a, b):
+    return jnp.dot(a, b, preferred_element_type=F32)
+
+
+def dot_nt(a, b):
+    return lax.dot_general(a, b, (((1,), (1,)), ((), ())), preferred_element_type=F32)
+
+
+def interleave(plan, parts):
+    half = plan.lanes // 2
+    lane = lax.broadcasted_iota(jnp.int32, (1, plan.lanes), 1)
+    tiles = []
+    for k in range(plan.gy // 2):
+        first, second = (p[:, k * plan.lanes : (k + 1) * plan.lanes] for p in parts)
+        tiles.append(jnp.where(lane < half, first, pltpu.roll(second, half, 1)))
+        tiles.append(jnp.where(lane < half, pltpu.roll(first, half, 1), second))
+    return jnp.concatenate(tiles, 1)
+
+
+def separate(plan, values):
+    half = plan.lanes // 2
+    lane = lax.broadcasted_iota(jnp.int32, (1, plan.lanes), 1)
+    parts = ([], [])
+    for k in range(plan.gy // 2):
+        even = values[:, 2 * k * plan.lanes : (2 * k + 1) * plan.lanes]
+        odd = values[:, (2 * k + 1) * plan.lanes : (2 * k + 2) * plan.lanes]
+        parts[0].append(jnp.where(lane < half, even, pltpu.roll(odd, half, 1)))
+        parts[1].append(jnp.where(lane < half, pltpu.roll(even, half, 1), odd))
+    return [jnp.concatenate(p, 1) for p in parts]
+
+
+def analyse_plane(plan, held, planes, weight, out_ref):
+    col = held["col"]
+    half = col.shape[1] // 2
+    along_y = [
+        dot(planes[:, c * plan.ny : (c + 1) * plan.ny], col[...]) for c in range(plan.cpd)
+    ]
+    stacked = jnp.concatenate(
+        [
+            interleave(plan, [p[:, :half] for p in along_y]),
+            interleave(plan, [p[:, half:] for p in along_y]),
+        ],
+        0,
+    ).astype(BF16)
+    modes = dot(held["row"][...], jnp.concatenate([stacked, stacked], 0)) * weight
+    modes = modes.astype(BF16)
+    for i in range(plan.gx):
+        for k in range(plan.gy):
+            out_ref[i * plan.gy + k, : plan.mx] = modes[
+                i * plan.mx : (i + 1) * plan.mx, k * plan.lanes : (k + 1) * plan.lanes
+            ]
+
+
+def put_edges(plan, held, planes, out_ref, start):
+    stacked = jnp.concatenate(
+        [planes[:, c * plan.ny : (c + 1) * plan.ny] for c in range(plan.cpd)], 0
+    )
+    edge_rows = dot(held["pick_rows"][...], stacked)
+    picked = dot_nt(held["pick_cols"][...], planes).astype(BF16)
+    edge_cols = dot(picked, held["window"][...])
+    for i in range(plan.gx):
+        for k in range(plan.gy):
+            tile = (
+                edge_rows[i * EDGE : (i + 1) * EDGE, k * plan.by : (k + 1) * plan.by]
+                + edge_cols[k * EDGE : (k + 1) * EDGE, i * plan.by : (i + 1) * plan.by]
+            )
+            out_ref[i * plan.gy + k, start : start + EDGE] = tile.astype(BF16)
+
+
+def synthesise_plane(plan, held, modes_ref, weight):
+    columns = []
+    for k in range(plan.gy):
+        columns.append(
+            jnp.concatenate([modes_ref[i * plan.gy + k, : plan.mx] for i in range(plan.gx)], 0)
+        )
+    sums = dot(held["row_s"][...], jnp.concatenate(columns, 1))
+    if weight is not None:
+        sums = sums * weight
+    top, bottom = separate(plan, sums[: plan.nx]), separate(plan, sums[plan.nx :])
+    planes = []
+    for c in range(plan.cpd):
+        left = jnp.concatenate([top[c], bottom[c]], 1).astype(BF16)
+        planes.append(dot_nt(left, held["col"][...]))
+    return jnp.concatenate(planes, 1)
+
+
+def read_plane(plan, ref, c, k):
+    rows = slice(c * plan.bx, (c + 1) * plan.bx)
+    return jnp.concatenate([ref[i * plan.gy + k, rows] for i in range(plan.gx)], 0)
+
+
+def write_plane(plan, ref, c, k, values):
+    rows = slice(c * plan.bx, (c + 1) * plan.bx)
+    for i in range(plan.gx):
+        ref[i * plan.gy + k, rows] = values[i * plan.bx : (i + 1) * plan.bx]
+
+
+def first_kernel(plan, held, field_ref, out_ref):
+    planes = jnp.concatenate(
+        [read_plane(plan, field_ref, c, k) for c in range(plan.cpd) for k in range(plan.gy)], 1
+    )
+    analyse_plane(plan, held, planes, plan.scale, out_ref)
+    put_edges(plan, held, planes, out_ref, plan.mx)
+
+
+def gelu_parts(z):
+    factor = math.sqrt(2.0 / math.pi)
+    tanh = jnp.tanh(factor * (z + 0.044715 * (z * z * z)))
+    cdf = 0.5 * (1.0 + tanh)
+    slope = cdf + 0.5 * z * (1.0 - tanh * tanh) * (factor * (1.0 + (3.0 * 0.044715) * (z * z)))
+    return z * cdf, slope
+
+
+def middle_kernel(plan, held, modes_ref, conv_ref, out_ref, z_ref, grads):
+    lane = lax.broadcasted_iota(jnp.int32, (1, plan.gy * plan.lanes), 1)
+    zero = jnp.logical_and(lane < plan.lanes, lax.rem(lane, plan.my) == 0)
+    doubled = jnp.where(zero, 1.0, 2.0)
+    syn = synthesise_plane(plan, held, modes_ref, doubled) * plan.scale
+    for c in range(plan.cpd):
+        for k in range(plan.gy):
+            start = c * plan.ny + k * plan.by
+            z = syn[:, start : start + plan.by] + read_plane(plan, conv_ref, c, k).astype(F32)
+            z = z.astype(BF16)
+            write_plane(plan, z_ref, c, k, z)
+            slope = gelu_parts(z.astype(F32))[1]
+            cot = read_plane(plan, conv_ref, plan.cpd + c, k).astype(F32)
+            grads[:, start : start + plan.by] = (cot * slope).astype(BF16)
+    planes = grads[...]
+    analyse_plane(plan, held, planes, doubled * plan.scale, out_ref)
+    put_edges(plan, held, planes, z_ref, plan.rows)
+
+
+def last_kernel(plan, held, both_ref, out_ref):
+    syn = synthesise_plane(plan, held, both_ref, None) * plan.scale
+    syn = syn.astype(BF16)
+    for c in range(plan.cpd):
+        for k in range(plan.gy):
+            start = c * plan.ny + k * plan.by
+            write_plane(plan, out_ref, c, k, syn[:, start : start + plan.by])
+    terms = both_ref[0, plan.mx :].astype(F32)
+    for s in range(1, plan.devices):
+        terms = terms + both_ref[s, plan.mx :].astype(F32)
+    terms = terms.astype(BF16)
+    for s in range(plan.devices):
+        out_ref[s, plan.rows :] = terms
+
+
+def gather_modes(plan, x_ref, flat, turned, j):
+    s, half = plan.devices, plan.lanes // 2
+    values = flat[pl.ds(j, s, stride=plan.mx), :]
+    for c in range(plan.cpd):
+        turned[j, pl.ds(c, s, stride=plan.cpd), :] = values[:, c * half : (c + 1) * half]
+
+
+def spread(plan, x_ref, flat):
+    flat[...] = x_ref[:, : plan.mx, :].astype(F32).reshape(plan.devices * plan.mx, plan.lanes)
+
+
+def modes_to_rows(plan, x_ref, flat, turned, rows):
+    spread(plan, x_ref, flat)
+    for j in range(plan.mx):
+        gather_modes(plan, x_ref, flat, turned, j)
+        rows[j] = turned[j].T
+
+
+def rows_to_modes(plan, values, turned, flat, j):
+    s = plan.devices
+    turned[j] = values.T
+    parts = [turned[j, pl.ds(c, s, stride=plan.cpd), :] for c in range(plan.cpd)]
+    flat[pl.ds(j, s, stride=plan.mx), :] = jnp.concatenate(parts, 1)
+
+
+def group_mask(rows, groups, width):
+    row = lax.broadcasted_iota(jnp.int32, (rows, groups * width), 0)
+    lane = lax.broadcasted_iota(jnp.int32, (rows, groups * width), 1)
+    return lax.rem(row, groups) == lax.div(lane, width)
+
+
+def load_kernel(plan, *refs):
+    count = len(refs) // 2
+    copies = [pltpu.make_async_copy(refs[i], refs[count + i], refs[-1].at[i]) for i in range(count)]
+    for copy in copies:
+        copy.start()
+    for copy in copies:
+        copy.wait()
+
+
+def each_mode_row(plan, product, r_ref, x_ref, y_ref, flat, turned, rows, held, sems):
+    width = plan.channels
+    copies = [
+        pltpu.make_async_copy(
+            r_ref.at[:, pl.ds(t * CHUNK, CHUNK)], held.at[:, pl.ds(t * CHUNK, CHUNK)], sems.at[t]
+        )
+        for t in range(plan.mx // CHUNK)
+    ]
+    for copy in copies:
+        copy.start()
+    modes_to_rows(plan, x_ref, flat, turned, rows)
+    mask = group_mask(2 * GROUP, GROUP, width)
+    for j in range(plan.mx):
+        if j % CHUNK == 0:
+            copies[j // CHUNK].wait()
+        real_out, imag_out = [], []
+        for g in range(plan.my // GROUP):
+            start = g * GROUP
+            real = rows[j, start : start + GROUP, :]
+            imag = rows[j, plan.my + start : plan.my + start + GROUP, :]
+            weights = [
+                held[part, j, start : start + GROUP].reshape(GROUP * width, width)
+                for part in range(2)
+            ]
+            real, imag = product(mask, real, imag, *weights)
+            real_out.append(real)
+            imag_out.append(imag)
+        rows_to_modes(plan, jnp.concatenate(real_out + imag_out, 0), turned, flat, j)
+    y_ref[...] = flat[...].reshape(plan.devices, plan.mx, plan.lanes).astype(BF16)
+
+
+def mix_kernel(plan, held, *refs):
+    def product(mask, real, imag, r_real, r_imag):
+        first = jnp.concatenate([jnp.concatenate([real, imag], 0)] * GROUP, 1)
+        second = jnp.concatenate([jnp.concatenate([-imag, real], 0)] * GROUP, 1)
+        mixed = dot(jnp.where(mask, first, 0.0).astype(BF16), r_real)
+        mixed = mixed + dot(jnp.where(mask, second, 0.0).astype(BF16), r_imag)
+        return mixed[:GROUP], mixed[GROUP:]
+
+    each_mode_row(plan, product, *refs)
+
+
+def back_kernel(plan, held, *refs):
+    width = plan.channels
+
+    def product(mask, real, imag, r_real, r_imag):
+        left = jnp.concatenate(
+            [jnp.concatenate([real, imag], 1), jnp.concatenate([imag, -real], 1)], 0
+        )
+        weights = jnp.concatenate([r_real, r_imag], 1)
+        mixed = jnp.where(mask, dot_nt(left.astype(BF16), weights), 0.0)
+        total = mixed[:, : 2 * width]
+        for i in range(1, GROUP // 2):
+            total = total + mixed[:, 2 * i * width : 2 * (i + 1) * width]
+        total = total[:, :width] + total[:, width:]
+        return total[:GROUP], total[GROUP:]
+
+    each_mode_row(plan, product, *refs)
+
+
+def outer_kernel(
+    plan, first_j, count, held, x_ref, g_ref, *refs
+):
+    out_ref, x_flat, g_flat, a_turned, g_turned, slots, sems = refs
+    my, width = plan.my, plan.channels
+    spread(plan, x_ref, x_flat)
+    spread(plan, g_ref, g_flat)
+    for j in range(first_j, first_j + count):
+        gather_modes(plan, x_ref, x_flat, a_turned, j)
+        gather_modes(plan, g_ref, g_flat, g_turned, j)
+    lane = lax.rem(lax.broadcasted_iota(jnp.int32, (width, 2 * my), 1), my)
+    copies = []
+    for j in range(first_j, first_j + count):
+        left = a_turned[j]
+        g_rows = g_turned[j].T
+        g_real, g_imag = g_rows[:my], g_rows[my:]
+        right = jnp.concatenate(
+            [jnp.concatenate([g_real, g_imag], 1), jnp.concatenate([g_imag, -g_real], 1)], 0
+        ).astype(BF16)
+        for g in range(my // GROUP):
+            picked = jnp.concatenate(
+                [jnp.where(lane == g * GROUP + l, left, 0.0) for l in range(GROUP)], 0
+            ).astype(BF16)
+            value = dot(picked, right).astype(BF16)
+            for part in range(2):
+                slots[part, j - first_j, g * GROUP : (g + 1) * GROUP] = value[
+                    :, part * width : (part + 1) * width
+                ].reshape(GROUP, width, width)
+        if (j + 1) % CHUNK == 0:
+            t = (j + 1 - first_j) // CHUNK - 1
+            copies.append(
+                pltpu.make_async_copy(
+                    slots.at[:, pl.ds(t * CHUNK, CHUNK)],
+                    out_ref.at[:, pl.ds(first_j + t * CHUNK, CHUNK)],
+                    sems.at[t],
+                )
+            )
+            copies[-1].start()
+    for copy in copies:
+        copy.wait()
+
+
+def fill_taps(plan, block, edges, paired, taps):
+    c, bx, by, s = plan.channels, plan.bx, plan.by, plan.devices
+
+    def edge(first):
+        for p in range(plan.cpd):
+            paired[pl.ds(p, s, stride=plan.cpd), :] = edges[
+                pl.ds(first + 2 * p, s, stride=EDGE), :
+            ]
+        return paired[...]
+
+    top, bottom = edge(0), edge(1)
+    left, right = edge(2 * plan.cpd), edge(2 * plan.cpd + 1)
+    lane = lax.broadcasted_iota(jnp.int32, (c, by), 1)
+    for x in range(bx + 2):
+        if x == 0:
+            row = top
+        elif x == bx + 1:
+            row = bottom
+        else:
+            row = block[pl.ds(x - 1, c, stride=bx), :]
+        lanes = slice(x * by, (x + 1) * by)
+        taps[:c, lanes] = jnp.where(
+            lane == 0, left[:, x : x + 1], pltpu.roll(row, 1, 1)
+        ).astype(BF16)
+        taps[c : 2 * c, lanes] = row.astype(BF16)
+        taps[2 * c :, lanes] = jnp.where(
+            lane == by - 1, right[:, x : x + 1], pltpu.roll(row, by - 1, 1)
+        ).astype(BF16)
+
+
+def convolve(plan, weights, taps, out):
+    bx, by = plan.bx, plan.by
+    total = dot(weights[0], taps[:, : bx * by])
+    for a in range(1, 3):
+        total = total + dot(weights[a], taps[:, a * by : (a + bx) * by])
+    for x in range(bx):
+        out[pl.ds(x, plan.channels, stride=bx), :] = total[:, x * by : (x + 1) * by]
+
+
+def conv_kernel(plan, held, both_ref, out_ref, block, edges, paired, taps):
+    edges[...] = both_ref[:, plan.mx :, :].astype(F32).reshape(edges.shape)
+    block[...] = held["field"][...].astype(F32).reshape(block.shape)
+    fill_taps(plan, block, edges, paired, taps)
+    kernel_ref = held["kernel"]
+    weights = [jnp.concatenate([kernel_ref[a, b] for b in range(3)], 1) for a in range(3)]
+    convolve(plan, weights, taps, block)
+    out_ref[:, : plan.rows] = block[...].reshape(plan.devices, plan.rows, plan.by).astype(BF16)
+    out_ref[:, plan.rows :] = held["cotangent"][...].reshape(plan.devices, plan.rows, plan.by)
+
+
+def space_kernel(
+    plan, held, z_ref, back_ref, layer_ref, grad_ref, both_ref, block, edges, paired, taps, flat
+):
+    c, bx, by, s = plan.channels, plan.bx, plan.by, plan.devices
+    z = z_ref[:, : plan.rows, :].astype(F32).reshape(c, bx, by)
+    activated, slope = gelu_parts(z)
+    field = held["field"][...].astype(F32)
+    layer_ref[...] = (field + activated).astype(BF16)
+    block[...] = field.reshape(block.shape)
+    for x in range(bx):
+        flat[:, x * by : (x + 1) * by] = block[pl.ds(x, c, stride=bx), :].astype(BF16)
+    cot_ref = held["cotangent"]
+    grads = (cot_ref[...].astype(F32) * slope).astype(BF16).astype(F32)
+    block[...] = grads.reshape(block.shape)
+    edges[...] = z_ref[:, plan.rows :, :].astype(F32).reshape(edges.shape)
+    fill_taps(plan, block, edges, paired, taps)
+    kernel_ref = held["kernel"]
+    weights = [
+        jnp.concatenate(
+            [kernel_ref[2 - a, 2 - b].astype(F32).T for b in range(3)], 1
+        ).astype(BF16)
+        for a in range(3)
+    ]
+    convolve(plan, weights, taps, block)
+    grad_ref[...] = cot_ref[...].astype(F32) + block[...].reshape(c, bx, by)
+    terms = jnp.concatenate(
+        [dot_nt(taps[:, a * by : (a + bx) * by], flat[...]) for a in range(3)], 0
+    )
+    half = terms.shape[0] // 2
+    terms = jnp.concatenate([terms[:half], terms[half:]], 1)
+    edges[...] = jnp.zeros(edges.shape, F32)
+    for t in range(half // s):
+        edges[pl.ds(t, s, stride=EDGE), :] = terms[t * s : (t + 1) * s]
+    both_ref[:, : plan.mx, :] = back_ref[...]
+    both_ref[:, plan.mx :, :] = edges[...].reshape(s, EDGE, by).astype(BF16)
+
+
+def end_kernel(plan, held, last_ref, grad_ref, out_ref, kernel_ref, edges):
+    c, bx, by, s = plan.channels, plan.bx, plan.by, plan.devices
+    edges[...] = last_ref[:, plan.rows :, :].astype(F32).reshape(edges.shape)
+    count = 9 * c // (2 * s)
+    for t in range(count):
+        rows = edges[pl.ds(t, s, stride=EDGE), :]
+        for h in range(2):
+            start = (h * count + t) * s
+            tap, first = start // c, start % c
+            a, b = 2 - tap // 3, 2 - tap % 3
+            kernel_ref[a, b, first : first + s, :] = rows[:, h * c : (h + 1) * c]
+    syn = last_ref[:, : plan.rows, :].astype(F32).reshape(c, bx, by)
+    out_ref[...] = (grad_ref[...] + syn).astype(BF16)
+
+
+def fast_body(plan, field, spectral_weight, kernel_weight, cotangent):
+    channels, bx, by, n, cpd = plan.channels, plan.bx, plan.by, plan.devices, plan.cpd
+    anywhere = pl.BlockSpec(memory_space=pl.ANY)
+    here = pl.BlockSpec(memory_space=pltpu.VMEM)
+
+    def exchange(x):
+        return lax.all_to_all(x, BOTH, 0, 0, tiled=True)
+
+    def rows_of(count):
+        return jax.ShapeDtypeStruct((n, count, by), BF16)
+
+    def call(
+        kernel, outs, *args, us=1.0, scratch=(), mib=56, raw=(), use=(), after=(), spec=None,
+        alias=False,
+    ):
+        several = isinstance(outs, tuple)
+        outs = outs if several else (outs,)
+        steps = (len(raw), len(args), len(use), len(after))
+
+        def run(*refs):
+            groups = []
+            for step in steps:
+                groups.append(refs[:step])
+                refs = refs[step:]
+            kernel(plan, dict(zip(use, groups[2])), *groups[0], *groups[1], *refs)
+
+        results = pl.pallas_call(
+            run,
+            out_shape=outs,
+            in_specs=[anywhere] * len(raw)
+            + [here] * (len(args) + len(use))
+            + [anywhere] * len(after),
+            out_specs=(spec or here,) * len(outs),
+            scratch_shapes=scratch,
+            input_output_aliases={sum(steps) - 1: 0} if alias else {},
+            cost_estimate=pl.CostEstimate(
+                flops=int(us * 1.0e9), bytes_accessed=1024, transcendentals=0
+            ),
+            compiler_params=pltpu.CompilerParams(vmem_limit_bytes=mib * 1024 * 1024),
+        )(*raw, *args, *(held[name] for name in use), *after)
+        return results if several else results[0]
+
+    flat = pltpu.VMEM((n * plan.mx, plan.lanes), F32)
+    turned = pltpu.VMEM((plan.mx, channels, 2 * plan.my), F32)
+    rows = pltpu.VMEM((plan.mx, 2 * plan.my, channels), F32)
+    block = pltpu.VMEM((channels * bx, by), F32)
+    edges = pltpu.VMEM((n * EDGE, by), F32)
+    paired = pltpu.VMEM((channels, by), F32)
+    taps = pltpu.VMEM((3 * channels, (bx + 2) * by), BF16)
+    field_flat = pltpu.VMEM((channels, bx * by), BF16)
+    modes_scratch = [
+        flat,
+        turned,
+        rows,
+        pltpu.VMEM((2, plan.mx, plan.my, channels, channels), BF16),
+        pltpu.SemaphoreType.DMA((plan.mx // CHUNK,)),
+    ]
+    edge_tables = ("pick_rows", "pick_cols", "window")
+
+    field_c = exchange(field.reshape(n, plan.rows, by))
+    sources = {name: jnp.asarray(t) for name, t in plan.named().items()}
+    sources.update(field=field, cotangent=cotangent, kernel=kernel_weight)
+    held = pl.pallas_call(
+        partial(load_kernel, plan),
+        out_shape=tuple(pltpu.VMEM(t.shape, t.dtype) for t in sources.values()),
+        in_specs=[anywhere] * len(sources),
+        out_specs=(here,) * len(sources),
+        scratch_shapes=[pltpu.SemaphoreType.DMA((len(sources),))],
+        cost_estimate=pl.CostEstimate(flops=2_500_000_000, bytes_accessed=1024, transcendentals=0),
+        compiler_params=pltpu.CompilerParams(vmem_limit_bytes=60 * 1024 * 1024),
+    )(*sources.values())
+    held = dict(zip(sources, held))
+    a_part = call(
+        first_kernel,
+        rows_of(plan.mx + EDGE),
+        field_c,
+        use=("col", "row") + edge_tables,
+        mib=20,
+    )
+    a_both = exchange(a_part)
+    conv = call(
+        conv_kernel,
+        rows_of(2 * plan.rows),
+        a_both,
+        use=("field", "cotangent", "kernel"),
+        scratch=[block, edges, paired, taps],
+        us=1.5,
+        mib=20,
+    )
+    conv_c = exchange(conv)
+    b_part = call(
+        mix_kernel,
+        rows_of(plan.mx),
+        a_both,
+        raw=(spectral_weight,),
+        scratch=modes_scratch,
+        us=6.5,
+        after=(conv,),
+    )
+    b_part, conv_c = lax.optimization_barrier((b_part, conv_c))
+    b_modes = exchange(b_part)
+    g_part, z_part = call(
+        middle_kernel,
+        (rows_of(plan.mx), rows_of(plan.rows + EDGE)),
+        b_modes,
+        conv_c,
+        use=("row_s", "col", "row") + edge_tables,
+        mib=20,
+        scratch=[pltpu.VMEM((plan.nx, cpd * plan.ny), BF16)],
+        us=2.6,
+    )
+    g_modes = exchange(g_part)
+    z_both = exchange(z_part)
+    back_part = call(
+        back_kernel,
+        rows_of(plan.mx),
+        g_modes,
+        raw=(spectral_weight,),
+        scratch=modes_scratch,
+        us=6.5,
+        after=(z_part,),
+    )
+    layer_out, grad_sum, back_terms = call(
+        space_kernel,
+        (
+            jax.ShapeDtypeStruct(field.shape, BF16),
+            jax.ShapeDtypeStruct(field.shape, F32),
+            rows_of(plan.mx + EDGE),
+        ),
+        z_both,
+        back_part,
+        use=("field", "cotangent", "kernel"),
+        mib=20,
+        scratch=[block, edges, paired, taps, field_flat],
+        us=3.8,
+    )
+    back_both = exchange(back_terms)
+
+    def outer_part(first_j, count, after, alias):
+        return call(
+            lambda plan, *refs: outer_kernel(plan, first_j, count, *refs),
+            jax.ShapeDtypeStruct(spectral_weight.shape, BF16),
+            a_both,
+            g_modes,
+            scratch=[
+                flat,
+                flat,
+                turned,
+                turned,
+                pltpu.VMEM((2, count, plan.my, channels, channels), BF16),
+                pltpu.SemaphoreType.DMA((count // CHUNK,)),
+            ],
+            spec=anywhere,
+            us=6.4,
+            after=after,
+            alias=alias,
+        )
+
+    half = plan.mx // 2
+    spectral_half = outer_part(0, half, (back_terms,), False)
+    last_part = call(
+        last_kernel,
+        rows_of(plan.rows + EDGE),
+        back_both,
+        use=("row_s", "col"),
+        us=1.3,
+        mib=44,
+        after=(spectral_half,),
+    )
+    last_both = exchange(last_part)
+    spectral_grad = outer_part(half, half, (last_part, spectral_half), True)
+    field_grad, kernel_grad = call(
+        end_kernel,
+        (
+            jax.ShapeDtypeStruct(field.shape, BF16),
+            jax.ShapeDtypeStruct((3, 3, channels, channels), F32),
+        ),
+        last_both,
+        grad_sum,
+        scratch=[edges],
+        mib=20,
+    )
+    return (layer_out, field_grad, spectral_grad, kernel_grad)
+
+
+def body(field, spectral_weight, kernel_weight, cotangent):
+    plan = Plan(*field.shape, lax.axis_size("gx"), lax.axis_size("gy"))
+    if plan.fits:
+        return fast_body(plan, field, spectral_weight, kernel_weight, cotangent)
+    return general_body(field, spectral_weight, kernel_weight, cotangent)
+
+
 def solution(mesh):
     in_specs = (P(None, "gx", "gy"), P(None, "gx", "gy", None, None), P(), P(None, "gx", "gy"))
     out_specs = (P(None, "gx", "gy"), P(None, "gx", "gy"), P(None, "gx", "gy", None, None), P())

time: 498 us -> 128 us (0.26); the launches traced: 489 us -> 125 us
  waiting for transfers between devices: 250 us -> 26.5 us
  matrix products: 131 us -> 0 us
  Pallas kernels: 0 us -> 43.4 us
  local copies, waits for them, and re-layouts: 28.8 us -> 0.91 us
  other arithmetic: 23.2 us -> 0 us
  between operations: 15.2 us -> 0.73 us
  starting transfers between devices: 10.1 us -> 21 us
    dot_general x55 -> x0, matrix products: 131 us -> none  [the longest x2 31 us: body(): back_real = back(wreal, greal) + back(wimag, gimag)]
    reduce_scatter x4 -> x0, waiting for transfers between devices: 119 us -> none  [the longest x2 67.3 us: analyse(): lax.psum_scatter(jnp.stack([real_out, imag_out], 2).reshape(lax.axis_size...]
    psum x1 -> x0, waiting for transfers between devices: 94.4 us -> none  [body(): kernel_grad = lax.psum(jnp.stack(tap_rows, 0), ('gx', 'gy'))]
    pallas_call x0 -> x11, Pallas kernels: none -> 43.4 us  [the longest x10 41.9 us: call(): pl.pallas_call(run, out_shape=outs, in_specs=[anywhere] * len(raw) + [her...]
    all_to_all x0 -> x3, blocking collectives: none -> 32.9 us  [exchange(): return lax.all_to_all(x, BOTH, 0, 0, tiled=True)]
    all_gather x2 -> x0, blocking collectives: 30.3 us -> none  [synthesise(): shard_rows = lax.all_gather(row_sum, 'gy', axis=0, tiled=True)]
    all_to_all x0 -> x5, waiting for transfers between devices: none -> 26.5 us  [exchange(): return lax.all_to_all(x, BOTH, 0, 0, tiled=True)]
    all_to_all x0 -> x5, starting transfers between devices: none -> 21 us  [exchange(): return lax.all_to_all(x, BOTH, 0, 0, tiled=True)]
  transfers between devices with their start and end apart: 15 -> 5, of which waited for: 9 -> 5; matrix products, arithmetic and copies ran while one was open for 29% -> 0% of each run, Pallas kernels for 0% -> 26%
where the time goes in v2:
time: 128 us; the launch traced here: 125 us
  Pallas kernels  43.4 us (34%)
  blocking collectives  32.9 us (26%)
  waiting for transfers between devices  26.5 us (21%)
  starting transfers between devices  21 us (16%)
    pallas_call x10, Pallas kernels, call(): pl.pallas_call(run, out_shape=outs, in_specs=[anywhere] * len(raw) + [her...  41.9 us
    all_to_all x3, blocking collectives, exchange(): return lax.all_to_all(x, BOTH, 0, 0, tiled=True)  32.9 us
    all_to_all x5, waiting for transfers between devices, exchange(): return lax.all_to_all(x, BOTH, 0, 0, tiled=True)  26.5 us
    all_to_all x5, starting transfers between devices, exchange(): return lax.all_to_all(x, BOTH, 0, 0, tiled=True)  21 us
  transfers between devices with their start and end apart: 5, of which 5 were waited for; matrix products, arithmetic and copies ran while one was open for 0% of the time, Pallas kernels for 26%

profile of v2, /device:TPU:8, one launch (start us, length us, event | category | flops | bytes accessed | tf_op | source)
XLA Modules:
  0.0 125.4 jit_solution(108426734410572550)
XLA Ops:
  0.6 6.0 %all-to-all-start = ((bf16[32,32,128]{2,1,0:T(8,128)(2,1)}), bf16[32,32,128]{2,1,0:T(8,128)(2,1)S(1)}, u32[]{:S(2)}, u32[]{:S(2)}) async-start(bf16[32,32,128]{2,1,0:T(8,128)(2,1)} %bitcast.1), calls=%async_computation | async-start | bytes 524288 | tf_op jit(solution)/shard_map/all_to_all | solution.py:661
  6.7 1.5 %shard_map.129 = (bf16[512,512]{1,0:T(8,128)(2,1)S(1)}, bf16[128,512]{1,0:T(8,128)(2,1)S(1)}, bf16[256,128]{1,0:T(8,128)(2,1)S(1)}, bf16[128,256]{1,0:T(8,128)(2...) custom-call(bf16[512,512]{1,0:T(8,128)(2,1)} %constant.12.clone.refs, ...), custom_call_target="tpu_custom_call" | custom-call | flops 2500000000 | bytes 1024 | tf_op jit(solution)/shard_map/pallas_call | solution.py:717
  8.2 8.0 %all-to-all-done.refs_0_ = bf16[32,32,128]{2,1,0:T(8,128)(2,1)S(1)} async-done(((bf16[32,32,128]{2,1,0:T(8,128)(2,1)}), bf16[32,32,128]{2,1,0:T(8,128)(2,1)S(1)}, u32[]{:S(2)}, u32[]{:S(2)}) %all-to-all-start) | async-done | bytes 262176 | tf_op jit(solution)/shard_map/all_to_all | solution.py:661
  16.2 0.9 shard_map.130
  17.1 12.7 %all_to_all.40.refs_0_.refs_1_ = bf16[32,32,128]{2,1,0:T(8,128)(2,1)S(1)} all-to-all(bf16[32,32,128]{2,1,0:T(8,128)(2,1)S(1)} %shard_map.130), channel_id=1, replica_groups=mesh['gx'=8,'gy'=4] {'gx','gy'}, dimensions={0} | all-to-all | bytes 524288 | tf_op jit(solution)/shard_map/all_to_all | solution.py:661
  29.8 0.0 copy-start
  29.8 1.9 %shard_map.131.refs_2_ = bf16[32,64,128]{2,1,0:T(8,128)(2,1)} custom-call(bf16[32,32,128]{2,1,0:T(8,128)(2,1)S(1)} %all_to_all.40.refs_0_.refs_1_, bf16[64,16,128]{2,1,0:T(8,128)(2,1)S(1)} %get-tuple-element.27.refs_1_.refs_2_, bf16[64,16,128]{2,1,0:T(8,128)(2,1)S(1)} %get-tuple-element.28.refs_2_.refs_3_, ...), custom_call_target="tpu_custom_call" | custom-call | flops 1500000000 | bytes 1024 | tf_op jit(solution)/shard_map/pallas_call | solution.py:681
  31.8 3.4 %all-to-all-start.2 = ((bf16[32,64,128]{2,1,0:T(8,128)(2,1)}), bf16[32,64,128]{2,1,0:T(8,128)(2,1)S(1)}, u32[]{:S(2)}, u32[]{:S(2)}) async-start(bf16[32,64,128]{2,1,0:T(8,128)(2,1)} %shard_map.131.refs_2_), calls=%async_computation.2 | async-start | bytes 1048576 | tf_op jit(solution)/shard_map/all_to_all | solution.py:661
  35.2 0.0 copy-done
  35.2 8.2 %shard_map.132 = bf16[32,16,128]{2,1,0:T(8,128)(2,1)} custom-call(bf16[2,16,32,64,64]{4,3,2,1,0:T(8,128)(2,1)} %refs_0_.4, bf16[32,32,128]{2,1,0:T(8,128)(2,1)} %copy-done, bf16[32,64,128]{2,1,0:T(8,128)(2,1)} %shard_map.131.refs_2_), custom_call_target="tpu_custom_call" | custom-call | flops 6499999744 | bytes 1024 | tf_op jit(solution)/shard_map/pallas_call | solution.py:681
  43.4 7.0 %all-to-all-done.2.refs_1_ = bf16[32,64,128]{2,1,0:T(8,128)(2,1)S(1)} async-done(((bf16[32,64,128]{2,1,0:T(8,128)(2,1)}), bf16[32,64,128]{2,1,0:T(8,128)(2,1)S(1)}, u32[]{:S(2)}, u32[]{:S(2)}) %all-to-all-start.2) | async-done | bytes 524320 | tf_op jit(solution)/shard_map/all_to_all | solution.py:661
  50.3 9.4 %all_to_all.41.refs_0_ = bf16[32,16,128]{2,1,0:T(8,128)(2,1)S(1)} all-to-all(bf16[32,16,128]{2,1,0:T(8,128)(2,1)} %shard_map.132), channel_id=1, replica_groups=mesh['gx'=8,'gy'=4] {'gx','gy'}, dimensions={0} | all-to-all | bytes 262144 | tf_op jit(solution)/shard_map/all_to_all | solution.py:661
  59.7 2.4 %shard_map.133 = (bf16[32,16,128]{2,1,0:T(8,128)(2,1)S(1)}, bf16[32,48,128]{2,1,0:T(8,128)(2,1)}) custom-call(bf16[32,16,128]{2,1,0:T(8,128)(2,1)S(1)} %all_to_all.41.refs_0_, bf16[32,64,128]{2,1,0:T(8,128)(2,1)S(1)} %all-to-all-done.2.refs_1_, bf16[256,128]{1,0:T(8,128)(2,1)S(1)} %get-tuple-element.32.refs_2_.refs_1_, ...), custom_call_target="tpu_custom_call" | custom-call | flops 2600000000 | bytes 1024 | tf_op jit(solution)/shard_map/pallas_call | solution.py:681
  62.2 10.8 %all_to_all.42.refs_1_ = bf16[32,16,128]{2,1,0:T(8,128)(2,1)} all-to-all(bf16[32,16,128]{2,1,0:T(8,128)(2,1)S(1)} %get-tuple-element.34), channel_id=1, replica_groups=mesh['gx'=8,'gy'=4] {'gx','gy'}, dimensions={0} | all-to-all | bytes 262144 | tf_op jit(solution)/shard_map/all_to_all | solution.py:661
  72.9 4.8 %all-to-all-start.4 = ((bf16[32,48,128]{2,1,0:T(8,128)(2,1)}), bf16[32,48,128]{2,1,0:T(8,128)(2,1)S(1)}, u32[]{:S(2)}, u32[]{:S(2)}) async-start(bf16[32,48,128]{2,1,0:T(8,128)(2,1)} %get-tuple-element.33.refs_2_), calls=%async_computation.4 | async-start | bytes 786432 | tf_op jit(solution)/shard_map/all_to_all | solution.py:661
  77.8 8.8 %shard_map.134.refs_1_ = bf16[32,16,128]{2,1,0:T(8,128)(2,1)} custom-call(bf16[2,16,32,64,64]{4,3,2,1,0:T(8,128)(2,1)} %refs_0_.4, bf16[32,16,128]{2,1,0:T(8,128)(2,1)} %all_to_all.42.refs_1_, bf16[32,48,128]{2,1,0:T(8,128)(2,1)} %get-tuple-element.33.refs_2_), custom_call_target="tpu_custom_call" | custom-call | flops 6499999744 | bytes 1024 | tf_op jit(solution)/shard_map/pallas_call | solution.py:681
  86.6 3.6 %all-to-all-done.4.refs_0_ = bf16[32,48,128]{2,1,0:T(8,128)(2,1)S(1)} async-done(((bf16[32,48,128]{2,1,0:T(8,128)(2,1)}), bf16[32,48,128]{2,1,0:T(8,128)(2,1)S(1)}, u32[]{:S(2)}, u32[]{:S(2)}) %all-to-all-start.4) | async-done | bytes 393248 | tf_op jit(solution)/shard_map/all_to_all | solution.py:661
  90.2 0.0 copy-start.1
  90.2 0.9 copy-done.1
  91.1 3.4 %shard_map.135 = (bf16[64,16,128]{2,1,0:T(8,128)(2,1)}, f32[64,16,128]{2,1,0:T(8,128)S(1)}, bf16[32,32,128]{2,1,0:T(8,128)(2,1)}) custom-call(bf16[32,48,128]{2,1,0:T(8,128)(2,1)S(1)} %all-to-all-done.4.refs_0_, bf16[32,16,128]{2,1,0:T(8,128)(2,1)S(1)} %copy-done.1, bf16[64,16,128]{2,1,0:T(8,128)(2,1)S(1)} %get-tuple-element.27.refs_1_.refs_2_, ...), custom_call_target="tpu_custom_call" | custom-call | flops 3800000000 | bytes 1024 | tf_op jit(solution)/shard_map/pallas_call | solution.py:681
  94.5 3.3 %all-to-all-start.6 = ((bf16[32,32,128]{2,1,0:T(8,128)(2,1)}), bf16[32,32,128]{2,1,0:T(8,128)(2,1)S(1)}, u32[]{:S(2)}, u32[]{:S(2)}) async-start(bf16[32,32,128]{2,1,0:T(8,128)(2,1)} %get-tuple-element.36.refs_2_), calls=%async_computation.6 | async-start | bytes 524288 | tf_op jit(solution)/shard_map/all_to_all | solution.py:661
  97.8 7.0 %shard_map.136.refs_3_ = bf16[2,16,32,64,64]{4,3,2,1,0:T(8,128)(2,1)} custom-call(bf16[32,32,128]{2,1,0:T(8,128)(2,1)} %copy-done, bf16[32,16,128]{2,1,0:T(8,128)(2,1)} %all_to_all.42.refs_1_, bf16[32,32,128]{2,1,0:T(8,128)(2,1)} %get-tuple-element.36.refs_2_), custom_call_target="tpu_custom_call" | custom-call | flops 6400000000 | bytes 1024 | tf_op jit(solution)/shard_map/pallas_call | solution.py:681
  104.8 2.6 %all-to-all-done.6.refs_0_ = bf16[32,32,128]{2,1,0:T(8,128)(2,1)S(1)} async-done(((bf16[32,32,128]{2,1,0:T(8,128)(2,1)}), bf16[32,32,128]{2,1,0:T(8,128)(2,1)S(1)}, u32[]{:S(2)}, u32[]{:S(2)}) %all-to-all-start.6) | async-done | bytes 262176 | tf_op jit(solution)/shard_map/all_to_all | solution.py:661
  107.3 1.4 %shard_map.137.refs_2_ = bf16[32,48,128]{2,1,0:T(8,128)(2,1)} custom-call(bf16[32,32,128]{2,1,0:T(8,128)(2,1)S(1)} %all-to-all-done.6.refs_0_, bf16[256,128]{1,0:T(8,128)(2,1)S(1)} %get-tuple-element.32.refs_2_.refs_1_, bf16[512,512]{1,0:T(8,128)(2,1)S(1)} %get-tuple-element.22.refs_1_.refs_3_.refs_2_, bf16[2,16,32,64,64]{4,3,2,1,0:T(8,128)(2,1)} %shard_map.136.refs_3_), custom_call_target="tpu_custom_call" | custom-call | flops 1300000000 | bytes 1024 | tf_op jit(solution)/shard_map/pallas_call | solution.py:681
  108.7 3.4 %all-to-all-start.7 = ((bf16[32,48,128]{2,1,0:T(8,128)(2,1)}), bf16[32,48,128]{2,1,0:T(8,128)(2,1)S(1)}, u32[]{:S(2)}, u32[]{:S(2)}) async-start(bf16[32,48,128]{2,1,0:T(8,128)(2,1)} %shard_map.137.refs_2_), calls=%async_computation.7 | async-start | bytes 786432 | tf_op jit(solution)/shard_map/all_to_all | solution.py:661
  112.1 7.0 %shard_map.139 = bf16[2,16,32,64,64]{4,3,2,1,0:T(8,128)(2,1)} custom-call(bf16[32,32,128]{2,1,0:T(8,128)(2,1)} %copy-done, bf16[32,16,128]{2,1,0:T(8,128)(2,1)} %all_to_all.42.refs_1_, bf16[32,48,128]{2,1,0:T(8,128)(2,1)} %shard_map.137.refs_2_, bf16[2,16,32,64,64]{4,3,2,1,0:T(8,128)(2,1)} %shard_map.136.refs_3_), custom_call_target="tpu_custom_call", output_to_operand_aliasing={{}: (3, {})} | custom-call | flops 6400000000 | bytes 1024 | tf_op jit(solution)/shard_map/pallas_call | solution.py:681
  119.1 5.4 %all-to-all-done.7.refs_0_ = bf16[32,48,128]{2,1,0:T(8,128)(2,1)S(1)} async-done(((bf16[32,48,128]{2,1,0:T(8,128)(2,1)}), bf16[32,48,128]{2,1,0:T(8,128)(2,1)S(1)}, u32[]{:S(2)}, u32[]{:S(2)}) %all-to-all-start.7) | async-done | bytes 393248 | tf_op jit(solution)/shard_map/all_to_all | solution.py:661
  124.5 0.9 shard_map.138
Async XLA Ops:
  0.6 15.6 %all-to-all-start = ((bf16[32,32,128]{2,1,0:T(8,128)(2,1)}), bf16[32,32,128]{2,1,0:T(8,128)(2,1)S(1)}, u32[]{:S(2)}, u32[]{:S(2)}) async-start(bf16[32,32,128]{2,1,0:T(8,128)(2,1)} %bitcast.1), calls=%async_computation | async-start | bytes 524288 | tf_op jit(solution)/shard_map/all_to_all | solution.py:661
  29.8 5.3 %copy-start = (bf16[32,32,128]{2,1,0:T(8,128)(2,1)}, bf16[32,32,128]{2,1,0:T(8,128)(2,1)S(1)}, u32[]{:S(2)}) copy-start(bf16[32,32,128]{2,1,0:T(8,128)(2,1)S(1)} %all_to_all.40.refs_0_.refs_1_) | copy-start | bytes 786436
  31.8 18.5 %all-to-all-start.2 = ((bf16[32,64,128]{2,1,0:T(8,128)(2,1)}), bf16[32,64,128]{2,1,0:T(8,128)(2,1)S(1)}, u32[]{:S(2)}, u32[]{:S(2)}) async-start(bf16[32,64,128]{2,1,0:T(8,128)(2,1)} %shard_map.131.refs_2_), calls=%async_computation.2 | async-start | bytes 1048576 | tf_op jit(solution)/shard_map/all_to_all | solution.py:661
  72.9 17.2 %all-to-all-start.4 = ((bf16[32,48,128]{2,1,0:T(8,128)(2,1)}), bf16[32,48,128]{2,1,0:T(8,128)(2,1)S(1)}, u32[]{:S(2)}, u32[]{:S(2)}) async-start(bf16[32,48,128]{2,1,0:T(8,128)(2,1)} %get-tuple-element.33.refs_2_), calls=%async_computation.4 | async-start | bytes 786432 | tf_op jit(solution)/shard_map/all_to_all | solution.py:661
  90.2 0.9 copy-start.1
  94.5 12.9 %all-to-all-start.6 = ((bf16[32,32,128]{2,1,0:T(8,128)(2,1)}), bf16[32,32,128]{2,1,0:T(8,128)(2,1)S(1)}, u32[]{:S(2)}, u32[]{:S(2)}) async-start(bf16[32,32,128]{2,1,0:T(8,128)(2,1)} %get-tuple-element.36.refs_2_), calls=%async_computation.6 | async-start | bytes 524288 | tf_op jit(solution)/shard_map/all_to_all | solution.py:661
  108.7 15.7 %all-to-all-start.7 = ((bf16[32,48,128]{2,1,0:T(8,128)(2,1)}), bf16[32,48,128]{2,1,0:T(8,128)(2,1)S(1)}, u32[]{:S(2)}, u32[]{:S(2)}) async-start(bf16[32,48,128]{2,1,0:T(8,128)(2,1)} %shard_map.137.refs_2_), calls=%async_computation.7 | async-start | bytes 786432 | tf_op jit(solution)/shard_map/all_to_all | solution.py:661

commit v3 on v2

--- a/solution.py
+++ b/solution.py
@@ -188,6 +188,7 @@
 EDGE = 16
 GROUP = 8
 CHUNK = 2
+MIXED = 8
 
 
 class Plan:
@@ -347,13 +348,13 @@
     return jnp.concatenate(planes, 1)
 
 
-def read_plane(plan, ref, c, k):
-    rows = slice(c * plan.bx, (c + 1) * plan.bx)
+def read_plane(plan, ref, c, k, first=0):
+    rows = slice(first + c * plan.bx, first + (c + 1) * plan.bx)
     return jnp.concatenate([ref[i * plan.gy + k, rows] for i in range(plan.gx)], 0)
 
 
-def write_plane(plan, ref, c, k, values):
-    rows = slice(c * plan.bx, (c + 1) * plan.bx)
+def write_plane(plan, ref, c, k, values, first=0):
+    rows = slice(first + c * plan.bx, first + (c + 1) * plan.bx)
     for i in range(plan.gx):
         ref[i * plan.gy + k, rows] = values[i * plan.bx : (i + 1) * plan.bx]
 
@@ -374,7 +375,7 @@
     return z * cdf, slope
 
 
-def middle_kernel(plan, held, modes_ref, conv_ref, out_ref, z_ref, grads):
+def middle_kernel(plan, held, modes_ref, out_ref, grads):
     lane = lax.broadcasted_iota(jnp.int32, (1, plan.gy * plan.lanes), 1)
     zero = jnp.logical_and(lane < plan.lanes, lax.rem(lane, plan.my) == 0)
     doubled = jnp.where(zero, 1.0, 2.0)
@@ -382,15 +383,15 @@
     for c in range(plan.cpd):
         for k in range(plan.gy):
             start = c * plan.ny + k * plan.by
-            z = syn[:, start : start + plan.by] + read_plane(plan, conv_ref, c, k).astype(F32)
+            z = syn[:, start : start + plan.by] + read_plane(plan, modes_ref, c, k, plan.mx).astype(F32)
             z = z.astype(BF16)
-            write_plane(plan, z_ref, c, k, z)
+            write_plane(plan, out_ref, c, k, z, plan.mx)
             slope = gelu_parts(z.astype(F32))[1]
-            cot = read_plane(plan, conv_ref, plan.cpd + c, k).astype(F32)
+            cot = read_plane(plan, modes_ref, plan.cpd + c, k, plan.mx).astype(F32)
             grads[:, start : start + plan.by] = (cot * slope).astype(BF16)
     planes = grads[...]
     analyse_plane(plan, held, planes, doubled * plan.scale, out_ref)
-    put_edges(plan, held, planes, z_ref, plan.rows)
+    put_edges(plan, held, planes, out_ref, plan.mx + plan.rows)
 
 
 def last_kernel(plan, held, both_ref, out_ref):
@@ -439,65 +440,129 @@
     return lax.rem(row, groups) == lax.div(lane, width)
 
 
-def load_kernel(plan, *refs):
-    count = len(refs) // 2
-    copies = [pltpu.make_async_copy(refs[i], refs[count + i], refs[-1].at[i]) for i in range(count)]
-    for copy in copies:
+def pack_rows(plan, first_j, count, r_ref, packed_ref, arrived, packed, in_sems, out_sems, others=()):
+    chunks = count // CHUNK
+
+    def part(t, start=0):
+        return pl.ds(start + t * CHUNK, CHUNK)
+
+    loads = [
+        pltpu.make_async_copy(r_ref.at[:, part(t, first_j)], arrived.at[:, part(t)], in_sems.at[t])
+        for t in range(chunks)
+    ]
+    stores = [
+        pltpu.make_async_copy(packed.at[part(t)], packed_ref.at[part(t, first_j)], out_sems.at[t])
+        for t in range(chunks)
+    ]
+    for copy in loads + list(others):
         copy.start()
-    for copy in copies:
+    for t in range(chunks):
+        loads[t].wait()
+        for j in range(t * CHUNK, (t + 1) * CHUNK):
+            packed[j] = jnp.concatenate([arrived[0, j], arrived[1, j]], -1)
+        stores[t].start()
+    for copy in list(others) + stores:
         copy.wait()
 
 
-def each_mode_row(plan, product, r_ref, x_ref, y_ref, flat, turned, rows, held, sems):
+def load_kernel(plan, half, *refs):
+    count = (len(refs) - 7) // 2
+    r_ref, sources = refs[0], refs[1 : 1 + count]
+    packed_ref, places = refs[1 + count], refs[2 + count : 2 + 2 * count]
+    arrived, packed, sems, in_sems, out_sems = refs[2 + 2 * count :]
+    copies = [
+        pltpu.make_async_copy(source, place, sems.at[i])
+        for i, (source, place) in enumerate(zip(sources, places))
+    ]
+    pack_rows(plan, 0, half, r_ref, packed_ref, arrived, packed, in_sems, out_sems, copies)
+
+
+def each_mode_row(plan, product, first, r_ref, x_ref, y_ref, flat, turned, rows, held, sems):
     width = plan.channels
     copies = [
         pltpu.make_async_copy(
-            r_ref.at[:, pl.ds(t * CHUNK, CHUNK)], held.at[:, pl.ds(t * CHUNK, CHUNK)], sems.at[t]
-        )
-        for t in range(plan.mx // CHUNK)
+            r_ref.at[pl.ds(t * MIXED, MIXED)], held.at[pl.ds(t * MIXED, MIXED)], sems.at[t]
+        )
+        for t in range(plan.mx // MIXED)
     ]
     for copy in copies:
         copy.start()
     modes_to_rows(plan, x_ref, flat, turned, rows)
+    first()
     mask = group_mask(2 * GROUP, GROUP, width)
-    for j in range(plan.mx):
-        if j % CHUNK == 0:
-            copies[j // CHUNK].wait()
+
+    def step(j, carry):
         real_out, imag_out = [], []
         for g in range(plan.my // GROUP):
             start = g * GROUP
             real = rows[j, start : start + GROUP, :]
             imag = rows[j, plan.my + start : plan.my + start + GROUP, :]
-            weights = [
-                held[part, j, start : start + GROUP].reshape(GROUP * width, width)
-                for part in range(2)
-            ]
-            real, imag = product(mask, real, imag, *weights)
+            weights = held[j, start : start + GROUP].reshape(GROUP * width, 2 * width)
+            real, imag = product(mask, real, imag, weights)
             real_out.append(real)
             imag_out.append(imag)
         rows_to_modes(plan, jnp.concatenate(real_out + imag_out, 0), turned, flat, j)
-    y_ref[...] = flat[...].reshape(plan.devices, plan.mx, plan.lanes).astype(BF16)
-
-
-def mix_kernel(plan, held, *refs):
-    def product(mask, real, imag, r_real, r_imag):
-        first = jnp.concatenate([jnp.concatenate([real, imag], 0)] * GROUP, 1)
-        second = jnp.concatenate([jnp.concatenate([-imag, real], 0)] * GROUP, 1)
-        mixed = dot(jnp.where(mask, first, 0.0).astype(BF16), r_real)
-        mixed = mixed + dot(jnp.where(mask, second, 0.0).astype(BF16), r_imag)
-        return mixed[:GROUP], mixed[GROUP:]
-
-    each_mode_row(plan, product, *refs)
-
-
-def back_kernel(plan, held, *refs):
+        return carry
+
+    for t, copy in enumerate(copies):
+        copy.wait()
+        lax.fori_loop(t * MIXED, (t + 1) * MIXED, step, 0, unroll=8)
+    values = flat[...].reshape(plan.devices, plan.mx, plan.lanes)
+    y_ref[:, : plan.mx] = values.astype(BF16)
+
+
+class Arrival:
+    def __init__(self, source, place, sem):
+        self.copy, self.place, self.there = pltpu.make_async_copy(source, place, sem), place, False
+        self.copy.start()
+
+    def __getitem__(self, index):
+        if not self.there:
+            self.copy.wait()
+            self.there = True
+        return self.place[index]
+
+
+def bring(sources, refs):
+    count = len(sources)
+    arrivals = {
+        name: Arrival(source, refs[i], refs[count].at[i])
+        for i, (name, source) in enumerate(sources)
+    }
+    return arrivals, refs[count + 1 :]
+
+
+def mix_kernel(plan, held, r_ref, field_ref, cot_ref, kernel_ref, x_ref, y_ref, *refs):
     width = plan.channels
-
-    def product(mask, real, imag, r_real, r_imag):
+    held, refs = bring((("field", field_ref), ("kernel", kernel_ref)), refs)
+    cot = pltpu.make_async_copy(cot_ref, y_ref.at[:, pl.ds(plan.mx + plan.rows, plan.rows)], refs[-1])
+    cot.start()
+    refs = refs[:-1]
+
+    def product(mask, real, imag, weights):
+        left = jnp.concatenate([jnp.concatenate([real, imag], 0)] * GROUP, 1)
+        mixed = dot(jnp.where(mask, left, 0.0).astype(BF16), weights)
+        return (
+            mixed[:GROUP, :width] - mixed[GROUP:, width:],
+            mixed[:GROUP, width:] + mixed[GROUP:, :width],
+        )
+
+    conv = partial(conv_part, plan, held, x_ref, y_ref, *refs[:4])
+    each_mode_row(plan, product, conv, r_ref, x_ref, y_ref, *refs[4:])
+    cot.wait()
+
+
+def back_kernel(
+    plan, held, r_ref, field_ref, cot_ref, kernel_ref, g_ref, layer_ref, grad_ref, both_ref, *refs
+):
+    width = plan.channels
+    sources = (("field", field_ref), ("cotangent", cot_ref), ("kernel", kernel_ref))
+    held, refs = bring(sources, refs)
+
+    def product(mask, real, imag, weights):
         left = jnp.concatenate(
             [jnp.concatenate([real, imag], 1), jnp.concatenate([imag, -real], 1)], 0
         )
-        weights = jnp.concatenate([r_real, r_imag], 1)
         mixed = jnp.where(mask, dot_nt(left.astype(BF16), weights), 0.0)
         total = mixed[:, : 2 * width]
         for i in range(1, GROUP // 2):
@@ -505,7 +570,8 @@
         total = total[:, :width] + total[:, width:]
         return total[:GROUP], total[GROUP:]
 
-    each_mode_row(plan, product, *refs)
+    space = partial(space_part, plan, held, g_ref, layer_ref, grad_ref, both_ref, *refs[:5])
+    each_mode_row(plan, product, space, r_ref, g_ref, both_ref, *refs[5:])
 
 
 def outer_kernel(
@@ -589,22 +655,22 @@
         out[pl.ds(x, plan.channels, stride=bx), :] = total[:, x * by : (x + 1) * by]
 
 
-def conv_kernel(plan, held, both_ref, out_ref, block, edges, paired, taps):
+def conv_part(plan, held, both_ref, out_ref, block, edges, paired, taps):
     edges[...] = both_ref[:, plan.mx :, :].astype(F32).reshape(edges.shape)
     block[...] = held["field"][...].astype(F32).reshape(block.shape)
     fill_taps(plan, block, edges, paired, taps)
     kernel_ref = held["kernel"]
     weights = [jnp.concatenate([kernel_ref[a, b] for b in range(3)], 1) for a in range(3)]
     convolve(plan, weights, taps, block)
-    out_ref[:, : plan.rows] = block[...].reshape(plan.devices, plan.rows, plan.by).astype(BF16)
-    out_ref[:, plan.rows :] = held["cotangent"][...].reshape(plan.devices, plan.rows, plan.by)
-
-
-def space_kernel(
-    plan, held, z_ref, back_ref, layer_ref, grad_ref, both_ref, block, edges, paired, taps, flat
+    shape = (plan.devices, plan.rows, plan.by)
+    out_ref[:, plan.mx : plan.mx + plan.rows] = block[...].reshape(shape).astype(BF16)
+
+
+def space_part(
+    plan, held, z_ref, layer_ref, grad_ref, both_ref, block, edges, paired, taps, flat
 ):
     c, bx, by, s = plan.channels, plan.bx, plan.by, plan.devices
-    z = z_ref[:, : plan.rows, :].astype(F32).reshape(c, bx, by)
+    z = z_ref[:, plan.mx : plan.mx + plan.rows, :].astype(F32).reshape(c, bx, by)
     activated, slope = gelu_parts(z)
     field = held["field"][...].astype(F32)
     layer_ref[...] = (field + activated).astype(BF16)
@@ -614,7 +680,7 @@
     cot_ref = held["cotangent"]
     grads = (cot_ref[...].astype(F32) * slope).astype(BF16).astype(F32)
     block[...] = grads.reshape(block.shape)
-    edges[...] = z_ref[:, plan.rows :, :].astype(F32).reshape(edges.shape)
+    edges[...] = z_ref[:, plan.mx + plan.rows :, :].astype(F32).reshape(edges.shape)
     fill_taps(plan, block, edges, paired, taps)
     kernel_ref = held["kernel"]
     weights = [
@@ -633,7 +699,6 @@
     edges[...] = jnp.zeros(edges.shape, F32)
     for t in range(half // s):
         edges[pl.ds(t, s, stride=EDGE), :] = terms[t * s : (t + 1) * s]
-    both_ref[:, : plan.mx, :] = back_ref[...]
     both_ref[:, plan.mx :, :] = edges[...].reshape(s, EDGE, by).astype(BF16)
 
 
@@ -701,28 +766,38 @@
     edges = pltpu.VMEM((n * EDGE, by), F32)
     paired = pltpu.VMEM((channels, by), F32)
     taps = pltpu.VMEM((3 * channels, (bx + 2) * by), BF16)
+    place = pltpu.VMEM(field.shape, BF16)
+    kernel_place = pltpu.VMEM(kernel_weight.shape, BF16)
     field_flat = pltpu.VMEM((channels, bx * by), BF16)
     modes_scratch = [
         flat,
         turned,
         rows,
-        pltpu.VMEM((2, plan.mx, plan.my, channels, channels), BF16),
+        pltpu.VMEM((plan.mx, plan.my, channels, 2 * channels), BF16),
         pltpu.SemaphoreType.DMA((plan.mx // CHUNK,)),
     ]
     edge_tables = ("pick_rows", "pick_cols", "window")
 
     field_c = exchange(field.reshape(n, plan.rows, by))
     sources = {name: jnp.asarray(t) for name, t in plan.named().items()}
-    sources.update(field=field, cotangent=cotangent, kernel=kernel_weight)
-    held = pl.pallas_call(
-        partial(load_kernel, plan),
-        out_shape=tuple(pltpu.VMEM(t.shape, t.dtype) for t in sources.values()),
-        in_specs=[anywhere] * len(sources),
-        out_specs=(here,) * len(sources),
-        scratch_shapes=[pltpu.SemaphoreType.DMA((len(sources),))],
-        cost_estimate=pl.CostEstimate(flops=2_500_000_000, bytes_accessed=1024, transcendentals=0),
-        compiler_params=pltpu.CompilerParams(vmem_limit_bytes=60 * 1024 * 1024),
-    )(*sources.values())
+    packed_shape = (plan.mx, plan.my, channels, 2 * channels)
+    half = plan.mx // 2
+    chunk_sems = pltpu.SemaphoreType.DMA((half // CHUNK,))
+    pack_scratch = [
+        pltpu.VMEM((2, half) + packed_shape[1:-1] + (channels,), BF16),
+        pltpu.VMEM((half,) + packed_shape[1:], BF16),
+    ]
+    weights, *held = pl.pallas_call(
+        partial(load_kernel, plan, half),
+        out_shape=(jax.ShapeDtypeStruct(packed_shape, BF16),)
+        + tuple(pltpu.VMEM(t.shape, t.dtype) for t in sources.values()),
+        in_specs=[anywhere] * (1 + len(sources)),
+        out_specs=(anywhere,) + (here,) * len(sources),
+        scratch_shapes=pack_scratch
+        + [pltpu.SemaphoreType.DMA((len(sources),)), chunk_sems, chunk_sems],
+        cost_estimate=pl.CostEstimate(flops=5_000_000_000, bytes_accessed=1024, transcendentals=0),
+        compiler_params=pltpu.CompilerParams(vmem_limit_bytes=58 * 1024 * 1024),
+    )(spectral_weight, *sources.values())
     held = dict(zip(sources, held))
     a_part = call(
         first_kernel,
@@ -732,61 +807,51 @@
         mib=20,
     )
     a_both = exchange(a_part)
-    conv = call(
-        conv_kernel,
-        rows_of(2 * plan.rows),
-        a_both,
-        use=("field", "cotangent", "kernel"),
-        scratch=[block, edges, paired, taps],
-        us=1.5,
-        mib=20,
-    )
-    conv_c = exchange(conv)
+    weights = call(
+        lambda plan, held, r_ref, after_ref, first_ref, *refs: pack_rows(
+            plan, half, half, r_ref, *refs
+        ),
+        jax.ShapeDtypeStruct(packed_shape, BF16),
+        raw=(spectral_weight, a_part, weights),
+        scratch=pack_scratch + [chunk_sems, chunk_sems],
+        spec=anywhere,
+        us=5.0,
+        alias=True,
+    )
     b_part = call(
         mix_kernel,
-        rows_of(plan.mx),
+        rows_of(plan.mx + 2 * plan.rows),
         a_both,
-        raw=(spectral_weight,),
-        scratch=modes_scratch,
-        us=6.5,
-        after=(conv,),
-    )
-    b_part, conv_c = lax.optimization_barrier((b_part, conv_c))
-    b_modes = exchange(b_part)
-    g_part, z_part = call(
+        raw=(weights, field, cotangent.reshape(n, plan.rows, by), kernel_weight),
+        scratch=[place, kernel_place, pltpu.SemaphoreType.DMA((2,))]
+        + [block, edges, paired, taps]
+        + modes_scratch
+        + [pltpu.SemaphoreType.DMA],
+        us=6.0,
+    )
+    g_part = call(
         middle_kernel,
-        (rows_of(plan.mx), rows_of(plan.rows + EDGE)),
-        b_modes,
-        conv_c,
+        rows_of(plan.mx + plan.rows + EDGE),
+        exchange(b_part),
         use=("row_s", "col", "row") + edge_tables,
         mib=20,
         scratch=[pltpu.VMEM((plan.nx, cpd * plan.ny), BF16)],
         us=2.6,
     )
-    g_modes = exchange(g_part)
-    z_both = exchange(z_part)
-    back_part = call(
+    g_both = exchange(g_part)
+    layer_out, grad_sum, back_terms = call(
         back_kernel,
-        rows_of(plan.mx),
-        g_modes,
-        raw=(spectral_weight,),
-        scratch=modes_scratch,
-        us=6.5,
-        after=(z_part,),
-    )
-    layer_out, grad_sum, back_terms = call(
-        space_kernel,
         (
             jax.ShapeDtypeStruct(field.shape, BF16),
             jax.ShapeDtypeStruct(field.shape, F32),
             rows_of(plan.mx + EDGE),
         ),
-        z_both,
-        back_part,
-        use=("field", "cotangent", "kernel"),
-        mib=20,
-        scratch=[block, edges, paired, taps, field_flat],
-        us=3.8,
+        g_both,
+        raw=(weights, field, cotangent, kernel_weight),
+        scratch=[place, place, kernel_place, pltpu.SemaphoreType.DMA((3,))]
+        + [block, edges, paired, taps, field_flat]
+        + modes_scratch,
+        us=8.0,
     )
     back_both = exchange(back_terms)
 
@@ -795,7 +860,7 @@
             lambda plan, *refs: outer_kernel(plan, first_j, count, *refs),
             jax.ShapeDtypeStruct(spectral_weight.shape, BF16),
             a_both,
-            g_modes,
+            g_both,
             scratch=[
                 flat,
                 flat,
@@ -810,7 +875,6 @@
             alias=alias,
         )
 
-    half = plan.mx // 2
     spectral_half = outer_part(0, half, (back_terms,), False)
     last_part = call(
         last_kernel,

time: 128 us -> 122 us (0.953)
  waiting for transfers between devices: 26.5 us -> 15 us
  blocking collectives: 32.9 us -> 39.7 us
  starting transfers between devices: 21 us -> 16.2 us
  Pallas kernels: 43.4 us -> 47.7 us
    all_to_all x5 -> x4, waiting for transfers between devices: 26.5 us -> 15 us  [exchange(): return lax.all_to_all(x, BOTH, 0, 0, tiled=True)]
    all_to_all x3 -> x2, blocking collectives: 32.9 us -> 39.7 us  [exchange(): return lax.all_to_all(x, BOTH, 0, 0, tiled=True)]
    all_to_all x5 -> x4, starting transfers between devices: 21 us -> 16.2 us  [exchange(): return lax.all_to_all(x, BOTH, 0, 0, tiled=True)]
    pallas_call x1, Pallas kernels: 1.51 us -> 5.96 us  [fast_body(): pl.pallas_call(partial(load_kernel, plan, half), out_shape=(jax.ShapeDtyp...]
    pallas_call x10 -> x9, Pallas kernels: 41.9 us -> 41.8 us  [call(): pl.pallas_call(run, out_shape=outs, in_specs=[anywhere] * len(raw) + [her...]
  transfers between devices with their start and end apart: 5 -> 4, of which waited for: 5 -> 4; matrix products, arithmetic and copies ran while one was open for 0% -> 0% of each run, Pallas kernels for 26% -> 22%
where the time goes in v3:
time: 122 us; the launch traced here: 120 us
  Pallas kernels  47.7 us (39%)
  blocking collectives  39.7 us (33%)
  starting transfers between devices  16.2 us (13%)
  waiting for transfers between devices  15 us (12%)
    pallas_call x9, Pallas kernels, call(): pl.pallas_call(run, out_shape=outs, in_specs=[anywhere] * len(raw) + [her...  41.8 us
    all_to_all x2, blocking collectives, exchange(): return lax.all_to_all(x, BOTH, 0, 0, tiled=True)  39.7 us
    all_to_all x4, starting transfers between devices, exchange(): return lax.all_to_all(x, BOTH, 0, 0, tiled=True)  16.2 us
    all_to_all x4, waiting for transfers between devices, exchange(): return lax.all_to_all(x, BOTH, 0, 0, tiled=True)  15 us
    pallas_call x1, Pallas kernels, fast_body(): pl.pallas_call(partial(load_kernel, plan, half), out_shape=(jax.ShapeDtyp...  5.96 us
  transfers between devices with their start and end apart: 4, of which 4 were waited for; matrix products, arithmetic and copies ran while one was open for 0% of the time, Pallas kernels for 22%

profile of v3, /device:TPU:8, one launch (start us, length us, event | category | flops | bytes accessed | tf_op | source)
XLA Modules:
  0.0 120.1 jit_solution(15903086378552545004)
XLA Ops:
  0.6 6.0 %all-to-all-start = ((bf16[32,32,128]{2,1,0:T(8,128)(2,1)}), bf16[32,32,128]{2,1,0:T(8,128)(2,1)S(1)}, u32[]{:S(2)}, u32[]{:S(2)}) async-start(bf16[32,32,128]{2,1,0:T(8,128)(2,1)} %bitcast.2), calls=%async_computation | async-start | bytes 524288 | tf_op jit(solution)/shard_map/all_to_all | solution.py:726
  6.7 6.0 %shard_map.129 = (bf16[16,32,64,128]{3,2,1,0:T(8,128)(2,1)}, bf16[512,512]{1,0:T(8,128)(2,1)S(1)}, bf16[128,512]{1,0:T(8,128)(2,1)S(1)}, bf16[256,128]{1,0:T(8,1...) custom-call(bf16[2,16,32,64,64]{4,3,2,1,0:T(8,128)(2,1)} %refs_0_.3, ...), custom_call_target="tpu_custom_call" | custom-call | flops 5000000000 | bytes 1024 | tf_op jit(solution)/shard_map/pallas_call | solution.py:790
  12.7 3.6 %all-to-all-done.refs_0_ = bf16[32,32,128]{2,1,0:T(8,128)(2,1)S(1)} async-done(((bf16[32,32,128]{2,1,0:T(8,128)(2,1)}), bf16[32,32,128]{2,1,0:T(8,128)(2,1)S(1)}, u32[]{:S(2)}, u32[]{:S(2)}) %all-to-all-start) | async-done | bytes 262176 | tf_op jit(solution)/shard_map/all_to_all | solution.py:726
  16.2 1.6 %shard_map.130.refs_1_ = bf16[32,32,128]{2,1,0:T(8,128)(2,1)} custom-call(bf16[32,32,128]{2,1,0:T(8,128)(2,1)S(1)} %all-to-all-done.refs_0_, bf16[512,512]{1,0:T(8,128)(2,1)S(1)} %get-tuple-element.16.refs_1_.refs_2_, bf16[128,512]{1,0:T(8,128)(2,1)S(1)} %get-tuple-element.17.refs_2_.refs_3_, bf16[128,256]{1,0:T(8,128)(2,1)S(1)} %get-tuple-element.18.refs_3_.refs_4_, ...), custom_call_target="tpu_custom_call" | custom-call | flops 1000000000 | bytes 1024 | tf_op jit(solution)/shard_map/pallas_call | solution.py:746
  17.8 3.4 %all-to-all-start.1 = ((bf16[32,32,128]{2,1,0:T(8,128)(2,1)}), bf16[32,32,128]{2,1,0:T(8,128)(2,1)S(1)}, u32[]{:S(2)}, u32[]{:S(2)}) async-start(bf16[32,32,128]{2,1,0:T(8,128)(2,1)} %shard_map.130.refs_1_), calls=%async_computation.1 | async-start | bytes 524288 | tf_op jit(solution)/shard_map/all_to_all | solution.py:726
  21.2 5.6 %shard_map.131.refs_0_ = bf16[16,32,64,128]{3,2,1,0:T(8,128)(2,1)} custom-call(bf16[2,16,32,64,64]{4,3,2,1,0:T(8,128)(2,1)} %refs_0_.3, bf16[32,32,128]{2,1,0:T(8,128)(2,1)} %shard_map.130.refs_1_, bf16[16,32,64,128]{3,2,1,0:T(8,128)(2,1)} %get-tuple-element.21.refs_2_), custom_call_target="tpu_custom_call", output_to_operand_aliasing={{}: (2, {})} | custom-call | flops 5000000000 | bytes 1024 | tf_op jit(solution)/shard_map/pallas_call | solution.py:746
  26.8 3.9 %all-to-all-done.1.refs_4_.refs_0_ = bf16[32,32,128]{2,1,0:T(8,128)(2,1)S(1)} async-done(((bf16[32,32,128]{2,1,0:T(8,128)(2,1)}), bf16[32,32,128]{2,1,0:T(8,128)(2,1)S(1)}, u32[]{:S(2)}, u32[]{:S(2)}) %all-to-all-start.1) | async-done | bytes 262176 | tf_op jit(solution)/shard_map/all_to_all | solution.py:726
  30.7 0.0 copy-start.1
  30.7 0.7 copy-done.1
  31.4 7.1 %shard_map.132 = bf16[32,80,128]{2,1,0:T(8,128)(2,1)} custom-call(bf16[16,32,64,128]{3,2,1,0:T(8,128)(2,1)} %shard_map.131.refs_0_, bf16[64,16,128]{2,1,0:T(8,128)(2,1)} %refs_1_.4, bf16[32,32,128]{2,1,0:T(8,128)(2,1)} %bitcast.3, bf16[3,3,64,64]{3,2,1,0:T(8,128)(2,1)} %refs_3_.4, bf16[32,32,128]{2,1,0:T(8,128)(2,1)} %copy-done.1), custom_call_target="tpu_custom_call" | custom-call | flops 6000000000 | bytes 1024 | tf_op jit(solution)/shard_map/pallas_call | solution.py:746
  38.6 21.4 %all_to_all.30.refs_0_ = bf16[32,80,128]{2,1,0:T(8,128)(2,1)S(1)} all-to-all(bf16[32,80,128]{2,1,0:T(8,128)(2,1)} %shard_map.132), channel_id=1, replica_groups=mesh['gx'=8,'gy'=4] {'gx','gy'}, dimensions={0} | all-to-all | bytes 1310720 | tf_op jit(solution)/shard_map/all_to_all | solution.py:726
  59.9 1.7 %shard_map.133 = bf16[32,64,128]{2,1,0:T(8,128)(2,1)S(1)} custom-call(bf16[32,80,128]{2,1,0:T(8,128)(2,1)S(1)} %all_to_all.30.refs_0_, bf16[256,128]{1,0:T(8,128)(2,1)S(1)} %get-tuple-element.22.refs_1_, bf16[512,512]{1,0:T(8,128)(2,1)S(1)} %get-tuple-element.16.refs_1_.refs_2_, bf16[128,512]{1,0:T(8,128)(2,1)S(1)} %get-tuple-element.17.refs_2_.refs_3_, ...), custom_call_target="tpu_custom_call" | custom-call | flops 2600000000 | bytes 1024 | tf_op jit(solution)/shard_map/pallas_call | solution.py:746
  61.6 18.3 %all_to_all.31.refs_4_.refs_1_ = bf16[32,64,128]{2,1,0:T(8,128)(2,1)} all-to-all(bf16[32,64,128]{2,1,0:T(8,128)(2,1)S(1)} %shard_map.133), channel_id=1, replica_groups=mesh['gx'=8,'gy'=4] {'gx','gy'}, dimensions={0} | all-to-all | bytes 1048576 | tf_op jit(solution)/shard_map/all_to_all | solution.py:726
  80.0 9.1 %shard_map.134 = (bf16[64,16,128]{2,1,0:T(8,128)(2,1)}, f32[64,16,128]{2,1,0:T(8,128)}, bf16[32,32,128]{2,1,0:T(8,128)(2,1)}) custom-call(bf16[16,32,64,128]{3,2,1,0:T(8,128)(2,1)} %shard_map.131.refs_0_, bf16[64,16,128]{2,1,0:T(8,128)(2,1)} %refs_1_.4, bf16[64,16,128]{2,1,0:T(8,128)(2,1)} %refs_2_.2, bf16[3,3,64,64]{3,2,1,0:T(8,128)(2,1)} %refs_3_.4, ...), custom_call_target="tpu_custom_call" | custom-call | flops 8000000000 | bytes 1024 | tf_op jit(solution)/shard_map/pallas_call | solution.py:746
  89.1 3.3 %all-to-all-start.4 = ((bf16[32,32,128]{2,1,0:T(8,128)(2,1)}), bf16[32,32,128]{2,1,0:T(8,128)(2,1)S(1)}, u32[]{:S(2)}, u32[]{:S(2)}) async-start(bf16[32,32,128]{2,1,0:T(8,128)(2,1)} %get-tuple-element.24.refs_2_), calls=%async_computation.4 | async-start | bytes 524288 | tf_op jit(solution)/shard_map/all_to_all | solution.py:726
  92.4 7.1 %shard_map.135.refs_3_ = bf16[2,16,32,64,64]{4,3,2,1,0:T(8,128)(2,1)} custom-call(bf16[32,32,128]{2,1,0:T(8,128)(2,1)} %copy-done.1, bf16[32,64,128]{2,1,0:T(8,128)(2,1)} %all_to_all.31.refs_4_.refs_1_, bf16[32,32,128]{2,1,0:T(8,128)(2,1)} %get-tuple-element.24.refs_2_), custom_call_target="tpu_custom_call" | custom-call | flops 6400000000 | bytes 1024 | tf_op jit(solution)/shard_map/pallas_call | solution.py:746
  99.5 2.4 %all-to-all-done.4.refs_0_ = bf16[32,32,128]{2,1,0:T(8,128)(2,1)S(1)} async-done(((bf16[32,32,128]{2,1,0:T(8,128)(2,1)}), bf16[32,32,128]{2,1,0:T(8,128)(2,1)S(1)}, u32[]{:S(2)}, u32[]{:S(2)}) %all-to-all-start.4) | async-done | bytes 262176 | tf_op jit(solution)/shard_map/all_to_all | solution.py:726
  102.0 1.4 %shard_map.136.refs_2_ = bf16[32,48,128]{2,1,0:T(8,128)(2,1)} custom-call(bf16[32,32,128]{2,1,0:T(8,128)(2,1)S(1)} %all-to-all-done.4.refs_0_, bf16[256,128]{1,0:T(8,128)(2,1)S(1)} %get-tuple-element.22.refs_1_, bf16[512,512]{1,0:T(8,128)(2,1)S(1)} %get-tuple-element.16.refs_1_.refs_2_, bf16[2,16,32,64,64]{4,3,2,1,0:T(8,128)(2,1)} %shard_map.135.refs_3_), custom_call_target="tpu_custom_call" | custom-call | flops 1300000000 | bytes 1024 | tf_op jit(solution)/shard_map/pallas_call | solution.py:746
  103.4 3.4 %all-to-all-start.5 = ((bf16[32,48,128]{2,1,0:T(8,128)(2,1)}), bf16[32,48,128]{2,1,0:T(8,128)(2,1)S(1)}, u32[]{:S(2)}, u32[]{:S(2)}) async-start(bf16[32,48,128]{2,1,0:T(8,128)(2,1)} %shard_map.136.refs_2_), calls=%async_computation.5 | async-start | bytes 786432 | tf_op jit(solution)/shard_map/all_to_all | solution.py:726
  106.8 0.0 copy-start
  106.8 7.1 %shard_map.138 = bf16[2,16,32,64,64]{4,3,2,1,0:T(8,128)(2,1)} custom-call(bf16[32,32,128]{2,1,0:T(8,128)(2,1)} %copy-done.1, bf16[32,64,128]{2,1,0:T(8,128)(2,1)} %all_to_all.31.refs_4_.refs_1_, bf16[32,48,128]{2,1,0:T(8,128)(2,1)} %shard_map.136.refs_2_, bf16[2,16,32,64,64]{4,3,2,1,0:T(8,128)(2,1)} %shard_map.135.refs_3_), custom_call_target="tpu_custom_call", output_to_operand_aliasing={{}: (3, {})} | custom-call | flops 6400000000 | bytes 1024 | tf_op jit(solution)/shard_map/pallas_call | solution.py:746
  114.0 5.2 %all-to-all-done.5.refs_0_ = bf16[32,48,128]{2,1,0:T(8,128)(2,1)S(1)} async-done(((bf16[32,48,128]{2,1,0:T(8,128)(2,1)}), bf16[32,48,128]{2,1,0:T(8,128)(2,1)S(1)}, u32[]{:S(2)}, u32[]{:S(2)}) %all-to-all-start.5) | async-done | bytes 393248 | tf_op jit(solution)/shard_map/all_to_all | solution.py:726
  119.1 0.0 copy-done
  119.1 0.9 shard_map.137
Async XLA Ops:
  0.6 15.6 %all-to-all-start = ((bf16[32,32,128]{2,1,0:T(8,128)(2,1)}), bf16[32,32,128]{2,1,0:T(8,128)(2,1)S(1)}, u32[]{:S(2)}, u32[]{:S(2)}) async-start(bf16[32,32,128]{2,1,0:T(8,128)(2,1)} %bitcast.2), calls=%async_computation | async-start | bytes 524288 | tf_op jit(solution)/shard_map/all_to_all | solution.py:726
  17.8 12.9 %all-to-all-start.1 = ((bf16[32,32,128]{2,1,0:T(8,128)(2,1)}), bf16[32,32,128]{2,1,0:T(8,128)(2,1)S(1)}, u32[]{:S(2)}, u32[]{:S(2)}) async-start(bf16[32,32,128]{2,1,0:T(8,128)(2,1)} %shard_map.130.refs_1_), calls=%async_computation.1 | async-start | bytes 524288 | tf_op jit(solution)/shard_map/all_to_all | solution.py:726
  30.7 0.7 copy-start.1
  89.1 12.8 %all-to-all-start.4 = ((bf16[32,32,128]{2,1,0:T(8,128)(2,1)}), bf16[32,32,128]{2,1,0:T(8,128)(2,1)S(1)}, u32[]{:S(2)}, u32[]{:S(2)}) async-start(bf16[32,32,128]{2,1,0:T(8,128)(2,1)} %get-tuple-element.24.refs_2_), calls=%async_computation.4 | async-start | bytes 524288 | tf_op jit(solution)/shard_map/all_to_all | solution.py:726
  103.4 15.8 %all-to-all-start.5 = ((bf16[32,48,128]{2,1,0:T(8,128)(2,1)}), bf16[32,48,128]{2,1,0:T(8,128)(2,1)S(1)}, u32[]{:S(2)}, u32[]{:S(2)}) async-start(bf16[32,48,128]{2,1,0:T(8,128)(2,1)} %shard_map.136.refs_2_), calls=%async_computation.5 | async-start | bytes 786432 | tf_op jit(solution)/shard_map/all_to_all | solution.py:726
  106.8 12.3 %copy-start = (f32[64,16,128]{2,1,0:T(8,128)S(1)}, f32[64,16,128]{2,1,0:T(8,128)}, u32[]{:S(2)}) copy-start(f32[64,16,128]{2,1,0:T(8,128)} %get-tuple-element.25.refs_1_) | copy-start | bytes 1572868

commit v4 on v3

--- a/solution.py
+++ b/solution.py
@@ -477,13 +477,13 @@
     pack_rows(plan, 0, half, r_ref, packed_ref, arrived, packed, in_sems, out_sems, copies)
 
 
-def each_mode_row(plan, product, first, r_ref, x_ref, y_ref, flat, turned, rows, held, sems):
+def each_mode_row(plan, product, first, mixed, r_ref, x_ref, y_ref, flat, turned, rows, held, sems):
     width = plan.channels
     copies = [
         pltpu.make_async_copy(
-            r_ref.at[pl.ds(t * MIXED, MIXED)], held.at[pl.ds(t * MIXED, MIXED)], sems.at[t]
-        )
-        for t in range(plan.mx // MIXED)
+            r_ref.at[pl.ds(t * mixed, mixed)], held.at[pl.ds(t * mixed, mixed)], sems.at[t]
+        )
+        for t in range(plan.mx // mixed)
     ]
     for copy in copies:
         copy.start()
@@ -506,7 +506,7 @@
 
     for t, copy in enumerate(copies):
         copy.wait()
-        lax.fori_loop(t * MIXED, (t + 1) * MIXED, step, 0, unroll=8)
+        lax.fori_loop(t * mixed, (t + 1) * mixed, step, 0, unroll=16 if mixed == 16 else 8)
     values = flat[...].reshape(plan.devices, plan.mx, plan.lanes)
     y_ref[:, : plan.mx] = values.astype(BF16)
 
@@ -532,7 +532,8 @@
     return arrivals, refs[count + 1 :]
 
 
-def mix_kernel(plan, held, r_ref, field_ref, cot_ref, kernel_ref, x_ref, y_ref, *refs):
+def mix_kernel(plan, held, r_ref, field_ref, cot_ref, kernel_ref, x_ref, y_ref, kept_ref, *refs):
+    kept_ref[...] = x_ref[:, : plan.mx]
     width = plan.channels
     held, refs = bring((("field", field_ref), ("kernel", kernel_ref)), refs)
     cot = pltpu.make_async_copy(cot_ref, y_ref.at[:, pl.ds(plan.mx + plan.rows, plan.rows)], refs[-1])
@@ -548,13 +549,15 @@
         )
 
     conv = partial(conv_part, plan, held, x_ref, y_ref, *refs[:4])
-    each_mode_row(plan, product, conv, r_ref, x_ref, y_ref, *refs[4:])
+    each_mode_row(plan, product, conv, MIXED, r_ref, x_ref, y_ref, *refs[4:])
     cot.wait()
 
 
 def back_kernel(
-    plan, held, r_ref, field_ref, cot_ref, kernel_ref, g_ref, layer_ref, grad_ref, both_ref, *refs
+    plan, held, r_ref, field_ref, cot_ref, kernel_ref, g_ref, layer_ref, grad_ref, both_ref,
+    kept_ref, *refs
 ):
+    kept_ref[...] = g_ref[:, : plan.mx]
     width = plan.channels
     sources = (("field", field_ref), ("cotangent", cot_ref), ("kernel", kernel_ref))
     held, refs = bring(sources, refs)
@@ -571,7 +574,7 @@
         return total[:GROUP], total[GROUP:]
 
     space = partial(space_part, plan, held, g_ref, layer_ref, grad_ref, both_ref, *refs[:5])
-    each_mode_row(plan, product, space, r_ref, g_ref, both_ref, *refs[5:])
+    each_mode_row(plan, product, space, plan.mx, r_ref, g_ref, both_ref, *refs[5:])
 
 
 def outer_kernel(
@@ -818,9 +821,9 @@
         us=5.0,
         alias=True,
     )
-    b_part = call(
+    b_part, a_kept = call(
         mix_kernel,
-        rows_of(plan.mx + 2 * plan.rows),
+        (rows_of(plan.mx + 2 * plan.rows), rows_of(plan.mx)),
         a_both,
         raw=(weights, field, cotangent.reshape(n, plan.rows, by), kernel_weight),
         scratch=[place, kernel_place, pltpu.SemaphoreType.DMA((2,))]
@@ -828,6 +831,7 @@
         + modes_scratch
         + [pltpu.SemaphoreType.DMA],
         us=6.0,
+        mib=54,
     )
     g_part = call(
         middle_kernel,
@@ -839,12 +843,13 @@
         us=2.6,
     )
     g_both = exchange(g_part)
-    layer_out, grad_sum, back_terms = call(
+    layer_out, grad_sum, back_terms, g_kept = call(
         back_kernel,
         (
             jax.ShapeDtypeStruct(field.shape, BF16),
             jax.ShapeDtypeStruct(field.shape, F32),
             rows_of(plan.mx + EDGE),
+            rows_of(plan.mx),
         ),
         g_both,
         raw=(weights, field, cotangent, kernel_weight),
@@ -852,6 +857,7 @@
         + [block, edges, paired, taps, field_flat]
         + modes_scratch,
         us=8.0,
+        mib=54,
     )
     back_both = exchange(back_terms)
 
@@ -859,8 +865,8 @@
         return call(
             lambda plan, *refs: outer_kernel(plan, first_j, count, *refs),
             jax.ShapeDtypeStruct(spectral_weight.shape, BF16),
-            a_both,
-            g_both,
+            a_kept,
+            g_kept,
             scratch=[
                 flat,
                 flat,

time: 122 us -> 121 us (level)
  transfers between devices with their start and end apart: 4 -> 4, of which waited for: 4 -> 4; matrix products, arithmetic and copies ran while one was open for 0% -> 0% of each run, Pallas kernels for 22% -> 21%
where the time goes in v4:
time: 121 us; the launch traced here: 119 us
  Pallas kernels  46.6 us (39%)
  blocking collectives  39.7 us (33%)
  starting transfers between devices  16.2 us (13%)
  waiting for transfers between devices  15.4 us (13%)
    pallas_call x9, Pallas kernels, call(): pl.pallas_call(run, out_shape=outs, in_specs=[anywhere] * len(raw) + [her...  40.6 us
    all_to_all x2, blocking collectives, exchange(): return lax.all_to_all(x, BOTH, 0, 0, tiled=True)  39.7 us
    all_to_all x4, starting transfers between devices, exchange(): return lax.all_to_all(x, BOTH, 0, 0, tiled=True)  16.2 us
    all_to_all x4, waiting for transfers between devices, exchange(): return lax.all_to_all(x, BOTH, 0, 0, tiled=True)  15.4 us
    pallas_call x1, Pallas kernels, fast_body(): pl.pallas_call(partial(load_kernel, plan, half), out_shape=(jax.ShapeDtyp...  5.96 us
  transfers between devices with their start and end apart: 4, of which 4 were waited for; matrix products, arithmetic and copies ran while one was open for 0% of the time, Pallas kernels for 21%

profile of v4, /device:TPU:8, one launch (start us, length us, event | category | flops | bytes accessed | tf_op | source)
XLA Modules:
  0.0 119.2 jit_solution(15479392802882821304)
XLA Ops:
  0.6 6.0 %all-to-all-start = ((bf16[32,32,128]{2,1,0:T(8,128)(2,1)}), bf16[32,32,128]{2,1,0:T(8,128)(2,1)S(1)}, u32[]{:S(2)}, u32[]{:S(2)}) async-start(bf16[32,32,128]{2,1,0:T(8,128)(2,1)} %bitcast.2), calls=%async_computation | async-start | bytes 524288 | tf_op jit(solution)/shard_map/all_to_all | solution.py:729
  6.7 6.0 %shard_map.129 = (bf16[16,32,64,128]{3,2,1,0:T(8,128)(2,1)}, bf16[512,512]{1,0:T(8,128)(2,1)S(1)}, bf16[128,512]{1,0:T(8,128)(2,1)S(1)}, bf16[256,128]{1,0:T(8,1...) custom-call(bf16[2,16,32,64,64]{4,3,2,1,0:T(8,128)(2,1)} %refs_0_.3, ...), custom_call_target="tpu_custom_call" | custom-call | flops 5000000000 | bytes 1024 | tf_op jit(solution)/shard_map/pallas_call | solution.py:793
  12.7 3.6 %all-to-all-done.refs_0_ = bf16[32,32,128]{2,1,0:T(8,128)(2,1)S(1)} async-done(((bf16[32,32,128]{2,1,0:T(8,128)(2,1)}), bf16[32,32,128]{2,1,0:T(8,128)(2,1)S(1)}, u32[]{:S(2)}, u32[]{:S(2)}) %all-to-all-start) | async-done | bytes 262176 | tf_op jit(solution)/shard_map/all_to_all | solution.py:729
  16.2 1.6 %shard_map.130.refs_1_ = bf16[32,32,128]{2,1,0:T(8,128)(2,1)} custom-call(bf16[32,32,128]{2,1,0:T(8,128)(2,1)S(1)} %all-to-all-done.refs_0_, bf16[512,512]{1,0:T(8,128)(2,1)S(1)} %get-tuple-element.19.refs_1_.refs_2_, bf16[128,512]{1,0:T(8,128)(2,1)S(1)} %get-tuple-element.20.refs_2_.refs_3_, bf16[128,256]{1,0:T(8,128)(2,1)S(1)} %get-tuple-element.21.refs_3_.refs_4_, ...), custom_call_target="tpu_custom_call" | custom-call | flops 1000000000 | bytes 1024 | tf_op jit(solution)/shard_map/pallas_call | solution.py:749
  17.8 3.4 %all-to-all-start.1 = ((bf16[32,32,128]{2,1,0:T(8,128)(2,1)}), bf16[32,32,128]{2,1,0:T(8,128)(2,1)S(1)}, u32[]{:S(2)}, u32[]{:S(2)}) async-start(bf16[32,32,128]{2,1,0:T(8,128)(2,1)} %shard_map.130.refs_1_), calls=%async_computation.1 | async-start | bytes 524288 | tf_op jit(solution)/shard_map/all_to_all | solution.py:729
  21.2 5.6 %shard_map.131.refs_0_ = bf16[16,32,64,128]{3,2,1,0:T(8,128)(2,1)} custom-call(bf16[2,16,32,64,64]{4,3,2,1,0:T(8,128)(2,1)} %refs_0_.3, bf16[32,32,128]{2,1,0:T(8,128)(2,1)} %shard_map.130.refs_1_, bf16[16,32,64,128]{3,2,1,0:T(8,128)(2,1)} %get-tuple-element.24.refs_2_), custom_call_target="tpu_custom_call", output_to_operand_aliasing={{}: (2, {})} | custom-call | flops 5000000000 | bytes 1024 | tf_op jit(solution)/shard_map/pallas_call | solution.py:749
  26.8 3.9 %all-to-all-done.1.refs_4_ = bf16[32,32,128]{2,1,0:T(8,128)(2,1)S(1)} async-done(((bf16[32,32,128]{2,1,0:T(8,128)(2,1)}), bf16[32,32,128]{2,1,0:T(8,128)(2,1)S(1)}, u32[]{:S(2)}, u32[]{:S(2)}) %all-to-all-start.1) | async-done | bytes 262176 | tf_op jit(solution)/shard_map/all_to_all | solution.py:729
  30.7 0.0 copy-start.1
  30.7 0.7 copy-done.1
  31.4 7.2 %shard_map.132 = (bf16[32,80,128]{2,1,0:T(8,128)(2,1)}, bf16[32,16,128]{2,1,0:T(8,128)(2,1)}) custom-call(bf16[16,32,64,128]{3,2,1,0:T(8,128)(2,1)} %shard_map.131.refs_0_, bf16[64,16,128]{2,1,0:T(8,128)(2,1)} %refs_1_.4, bf16[32,32,128]{2,1,0:T(8,128)(2,1)} %bitcast.3, bf16[3,3,64,64]{3,2,1,0:T(8,128)(2,1)} %refs_3_.4, bf16[32,32,128]{2,1,0:T(8,128)(2,1)} %copy-done.1), custom_call_target="tpu_custom_call" | custom-call | flops 6000000000 | bytes 1024 | tf_op jit(solution)/shard_map/pallas_call | solution.py:749
  38.6 21.4 %all_to_all.30.refs_0_ = bf16[32,80,128]{2,1,0:T(8,128)(2,1)S(1)} all-to-all(bf16[32,80,128]{2,1,0:T(8,128)(2,1)} %get-tuple-element.25), channel_id=1, replica_groups=mesh['gx'=8,'gy'=4] {'gx','gy'}, dimensions={0} | all-to-all | bytes 1310720 | tf_op jit(solution)/shard_map/all_to_all | solution.py:729
  60.0 1.7 %shard_map.133 = bf16[32,64,128]{2,1,0:T(8,128)(2,1)S(1)} custom-call(bf16[32,80,128]{2,1,0:T(8,128)(2,1)S(1)} %all_to_all.30.refs_0_, bf16[256,128]{1,0:T(8,128)(2,1)S(1)} %get-tuple-element.26.refs_1_, bf16[512,512]{1,0:T(8,128)(2,1)S(1)} %get-tuple-element.19.refs_1_.refs_2_, bf16[128,512]{1,0:T(8,128)(2,1)S(1)} %get-tuple-element.20.refs_2_.refs_3_, ...), custom_call_target="tpu_custom_call" | custom-call | flops 2600000000 | bytes 1024 | tf_op jit(solution)/shard_map/pallas_call | solution.py:749
  61.7 18.3 %all_to_all.31.refs_4_ = bf16[32,64,128]{2,1,0:T(8,128)(2,1)} all-to-all(bf16[32,64,128]{2,1,0:T(8,128)(2,1)S(1)} %shard_map.133), channel_id=1, replica_groups=mesh['gx'=8,'gy'=4] {'gx','gy'}, dimensions={0} | all-to-all | bytes 1048576 | tf_op jit(solution)/shard_map/all_to_all | solution.py:729
  80.0 8.3 %shard_map.134 = (bf16[64,16,128]{2,1,0:T(8,128)(2,1)}, f32[64,16,128]{2,1,0:T(8,128)}, bf16[32,32,128]{2,1,0:T(8,128)(2,1)}, bf16[32,16,128]{2,1,0:T(8,128)(2,1)}) custom-call(bf16[16,32,64,128]{3,2,1,0:T(8,128)(2,1)} %shard_map.131.refs_0_, bf16[64,16,128]{2,1,0:T(8,128)(2,1)} %refs_1_.4, bf16[64,16,128]{2,1,0:T(8,128)(2,1)} %refs_2_.2, ...), custom_call_target="tpu_custom_call" | custom-call | flops 8000000000 | bytes 1024 | tf_op jit(solution)/shard_map/pallas_call | solution.py:749
  88.3 3.3 %all-to-all-start.4 = ((bf16[32,32,128]{2,1,0:T(8,128)(2,1)}), bf16[32,32,128]{2,1,0:T(8,128)(2,1)S(1)}, u32[]{:S(2)}, u32[]{:S(2)}) async-start(bf16[32,32,128]{2,1,0:T(8,128)(2,1)} %get-tuple-element.28.refs_2_), calls=%async_computation.4 | async-start | bytes 524288 | tf_op jit(solution)/shard_map/all_to_all | solution.py:729
  91.6 6.9 %shard_map.135.refs_3_ = bf16[2,16,32,64,64]{4,3,2,1,0:T(8,128)(2,1)} custom-call(bf16[32,16,128]{2,1,0:T(8,128)(2,1)} %get-tuple-element.29.refs_0_, bf16[32,16,128]{2,1,0:T(8,128)(2,1)} %get-tuple-element.30.refs_1_, bf16[32,32,128]{2,1,0:T(8,128)(2,1)} %get-tuple-element.28.refs_2_), custom_call_target="tpu_custom_call" | custom-call | flops 6400000000 | bytes 1024 | tf_op jit(solution)/shard_map/pallas_call | solution.py:749
  98.6 2.6 %all-to-all-done.4.refs_0_ = bf16[32,32,128]{2,1,0:T(8,128)(2,1)S(1)} async-done(((bf16[32,32,128]{2,1,0:T(8,128)(2,1)}), bf16[32,32,128]{2,1,0:T(8,128)(2,1)S(1)}, u32[]{:S(2)}, u32[]{:S(2)}) %all-to-all-start.4) | async-done | bytes 262176 | tf_op jit(solution)/shard_map/all_to_all | solution.py:729
  101.1 1.4 %shard_map.136.refs_2_ = bf16[32,48,128]{2,1,0:T(8,128)(2,1)} custom-call(bf16[32,32,128]{2,1,0:T(8,128)(2,1)S(1)} %all-to-all-done.4.refs_0_, bf16[256,128]{1,0:T(8,128)(2,1)S(1)} %get-tuple-element.26.refs_1_, bf16[512,512]{1,0:T(8,128)(2,1)S(1)} %get-tuple-element.19.refs_1_.refs_2_, bf16[2,16,32,64,64]{4,3,2,1,0:T(8,128)(2,1)} %shard_map.135.refs_3_), custom_call_target="tpu_custom_call" | custom-call | flops 1300000000 | bytes 1024 | tf_op jit(solution)/shard_map/pallas_call | solution.py:749
  102.5 3.4 %all-to-all-start.5 = ((bf16[32,48,128]{2,1,0:T(8,128)(2,1)}), bf16[32,48,128]{2,1,0:T(8,128)(2,1)S(1)}, u32[]{:S(2)}, u32[]{:S(2)}) async-start(bf16[32,48,128]{2,1,0:T(8,128)(2,1)} %shard_map.136.refs_2_), calls=%async_computation.5 | async-start | bytes 786432 | tf_op jit(solution)/shard_map/all_to_all | solution.py:729
  105.9 0.0 copy-start
  105.9 7.0 %shard_map.138 = bf16[2,16,32,64,64]{4,3,2,1,0:T(8,128)(2,1)} custom-call(bf16[32,16,128]{2,1,0:T(8,128)(2,1)} %get-tuple-element.29.refs_0_, bf16[32,16,128]{2,1,0:T(8,128)(2,1)} %get-tuple-element.30.refs_1_, bf16[32,48,128]{2,1,0:T(8,128)(2,1)} %shard_map.136.refs_2_, bf16[2,16,32,64,64]{4,3,2,1,0:T(8,128)(2,1)} %shard_map.135.refs_3_), custom_call_target="tpu_custom_call", output_to_operand_aliasing={{}: (3, {})} | custom-call | flops 6400000000 | bytes 1024 | tf_op jit(solution)/shard_map/pallas_call | solution.py:749
  112.9 5.3 %all-to-all-done.5.refs_0_ = bf16[32,48,128]{2,1,0:T(8,128)(2,1)S(1)} async-done(((bf16[32,48,128]{2,1,0:T(8,128)(2,1)}), bf16[32,48,128]{2,1,0:T(8,128)(2,1)S(1)}, u32[]{:S(2)}, u32[]{:S(2)}) %all-to-all-start.5) | async-done | bytes 393248 | tf_op jit(solution)/shard_map/all_to_all | solution.py:729
  118.3 0.0 copy-done
  118.3 0.9 shard_map.137
Async XLA Ops:
  0.6 15.6 %all-to-all-start = ((bf16[32,32,128]{2,1,0:T(8,128)(2,1)}), bf16[32,32,128]{2,1,0:T(8,128)(2,1)S(1)}, u32[]{:S(2)}, u32[]{:S(2)}) async-start(bf16[32,32,128]{2,1,0:T(8,128)(2,1)} %bitcast.2), calls=%async_computation | async-start | bytes 524288 | tf_op jit(solution)/shard_map/all_to_all | solution.py:729
  17.8 12.9 %all-to-all-start.1 = ((bf16[32,32,128]{2,1,0:T(8,128)(2,1)}), bf16[32,32,128]{2,1,0:T(8,128)(2,1)S(1)}, u32[]{:S(2)}, u32[]{:S(2)}) async-start(bf16[32,32,128]{2,1,0:T(8,128)(2,1)} %shard_map.130.refs_1_), calls=%async_computation.1 | async-start | bytes 524288 | tf_op jit(solution)/shard_map/all_to_all | solution.py:729
  30.7 0.7 copy-start.1
  88.3 12.8 %all-to-all-start.4 = ((bf16[32,32,128]{2,1,0:T(8,128)(2,1)}), bf16[32,32,128]{2,1,0:T(8,128)(2,1)S(1)}, u32[]{:S(2)}, u32[]{:S(2)}) async-start(bf16[32,32,128]{2,1,0:T(8,128)(2,1)} %get-tuple-element.28.refs_2_), calls=%async_computation.4 | async-start | bytes 524288 | tf_op jit(solution)/shard_map/all_to_all | solution.py:729
  102.5 15.7 %all-to-all-start.5 = ((bf16[32,48,128]{2,1,0:T(8,128)(2,1)}), bf16[32,48,128]{2,1,0:T(8,128)(2,1)S(1)}, u32[]{:S(2)}, u32[]{:S(2)}) async-start(bf16[32,48,128]{2,1,0:T(8,128)(2,1)} %shard_map.136.refs_2_), calls=%async_computation.5 | async-start | bytes 786432 | tf_op jit(solution)/shard_map/all_to_all | solution.py:729
  105.9 12.3 %copy-start = (f32[64,16,128]{2,1,0:T(8,128)S(1)}, f32[64,16,128]{2,1,0:T(8,128)}, u32[]{:S(2)}) copy-start(f32[64,16,128]{2,1,0:T(8,128)} %get-tuple-element.31.refs_1_) | copy-start | bytes 1572868

commit v5 on v4

--- a/solution.py
+++ b/solution.py
@@ -785,13 +785,14 @@
     sources = {name: jnp.asarray(t) for name, t in plan.named().items()}
     packed_shape = (plan.mx, plan.my, channels, 2 * channels)
     half = plan.mx // 2
-    chunk_sems = pltpu.SemaphoreType.DMA((half // CHUNK,))
+    early, late = half - CHUNK, half + CHUNK
+    chunk_sems = pltpu.SemaphoreType.DMA((late // CHUNK,))
     pack_scratch = [
-        pltpu.VMEM((2, half) + packed_shape[1:-1] + (channels,), BF16),
-        pltpu.VMEM((half,) + packed_shape[1:], BF16),
+        pltpu.VMEM((2, late) + packed_shape[1:-1] + (channels,), BF16),
+        pltpu.VMEM((late,) + packed_shape[1:], BF16),
     ]
     weights, *held = pl.pallas_call(
-        partial(load_kernel, plan, half),
+        partial(load_kernel, plan, early),
         out_shape=(jax.ShapeDtypeStruct(packed_shape, BF16),)
         + tuple(pltpu.VMEM(t.shape, t.dtype) for t in sources.values()),
         in_specs=[anywhere] * (1 + len(sources)),
@@ -812,7 +813,7 @@
     a_both = exchange(a_part)
     weights = call(
         lambda plan, held, r_ref, after_ref, first_ref, *refs: pack_rows(
-            plan, half, half, r_ref, *refs
+            plan, early, late, r_ref, *refs
         ),
         jax.ShapeDtypeStruct(packed_shape, BF16),
         raw=(spectral_weight, a_part, weights),

time: 121 us -> 121 us (level)
    pallas_call x1, Pallas kernels: 5.96 us -> 4.61 us  [fast_body(): pl.pallas_call(partial(load_kernel, plan, early), out_shape=(jax.ShapeDty...]
where the time goes in v5:
time: 121 us; the launch traced here: 119 us
  Pallas kernels  46.2 us (38%)
  blocking collectives  39.7 us (33%)
  starting transfers between devices  16.2 us (13%)
  waiting for transfers between devices  15.7 us (13%)
    pallas_call x9, Pallas kernels, call(): pl.pallas_call(run, out_shape=outs, in_specs=[anywhere] * len(raw) + [her...  41.6 us
    all_to_all x2, blocking collectives, exchange(): return lax.all_to_all(x, BOTH, 0, 0, tiled=True)  39.7 us
    all_to_all x4, starting transfers between devices, exchange(): return lax.all_to_all(x, BOTH, 0, 0, tiled=True)  16.2 us
    all_to_all x4, waiting for transfers between devices, exchange(): return lax.all_to_all(x, BOTH, 0, 0, tiled=True)  15.7 us
    pallas_call x1, Pallas kernels, fast_body(): pl.pallas_call(partial(load_kernel, plan, early), out_shape=(jax.ShapeDty...  4.61 us
  transfers between devices with their start and end apart: 4, of which 4 were waited for; matrix products, arithmetic and copies ran while one was open for 0% of the time, Pallas kernels for 21%

profile of v5, /device:TPU:8, one launch (start us, length us, event | category | flops | bytes accessed | tf_op | source)
XLA Modules:
  0.0 119.2 jit_solution(18437920819100238531)
XLA Ops:
  0.6 6.0 %all-to-all-start = ((bf16[32,32,128]{2,1,0:T(8,128)(2,1)}), bf16[32,32,128]{2,1,0:T(8,128)(2,1)S(1)}, u32[]{:S(2)}, u32[]{:S(2)}) async-start(bf16[32,32,128]{2,1,0:T(8,128)(2,1)} %bitcast.2), calls=%async_computation | async-start | bytes 524288 | tf_op jit(solution)/shard_map/all_to_all | solution.py:729
  6.7 4.6 %shard_map.129 = (bf16[16,32,64,128]{3,2,1,0:T(8,128)(2,1)}, bf16[512,512]{1,0:T(8,128)(2,1)S(1)}, bf16[128,512]{1,0:T(8,128)(2,1)S(1)}, bf16[256,128]{1,0:T(8,1...) custom-call(bf16[2,16,32,64,64]{4,3,2,1,0:T(8,128)(2,1)} %refs_0_.3, ...), custom_call_target="tpu_custom_call" | custom-call | flops 5000000000 | bytes 1024 | tf_op jit(solution)/shard_map/pallas_call | solution.py:794
  11.3 4.9 %all-to-all-done.refs_0_ = bf16[32,32,128]{2,1,0:T(8,128)(2,1)S(1)} async-done(((bf16[32,32,128]{2,1,0:T(8,128)(2,1)}), bf16[32,32,128]{2,1,0:T(8,128)(2,1)S(1)}, u32[]{:S(2)}, u32[]{:S(2)}) %all-to-all-start) | async-done | bytes 262176 | tf_op jit(solution)/shard_map/all_to_all | solution.py:729
  16.2 1.6 %shard_map.130.refs_1_ = bf16[32,32,128]{2,1,0:T(8,128)(2,1)} custom-call(bf16[32,32,128]{2,1,0:T(8,128)(2,1)S(1)} %all-to-all-done.refs_0_, bf16[512,512]{1,0:T(8,128)(2,1)S(1)} %get-tuple-element.19.refs_1_.refs_2_, bf16[128,512]{1,0:T(8,128)(2,1)S(1)} %get-tuple-element.20.refs_2_.refs_3_, bf16[128,256]{1,0:T(8,128)(2,1)S(1)} %get-tuple-element.21.refs_3_.refs_4_, ...), custom_call_target="tpu_custom_call" | custom-call | flops 1000000000 | bytes 1024 | tf_op jit(solution)/shard_map/pallas_call | solution.py:749
  17.8 3.4 %all-to-all-start.1 = ((bf16[32,32,128]{2,1,0:T(8,128)(2,1)}), bf16[32,32,128]{2,1,0:T(8,128)(2,1)S(1)}, u32[]{:S(2)}, u32[]{:S(2)}) async-start(bf16[32,32,128]{2,1,0:T(8,128)(2,1)} %shard_map.130.refs_1_), calls=%async_computation.1 | async-start | bytes 524288 | tf_op jit(solution)/shard_map/all_to_all | solution.py:729
  21.2 6.6 %shard_map.131.refs_0_ = bf16[16,32,64,128]{3,2,1,0:T(8,128)(2,1)} custom-call(bf16[2,16,32,64,64]{4,3,2,1,0:T(8,128)(2,1)} %refs_0_.3, bf16[32,32,128]{2,1,0:T(8,128)(2,1)} %shard_map.130.refs_1_, bf16[16,32,64,128]{3,2,1,0:T(8,128)(2,1)} %get-tuple-element.24.refs_2_), custom_call_target="tpu_custom_call", output_to_operand_aliasing={{}: (2, {})} | custom-call | flops 5000000000 | bytes 1024 | tf_op jit(solution)/shard_map/pallas_call | solution.py:749
  27.8 2.9 %all-to-all-done.1.refs_4_ = bf16[32,32,128]{2,1,0:T(8,128)(2,1)S(1)} async-done(((bf16[32,32,128]{2,1,0:T(8,128)(2,1)}), bf16[32,32,128]{2,1,0:T(8,128)(2,1)S(1)}, u32[]{:S(2)}, u32[]{:S(2)}) %all-to-all-start.1) | async-done | bytes 262176 | tf_op jit(solution)/shard_map/all_to_all | solution.py:729
  30.7 0.0 copy-start.1
  30.7 0.7 copy-done.1
  31.4 7.2 %shard_map.132 = (bf16[32,80,128]{2,1,0:T(8,128)(2,1)}, bf16[32,16,128]{2,1,0:T(8,128)(2,1)}) custom-call(bf16[16,32,64,128]{3,2,1,0:T(8,128)(2,1)} %shard_map.131.refs_0_, bf16[64,16,128]{2,1,0:T(8,128)(2,1)} %refs_1_.4, bf16[32,32,128]{2,1,0:T(8,128)(2,1)} %bitcast.3, bf16[3,3,64,64]{3,2,1,0:T(8,128)(2,1)} %refs_3_.4, bf16[32,32,128]{2,1,0:T(8,128)(2,1)} %copy-done.1), custom_call_target="tpu_custom_call" | custom-call | flops 6000000000 | bytes 1024 | tf_op jit(solution)/shard_map/pallas_call | solution.py:749
  38.6 21.4 %all_to_all.30.refs_0_ = bf16[32,80,128]{2,1,0:T(8,128)(2,1)S(1)} all-to-all(bf16[32,80,128]{2,1,0:T(8,128)(2,1)} %get-tuple-element.25), channel_id=1, replica_groups=mesh['gx'=8,'gy'=4] {'gx','gy'}, dimensions={0} | all-to-all | bytes 1310720 | tf_op jit(solution)/shard_map/all_to_all | solution.py:729
  60.0 1.7 %shard_map.133 = bf16[32,64,128]{2,1,0:T(8,128)(2,1)S(1)} custom-call(bf16[32,80,128]{2,1,0:T(8,128)(2,1)S(1)} %all_to_all.30.refs_0_, bf16[256,128]{1,0:T(8,128)(2,1)S(1)} %get-tuple-element.26.refs_1_, bf16[512,512]{1,0:T(8,128)(2,1)S(1)} %get-tuple-element.19.refs_1_.refs_2_, bf16[128,512]{1,0:T(8,128)(2,1)S(1)} %get-tuple-element.20.refs_2_.refs_3_, ...), custom_call_target="tpu_custom_call" | custom-call | flops 2600000000 | bytes 1024 | tf_op jit(solution)/shard_map/pallas_call | solution.py:749
  61.7 18.3 %all_to_all.31.refs_4_ = bf16[32,64,128]{2,1,0:T(8,128)(2,1)} all-to-all(bf16[32,64,128]{2,1,0:T(8,128)(2,1)S(1)} %shard_map.133), channel_id=1, replica_groups=mesh['gx'=8,'gy'=4] {'gx','gy'}, dimensions={0} | all-to-all | bytes 1048576 | tf_op jit(solution)/shard_map/all_to_all | solution.py:729
  80.0 8.3 %shard_map.134 = (bf16[64,16,128]{2,1,0:T(8,128)(2,1)}, f32[64,16,128]{2,1,0:T(8,128)}, bf16[32,32,128]{2,1,0:T(8,128)(2,1)}, bf16[32,16,128]{2,1,0:T(8,128)(2,1)}) custom-call(bf16[16,32,64,128]{3,2,1,0:T(8,128)(2,1)} %shard_map.131.refs_0_, bf16[64,16,128]{2,1,0:T(8,128)(2,1)} %refs_1_.4, bf16[64,16,128]{2,1,0:T(8,128)(2,1)} %refs_2_.2, ...), custom_call_target="tpu_custom_call" | custom-call | flops 8000000000 | bytes 1024 | tf_op jit(solution)/shard_map/pallas_call | solution.py:749
  88.3 3.3 %all-to-all-start.4 = ((bf16[32,32,128]{2,1,0:T(8,128)(2,1)}), bf16[32,32,128]{2,1,0:T(8,128)(2,1)S(1)}, u32[]{:S(2)}, u32[]{:S(2)}) async-start(bf16[32,32,128]{2,1,0:T(8,128)(2,1)} %get-tuple-element.28.refs_2_), calls=%async_computation.4 | async-start | bytes 524288 | tf_op jit(solution)/shard_map/all_to_all | solution.py:729
  91.6 6.9 %shard_map.135.refs_3_ = bf16[2,16,32,64,64]{4,3,2,1,0:T(8,128)(2,1)} custom-call(bf16[32,16,128]{2,1,0:T(8,128)(2,1)} %get-tuple-element.29.refs_0_, bf16[32,16,128]{2,1,0:T(8,128)(2,1)} %get-tuple-element.30.refs_1_, bf16[32,32,128]{2,1,0:T(8,128)(2,1)} %get-tuple-element.28.refs_2_), custom_call_target="tpu_custom_call" | custom-call | flops 6400000000 | bytes 1024 | tf_op jit(solution)/shard_map/pallas_call | solution.py:749
  98.6 2.6 %all-to-all-done.4.refs_0_ = bf16[32,32,128]{2,1,0:T(8,128)(2,1)S(1)} async-done(((bf16[32,32,128]{2,1,0:T(8,128)(2,1)}), bf16[32,32,128]{2,1,0:T(8,128)(2,1)S(1)}, u32[]{:S(2)}, u32[]{:S(2)}) %all-to-all-start.4) | async-done | bytes 262176 | tf_op jit(solution)/shard_map/all_to_all | solution.py:729
  101.1 1.4 %shard_map.136.refs_2_ = bf16[32,48,128]{2,1,0:T(8,128)(2,1)} custom-call(bf16[32,32,128]{2,1,0:T(8,128)(2,1)S(1)} %all-to-all-done.4.refs_0_, bf16[256,128]{1,0:T(8,128)(2,1)S(1)} %get-tuple-element.26.refs_1_, bf16[512,512]{1,0:T(8,128)(2,1)S(1)} %get-tuple-element.19.refs_1_.refs_2_, bf16[2,16,32,64,64]{4,3,2,1,0:T(8,128)(2,1)} %shard_map.135.refs_3_), custom_call_target="tpu_custom_call" | custom-call | flops 1300000000 | bytes 1024 | tf_op jit(solution)/shard_map/pallas_call | solution.py:749
  102.5 3.4 %all-to-all-start.5 = ((bf16[32,48,128]{2,1,0:T(8,128)(2,1)}), bf16[32,48,128]{2,1,0:T(8,128)(2,1)S(1)}, u32[]{:S(2)}, u32[]{:S(2)}) async-start(bf16[32,48,128]{2,1,0:T(8,128)(2,1)} %shard_map.136.refs_2_), calls=%async_computation.5 | async-start | bytes 786432 | tf_op jit(solution)/shard_map/all_to_all | solution.py:729
  105.9 0.0 copy-start
  105.9 7.0 %shard_map.138 = bf16[2,16,32,64,64]{4,3,2,1,0:T(8,128)(2,1)} custom-call(bf16[32,16,128]{2,1,0:T(8,128)(2,1)} %get-tuple-element.29.refs_0_, bf16[32,16,128]{2,1,0:T(8,128)(2,1)} %get-tuple-element.30.refs_1_, bf16[32,48,128]{2,1,0:T(8,128)(2,1)} %shard_map.136.refs_2_, bf16[2,16,32,64,64]{4,3,2,1,0:T(8,128)(2,1)} %shard_map.135.refs_3_), custom_call_target="tpu_custom_call", output_to_operand_aliasing={{}: (3, {})} | custom-call | flops 6400000000 | bytes 1024 | tf_op jit(solution)/shard_map/pallas_call | solution.py:749
  112.9 5.3 %all-to-all-done.5.refs_0_ = bf16[32,48,128]{2,1,0:T(8,128)(2,1)S(1)} async-done(((bf16[32,48,128]{2,1,0:T(8,128)(2,1)}), bf16[32,48,128]{2,1,0:T(8,128)(2,1)S(1)}, u32[]{:S(2)}, u32[]{:S(2)}) %all-to-all-start.5) | async-done | bytes 393248 | tf_op jit(solution)/shard_map/all_to_all | solution.py:729
  118.3 0.0 copy-done
  118.3 0.9 shard_map.137
Async XLA Ops:
  0.6 15.6 %all-to-all-start = ((bf16[32,32,128]{2,1,0:T(8,128)(2,1)}), bf16[32,32,128]{2,1,0:T(8,128)(2,1)S(1)}, u32[]{:S(2)}, u32[]{:S(2)}) async-start(bf16[32,32,128]{2,1,0:T(8,128)(2,1)} %bitcast.2), calls=%async_computation | async-start | bytes 524288 | tf_op jit(solution)/shard_map/all_to_all | solution.py:729
  17.8 12.9 %all-to-all-start.1 = ((bf16[32,32,128]{2,1,0:T(8,128)(2,1)}), bf16[32,32,128]{2,1,0:T(8,128)(2,1)S(1)}, u32[]{:S(2)}, u32[]{:S(2)}) async-start(bf16[32,32,128]{2,1,0:T(8,128)(2,1)} %shard_map.130.refs_1_), calls=%async_computation.1 | async-start | bytes 524288 | tf_op jit(solution)/shard_map/all_to_all | solution.py:729
  30.7 0.7 copy-start.1
  88.3 12.8 %all-to-all-start.4 = ((bf16[32,32,128]{2,1,0:T(8,128)(2,1)}), bf16[32,32,128]{2,1,0:T(8,128)(2,1)S(1)}, u32[]{:S(2)}, u32[]{:S(2)}) async-start(bf16[32,32,128]{2,1,0:T(8,128)(2,1)} %get-tuple-element.28.refs_2_), calls=%async_computation.4 | async-start | bytes 524288 | tf_op jit(solution)/shard_map/all_to_all | solution.py:729
  102.5 15.7 %all-to-all-start.5 = ((bf16[32,48,128]{2,1,0:T(8,128)(2,1)}), bf16[32,48,128]{2,1,0:T(8,128)(2,1)S(1)}, u32[]{:S(2)}, u32[]{:S(2)}) async-start(bf16[32,48,128]{2,1,0:T(8,128)(2,1)} %shard_map.136.refs_2_), calls=%async_computation.5 | async-start | bytes 786432 | tf_op jit(solution)/shard_map/all_to_all | solution.py:729
  105.9 12.3 %copy-start = (f32[64,16,128]{2,1,0:T(8,128)S(1)}, f32[64,16,128]{2,1,0:T(8,128)}, u32[]{:S(2)}) copy-start(f32[64,16,128]{2,1,0:T(8,128)} %get-tuple-element.31.refs_1_) | copy-start | bytes 1572868
